TPU v7x, 128 devices: a whole 4x4x4 slice. The times are simulated.
128 devices in a mesh: gx: 32 (over y, x, core), gy: 4 (over z).
Axes of the slice: x: 4, y: 4, z: 4, core: 2. Of those that a mesh axis runs over, the one named last changes fastest.
Arguments:
- field: bfloat16 [64, 16, 64, 4096], P('gy', None, None, 'gx'), may hold values from -6 to 6
- conv_w: bfloat16 [27, 64, 64], replicated, may hold values from -0.15625 to 0.15625
- spec_re: float32 [16, 64, 64], replicated, may hold values from -6 to 6
- spec_im: float32 [16, 64, 64], replicated, may hold values from -6 to 6
- mlp_in: bfloat16 [256, 64], replicated, may hold values from -0.75 to 0.75
- mlp_out: bfloat16 [64, 256], replicated, may hold values from -0.375 to 0.375
Outputs:
- result: bfloat16 [64, 16, 64, 4096], P('gy', None, None, 'gx')
All inputs are finite; a program needn't handle non-finite values.
Results may differ from a plain program's by a relative error of at most 0.0062.
Values may be sent and summed in bfloat16 or wider, within the bound.
No kernel may reach another device: no remote copies, remote signals or barrier semaphores. Data moves between devices by JAX's collectives and lax.ppermute only.
A program may use at most 128 MiB of HBM per device.

v0:
```python
import math

import jax
import jax.numpy as jnp
from jax import lax
from jax.sharding import PartitionSpec as P


def with_halo(x, sides, width):
    for axis, dim in sides:
        devices, length = (lax.axis_size(axis), x.shape[dim])
        up = [(i, (i + 1) % devices) for i in range(devices - 1)]
        down = [(j, i) for i, j in up]
        last = lax.slice_in_dim(x, length - width, length, axis=dim)
        leading = lax.slice_in_dim(x, 0, width, axis=dim)
        before = lax.ppermute(last, axis, up)
        after = lax.ppermute(leading, axis, down)
        x = jnp.concatenate([before, x, after], axis=dim)
    return x


def in_blocks(x, dim, devices):
    lengths = x.shape
    pieces = x.reshape(*lengths[:dim], devices, lengths[dim] // devices, *lengths[dim + 1 :])
    return jnp.moveaxis(pieces, dim, 0)


def summed_on_arrival(x, axis, dim):
    devices = lax.axis_size(axis)
    pieces = lax.all_to_all(in_blocks(x, dim, devices), axis, 0, 0, tiled=True)
    return jnp.sum(pieces, axis=0)


def in_order(pieces, dim):
    lengths = list(pieces.shape[1:])
    lengths[dim] *= pieces.shape[0]
    return jnp.moveaxis(pieces, 0, dim).reshape(lengths)


def sent_to_all(x, axis):
    copies = jnp.broadcast_to(x, (lax.axis_size(axis), *x.shape))
    return lax.all_to_all(copies, axis, split_axis=0, concat_axis=0, tiled=True)


def gather_directly(x, axis, dim):
    return in_order(sent_to_all(x, axis), dim)


def forward_table(start, count, total, modes):
    places = start + jnp.arange(count, dtype=jnp.int32)
    orders = jnp.arange(modes, dtype=jnp.int32)
    phase = places[:, None] * orders[None, :] % total
    angle = phase.astype(jnp.float32) * (2.0 * math.pi / total)
    return jnp.concatenate([jnp.cos(angle), -jnp.sin(angle)], axis=1).astype(jnp.bfloat16)


def inverse_table(start, count, total, modes):
    places = start + jnp.arange(count, dtype=jnp.int32)
    orders = jnp.arange(modes, dtype=jnp.int32)
    phase = orders[:, None] * places[None, :] % total
    angle = phase.astype(jnp.float32) * (2.0 * math.pi / total)
    scales = jnp.where(orders == 0, 1.0, 2.0).astype(jnp.float32) / total
    return jnp.concatenate(
        [jnp.cos(angle) * scales[:, None], -jnp.sin(angle) * scales[:, None]], axis=0
    )


def mix_modes(spectrum, spec_re, spec_im):
    modes = spec_re.shape[0]
    real_part = spectrum[..., :modes]
    imag_part = spectrum[..., modes:]
    highest = lax.Precision.HIGHEST
    out_real = jnp.einsum("koc,...ck->...ok", spec_re, real_part, precision=highest) - jnp.einsum(
        "koc,...ck->...ok", spec_im, imag_part, precision=highest
    )
    out_imag = jnp.einsum("koc,...ck->...ok", spec_re, imag_part, precision=highest) + jnp.einsum(
        "koc,...ck->...ok", spec_im, real_part, precision=highest
    )
    return jnp.concatenate([out_real, out_imag], axis=-1)


def per_device(field, conv_w, spec_re, spec_im, mlp_in, mlp_out):
    rows_y, depth, channels, width = field.shape
    modes = spec_re.shape[0]
    along_y = with_halo(field, (("gy", 0),), 1)
    padded = with_halo(along_y, (("gx", 3),), 1)
    kernel = conv_w.reshape(3, 3, 3, channels, channels)
    conv_out = lax.conv_general_dilated(
        padded[None],
        kernel,
        (1, 1, 1),
        ((0, 0), (1, 1), (0, 0)),
        dimension_numbers=("NHWCD", "HWDOI", "NHWCD"),
        preferred_element_type=jnp.float32,
    )
    lifted = (field.astype(jnp.float32) + conv_out[0]).astype(jnp.bfloat16)
    grid_len = width * lax.axis_size("gx")
    offset = lax.axis_index("gx") * width
    forward = forward_table(offset, width, grid_len, modes)
    partial_modes = jnp.dot(lifted, forward, preferred_element_type=jnp.float32)
    columns = partial_modes.reshape(rows_y * depth, channels, 2 * modes)
    owned = summed_on_arrival(columns, "gx", 0)
    owned_mixed = mix_modes(owned, spec_re, spec_im)
    all_mixed = gather_directly(owned_mixed, "gx", 0)
    mixed = all_mixed.reshape(rows_y, depth, channels, 2 * modes)
    inverse = inverse_table(offset, width, grid_len, modes)

    def finish(row_index):
        mixed_row = lax.dynamic_index_in_dim(mixed, row_index, 0, keepdims=False)
        lifted_row = lax.dynamic_index_in_dim(lifted, row_index, 0, keepdims=False)
        branch = jnp.dot(mixed_row, inverse, precision=lax.Precision.HIGHEST)
        blended = (lifted_row.astype(jnp.float32) + branch).astype(jnp.bfloat16)
        hidden = jax.nn.gelu(
            jnp.einsum("hc,zcx->zhx", mlp_in, blended, preferred_element_type=jnp.float32)
        ).astype(jnp.bfloat16)
        down = jnp.einsum("ch,zhx->zcx", mlp_out, hidden, preferred_element_type=jnp.float32)
        return (blended.astype(jnp.float32) + down).astype(jnp.bfloat16)

    return lax.map(finish, jnp.arange(rows_y, dtype=jnp.int32))


def solution(mesh):
    in_specs = (P("gy", None, None, "gx"), P(), P(), P(), P(), P())
    out_specs = P("gy", None, None, "gx")
    return jax.shard_map(
        per_device, mesh=mesh, in_specs=in_specs, out_specs=out_specs, check_vma=False
    )
```

profile of v0, /device:TPU:1, one launch (start us, length us, event | category | flops | bytes accessed | tf_op | source)
XLA Modules:
  0.0 397.9 jit_solution(10574957004663589112)
XLA Ops:
  0.0 10.1 %copy.21 = bf16[16,16,64,128]{2,1,3,0:T(8,128)(2,1)} copy(bf16[16,16,64,128]{3,2,1,0:T(8,128)(2,1)} %param.8) | data formatting | bytes 8388608 | tf_op args[0]
  11.4 4.4 %collective-permute-start = (bf16[1,16,64,128]{2,1,3,0:T(8,128)(2,1)S(1)}, bf16[1,16,64,128]{2,1,3,0:T(8,128)(2,1)S(1)}, u32[]{:S(2)}, u32[]{:S(2)}) collective-permute-start(bf16[1,16,64,128]{2,1,3,0:T(8,128)(2,1)S(1)} %get-tuple-element.82), channel_id=1, source_target_pairs={{0,1},{1,2},{2,3},{4,5},{5,6},{6,7},{8,9},{9,10},{10,11},{12,13},{... | collective-permute-start | bytes 786440 | tf_op jit(solution)/shard_map/ppermute | solution.py:16
  17.2 9.2 %collective-permute-done = bf16[1,16,64,128]{2,1,3,0:T(8,128)(2,1)S(1)} collective-permute-done((bf16[1,16,64,128]{2,1,3,0:T(8,128)(2,1)S(1)}, bf16[1,16,64,128]{2,1,3,0:T(8,128)(2,1)S(1)}, u32[]{:S(2)}, u32[]{:S(2)}) %collective-permute-start) | collective-permute-done | bytes 262176 | tf_op jit(solution)/shard_map/ppermute | solution.py:16
  26.4 4.2 %collective-permute-done.1 = bf16[1,16,64,128]{2,1,3,0:T(8,128)(2,1)S(1)} collective-permute-done((bf16[1,16,64,128]{2,1,3,0:T(8,128)(2,1)S(1)}, bf16[1,16,64,128]{2,1,3,0:T(8,128)(2,1)S(1)}, u32[]{:S(2)}, u32[]{:S(2)}) %collective-permute-start.1) | collective-permute-done | bytes 262176 | tf_op jit(solution)/shard_map/ppermute | solution.py:17
  31.5 4.7 %collective-permute-start.2 = (bf16[18,16,64,1]{2,1,3,0:T(8,128)(2,1)S(1)}, bf16[18,16,64,1]{2,1,3,0:T(8,128)(2,1)S(1)}, u32[]{:S(2)}, u32[]{:S(2)}) collective-permute-start(bf16[18,16,64,1]{2,1,3,0:T(8,128)(2,1)S(1)} %get-tuple-element.80), channel_id=1, source_target_pairs={{0,4},{4,8},{8,12},{12,16},{16,20},{20,24},{24,28},{28,32},{32,36}... | collective-permute-start | bytes 110600 | tf_op jit(solution)/shard_map/ppermute | solution.py:16
  38.2 3.7 collective-permute-done.3
  41.8 7.0 %maximum_bitcast_fusion = bf16[18,16,64,1,130]{2,1,4,0,3:T(8,128)(2,1)} fusion(bf16[18,16,64,1]{2,1,3,0:T(8,128)(2,1)S(1)} %collective-permute-done.3, bf16[1,16,64,128]{2,1,3,0:T(8,128)(2,1)S(1)} %collective-permute-done.1, bf16[16,16,64,128]{2,1,3,0:T(8,128)(2,1)S(1)} %copy-done.1, bf16[1,16,64,128]{2,1,3,0:T(8,128)(2,1)S(1)} %collective-permute-done, ...), kind=kLoop, calls=%fused_computation.42 | loop fusion | flops 9584640 | bytes 9584640 | tf_op jit(solution)/shard_map/broadcast_in_dim | solution.py:89
  48.8 10.1 %pad = bf16[18,16,64,1,136]{2,1,4,0,3:T(8,128)(2,1)} pad(bf16[18,16,64,1,130]{2,1,4,0,3:T(8,128)(2,1)} %maximum_bitcast_fusion, bf16[]{:T(256)} %constant.60.clone.1), padding=0_0x0_0x0_0x0_0x0_6 | pad | bytes 9805826 | tf_op jit(solution)/shard_map/broadcast_in_dim | solution.py:89
  58.9 10.4 %copy.26 = bf16[18,16,64,1,8,17]{2,4,5,1,0,3:T(8,128)(2,1)} copy(bf16[18,16,64,1,8,17]{2,1,5,4,0,3:T(8,128)(2,1)} %bitcast.111) | data formatting | bytes 10027008 | tf_op jit(solution)/shard_map/conv_general_dilated | solution.py:88
  70.9 82.5 %fusion.40 = f32[16,16,8,17,64]{4,2,3,1,0:T(8,128)} fusion(bf16[3,3,3,64,64]{4,3,2,1,0:T(8,128)(2,1)S(1)} %bitcast.114, bf16[18,16,64,1,7,2]{2,4,5,1,0,3:T(8,128)(2,1)S(1)} %slice.28, bf16[18,16,64,1,8,17]{2,4,5,1,0,3:T(8,128)(2,1)} %copy.26, pred[8,17]{0,1:T(8,128)(4,1)S(1)} %copy-done.6), kind=kOutput, calls=%fused_computation.43 | convolution fusion | flops 7398916096 | bytes 14663816 | tf_op jit(solution)/shard_map/conv_general_dilated | solution.py:88
  153.4 9.9 %copy.27 = f32[16,16,8,17,64]{4,1,3,2,0:T(8,128)S(1)} copy(f32[16,16,8,17,64]{4,2,3,1,0:T(8,128)} %fusion.40) | data formatting | bytes 17825792 | tf_op jit(solution)/shard_map/conv_general_dilated | solution.py:88
  163.3 7.8 %fusion.32 = bf16[16,16,64,128]{2,1,3,0:T(8,128)(2,1)} fusion(f32[16,16,1,136,64]{4,1,3,0,2:T(8,128)S(1)} %bitcast.110, bf16[16,16,64,128]{2,1,3,0:T(8,128)(2,1)} %copy.21), kind=kLoop, calls=%fused_computation.35 | loop fusion | flops 6291456 | bytes 16777216 | tf_op jit(solution)/shard_map/convert_element_type | solution.py:96
  171.1 10.3 %copy.32 = bf16[16,16,64,128]{3,2,1,0:T(8,128)(2,1)} copy(bf16[16,16,64,128]{2,1,3,0:T(8,128)(2,1)} %fusion.32) | data formatting | bytes 8388608 | tf_op jit(solution)/shard_map/while | solution.py:119
  181.3 8.3 %fusion.58 = f32[16,16,64,32]{2,3,1,0:T(8,128)} fusion(bf16[16,16,64,128]{3,2,1,0:T(8,128)(2,1)} %copy.32, bf16[128,16]{0,1:T(8,128)(2,1)S(1)} %get-tuple-element.89, bf16[128,16]{0,1:T(8,128)(2,1)S(1)} %get-tuple-element.88), kind=kOutput, calls=%fused_computation.73 | convolution fusion | flops 134234112 | bytes 6299648 | tf_op jit(solution)/shard_map/dot_general | solution.py:100
  189.6 4.5 %reshape.37 = f32[32,1,16384]{2,1,0:T(1,128)S(1)} reshape(f32[32,8,32,64]{3,2,1,0:T(8,128)} %bitcast.112) | data formatting | bytes 4194304
  194.1 37.1 %all_to_all.10 = f32[32,1,16384]{2,1,0:T(1,128)} all-to-all(f32[32,1,16384]{2,1,0:T(1,128)S(1)} %reshape.37), channel_id=1, replica_groups=mesh['gx'=32,'gy'=4] {'gx'}, dimensions={0} | all-to-all | bytes 4194304 | tf_op jit(solution)/shard_map/all_to_all | solution.py:30
  231.7 7.3 %reduce = f32[32,16384]{1,0:T(8,128)S(1)} reduce(f32[32,1,16384]{2,1,0:T(1,128)} %all_to_all.10, f32[]{:T(128)} %broadcast.109), dimensions={1}, to_apply=%all_to_all.6.reduce_sub_computation | reduce | bytes 4194308 | tf_op jit(solution)/shard_map/all_to_all | solution.py:30
  239.0 3.0 reshape.38
  251.2 5.5 %reshape.39 = f32[32,1,16384]{2,1,0:T(1,128)} reshape(f32[32,8,32,64]{3,2,1,0:T(8,128)} %broadcast_bitcast_fusion) | data formatting | bytes 4194304
  256.7 4.8 %all-to-all-start.1 = ((f32[32,1,16384]{2,1,0:T(1,128)}), f32[32,1,16384]{2,1,0:T(1,128)}, u32[]{:S(2)}, u32[]{:S(2)}) async-start(f32[32,1,16384]{2,1,0:T(1,128)} %reshape.39), calls=%async_computation.1 | async-start | bytes 4194304 | tf_op jit(solution)/shard_map/all_to_all | solution.py:42
  261.6 27.7 %all-to-all-done.1 = f32[32,1,16384]{2,1,0:T(1,128)} async-done(((f32[32,1,16384]{2,1,0:T(1,128)}), f32[32,1,16384]{2,1,0:T(1,128)}, u32[]{:S(2)}, u32[]{:S(2)}) %all-to-all-start.1) | async-done | bytes 2097184 | tf_op jit(solution)/shard_map/all_to_all | solution.py:42
  289.3 7.3 %reduce.1 = f32[32,16384]{1,0:T(8,128)S(1)} reduce(f32[32,1,16384]{2,1,0:T(1,128)} %all-to-all-done.1, f32[]{:T(128)} %broadcast.109), dimensions={1}, to_apply=%all_to_all.7.reduce_sub_computation | reduce | bytes 4194308 | tf_op jit(solution)/shard_map/all_to_all | solution.py:42
  296.6 3.0 reshape.40
  299.7 98.0 %while.10 = (s32[]{:T(128)}, bf16[16,16,64,128]{3,2,1,0:T(8,128)(2,1)}, s32[16]{0:T(128)S(1)}, bf16[16,16,64,128]{3,2,1,0:T(8,128)(2,1)}, f32[16,16,64,32]{2,3,1...) while((s32[]{:T(128)}, ...), condition=%wide.region_2.3_spmd, body=%wide.region_1.2_spmd.sunk | while | flops 190054400 | bytes 1656475 | solution.py:119
  (85 shorter events, 87.4 us)
Async XLA Ops:
  0.0 244.8 %copy-start = (f32[16,64,64]{2,1,0:T(8,128)S(1)}, f32[16,64,64]{2,1,0:T(8,128)}, u32[]{:S(2)}) copy-start(f32[16,64,64]{2,1,0:T(8,128)} %param.10) | copy-start | bytes 786436
  11.4 15.0 %collective-permute-start = (bf16[1,16,64,128]{2,1,3,0:T(8,128)(2,1)S(1)}, bf16[1,16,64,128]{2,1,3,0:T(8,128)(2,1)S(1)}, u32[]{:S(2)}, u32[]{:S(2)}) collective-permute-start(bf16[1,16,64,128]{2,1,3,0:T(8,128)(2,1)S(1)} %get-tuple-element.82), channel_id=1, source_target_pairs={{0,1},{1,2},{2,3},{4,5},{5,6},{6,7},{8,9},{9,10},{10,11},{12,13},{... | collective-permute-start | bytes 786440 | tf_op jit(solution)/shard_map/ppermute | solution.py:16
  15.9 14.7 %collective-permute-start.1 = (bf16[1,16,64,128]{2,1,3,0:T(8,128)(2,1)S(1)}, bf16[1,16,64,128]{2,1,3,0:T(8,128)(2,1)S(1)}, u32[]{:S(2)}, u32[]{:S(2)}) collective-permute-start(bf16[1,16,64,128]{2,1,3,0:T(8,128)(2,1)S(1)} %get-tuple-element.83), channel_id=1, source_target_pairs={{1,0},{2,1},{3,2},{5,4},{6,5},{7,6},{9,8},{10,9},{11,10},{13,12},{... | collective-permute-start | bytes 786440 | tf_op jit(solution)/shard_map/ppermute | solution.py:17
  17.2 24.7 %copy-start.1 = (bf16[16,16,64,128]{2,1,3,0:T(8,128)(2,1)S(1)}, bf16[16,16,64,128]{2,1,3,0:T(8,128)(2,1)}, u32[]{:S(2)}) copy-start(bf16[16,16,64,128]{2,1,3,0:T(8,128)(2,1)} %copy.21) | copy-start | bytes 12582916
  31.5 6.7 %collective-permute-start.2 = (bf16[18,16,64,1]{2,1,3,0:T(8,128)(2,1)S(1)}, bf16[18,16,64,1]{2,1,3,0:T(8,128)(2,1)S(1)}, u32[]{:S(2)}, u32[]{:S(2)}) collective-permute-start(bf16[18,16,64,1]{2,1,3,0:T(8,128)(2,1)S(1)} %get-tuple-element.80), channel_id=1, source_target_pairs={{0,4},{4,8},{8,12},{12,16},{16,20},{20,24},{24,28},{28,32},{32,36}... | collective-permute-start | bytes 110600 | tf_op jit(solution)/shard_map/ppermute | solution.py:16
  36.2 5.7 %collective-permute-start.3 = (bf16[18,16,64,1]{2,1,3,0:T(8,128)(2,1)S(1)}, bf16[18,16,64,1]{2,1,3,0:T(8,128)(2,1)S(1)}, u32[]{:S(2)}, u32[]{:S(2)}) collective-permute-start(bf16[18,16,64,1]{2,1,3,0:T(8,128)(2,1)S(1)} %get-tuple-element.81), channel_id=1, source_target_pairs={{4,0},{8,4},{12,8},{16,12},{20,16},{24,20},{28,24},{32,28},{36,32}... | collective-permute-start | bytes 110600 | tf_op jit(solution)/shard_map/ppermute | solution.py:17
  58.9 12.0 %copy-start.3 = (bf16[27,64,64]{2,1,0:T(8,128)(2,1)S(1)}, bf16[27,64,64]{2,1,0:T(8,128)(2,1)}, u32[]{:S(2)}) copy-start(bf16[27,64,64]{2,1,0:T(8,128)(2,1)} %param.9) | copy-start | bytes 663556
  58.9 12.0 %copy-start.6 = (pred[8,17]{0,1:T(8,128)(4,1)S(1)}, pred[8,17]{0,1:T(8,128)(4,1)}, u32[]{:S(2)}) copy-start(pred[8,17]{0,1:T(8,128)(4,1)} %constant.75) | copy-start | bytes 412
  242.0 4.7 %copy-start.2 = (f32[16,64,64]{2,1,0:T(8,128)S(1)}, f32[16,64,64]{2,1,0:T(8,128)}, u32[]{:S(2)}) copy-start(f32[16,64,64]{2,1,0:T(8,128)} %param.11) | copy-start | bytes 786436
  256.7 32.6 %all-to-all-start.1 = ((f32[32,1,16384]{2,1,0:T(1,128)}), f32[32,1,16384]{2,1,0:T(1,128)}, u32[]{:S(2)}, u32[]{:S(2)}) async-start(f32[32,1,16384]{2,1,0:T(1,128)} %reshape.39), calls=%async_computation.1 | async-start | bytes 4194304 | tf_op jit(solution)/shard_map/all_to_all | solution.py:42
  296.6 3.1 copy-start.4
  296.6 3.1 copy-start.5
where the time goes:
time: 401 us; the launch traced here: 398 us
  matrix products  156 us (39%)
  local copies, waits for them, and re-layouts  82.2 us (20%)
  waiting for transfers between devices  44.8 us (11%)
  blocking collectives  37.1 us (9%)
  other arithmetic  33.3 us (8%)
  loops' own time  27.6 us (7%)
  starting transfers between devices  17.1 us (4%)
    conv_general_dilated x1, matrix products, per_device(): lax.conv_general_dilated(padded[None], kernel, (1, 1, 1), ((0, 0), (1, 1)...  82.5 us
    all_to_all x1, blocking collectives, summed_on_arrival(): pieces = lax.all_to_all(in_blocks(x, dim, devices), axis, 0, 0, tiled=True)  37.1 us
    dot_general x16, matrix products, finish(): branch = jnp.dot(mixed_row, inverse, precision=lax.Precision.HIGHEST)  32.8 us
    unnamed x20, local copies, waits for them, and re-layouts  28.7 us
    dot_general x16, matrix products, finish(): jnp.einsum('ch,zhx->zcx', mlp_out, hidden, preferred_element_type=jnp.flo...  28.3 us
    all_to_all x1, waiting for transfers between devices, sent_to_all(): return lax.all_to_all(copies, axis, split_axis=0, concat_axis=0, tiled=True)  27.7 us
    another operation x1, loops' own time, per_device(): return lax.map(finish, jnp.arange(rows_y, dtype=jnp.int32))  27.6 us
    conv_general_dilated x3, local copies, waits for them, and re-layouts, per_device(): lax.conv_general_dilated(padded[None], kernel, (1, 1, 1), ((0, 0), (1, 1)...  21.8 us
  transfers between devices with their start and end apart: 5, of which 4 were waited for; matrix products, arithmetic and copies ran while one was open for 0% of the time, Pallas kernels for 0%

commit v1 on v0

v1 whole, which is shorter than its diff:
```python
import functools
import math

import jax
import jax.numpy as jnp
import numpy as np
from jax import lax
from jax.experimental import pallas as pl
from jax.experimental.pallas import tpu as pltpu
from jax.sharding import PartitionSpec as P

BF = jnp.bfloat16
F32 = jnp.float32
LANES = 128
CH = 64
ROWS = 1024
PADDED = ROWS + 2 * CH
MODES = 16
HID = 256
VMEM = pltpu.VMEM


def params(mib):
    return pltpu.CompilerParams(vmem_limit_bytes=mib * 2**20)


def cost(flops, read):
    return pl.CostEstimate(flops=int(flops), bytes_accessed=int(read), transcendentals=0)


def tables(blocks, width):
    total = blocks * width
    places = np.arange(-1, total + 1, dtype=np.int64)
    orders = np.arange(MODES, dtype=np.int64)
    phase = (places[:, None] * orders[None, :]) % total
    angle = phase.astype(np.float32) * np.float32(2.0 * math.pi / total)
    both = np.concatenate([np.cos(angle), -np.sin(angle)], axis=1).astype(np.float32)
    inside = both.copy()
    inside[0] = 0
    inside[-1] = 0
    forward = np.zeros((blocks, width, 3, 4, 2 * MODES), np.float32)
    inverse = np.zeros((blocks, 2 * MODES, width), np.float32)
    weight = np.where(orders == 0, 1.0, 2.0).astype(np.float32) / np.float32(total)
    weight = np.concatenate([weight, weight])
    for b in range(blocks):
        for d in range(3):
            first = b * width - d + 1 + 1
            forward[b, :, d, :, :] = inside[first : first + width][:, None, :]
        inverse[b] = (both[b * width + 1 : (b + 1) * width + 1] * weight).T
    forward = forward.reshape(blocks, width, 3 * 4 * 2 * MODES).astype(jnp.bfloat16)
    inverse = np.tile(inverse, (1, 4, 1))
    high = inverse.astype(jnp.bfloat16)
    low = (inverse - high.astype(np.float32)).astype(jnp.bfloat16)
    return forward, np.concatenate([high, low], axis=1)


def band_kernel(w_ref, o_ref):
    zero = jnp.zeros((CH, CH), BF)
    for a in range(3):
        for zo in range(2):
            for d in range(3):
                parts = []
                for zi in range(4):
                    b = zi - zo
                    parts.append(w_ref[(3 * a + b) * 3 + d] if 0 <= b <= 2 else zero)
                o_ref[a * 128 + zo * 64 : a * 128 + zo * 64 + 64, d * 256 : d * 256 + 256] = (
                    jnp.concatenate(parts, axis=1)
                )


def banded(conv_w):
    return pl.pallas_call(
        band_kernel, out_shape=jax.ShapeDtypeStruct((384, 768), BF), name="band"
    )(conv_w)


def one_hot(height, pairs):
    x = lax.broadcasted_iota(jnp.int32, (height, LANES), 0)
    lane = lax.broadcasted_iota(jnp.int32, (height, LANES), 1)
    hit = jnp.zeros((height, LANES), F32)
    for row, column in pairs:
        hit = jnp.where((x == row) & (lane == column), 1.0, hit)
    return hit.astype(BF)


def group_mask(height, group):
    lane = lax.broadcasted_iota(jnp.int32, (height, LANES), 1)
    return lane // 32 == group


def dft_kernel(f_ref, t_ref, g_ref, own_ref, e_ref, tab_ref):
    for g in range(4):
        for d in range(3):
            part = t_ref[:, d * 128 : d * 128 + 128]
            tab_ref[g * 128 : g * 128 + 128, d * 128 : d * 128 + 128] = jnp.where(
                group_mask(128, g), part, jnp.zeros_like(part)
            )
    for i in range(4):
        for g in range(4):
            y = 4 * g + i
            tab_ref[g * 128 : g * 128 + 128, 384:512] = one_hot(
                128, [(127, 2 * y + 2), (0, 2 * y + 1)]
            )

        @pl.loop(0, 4)
        def _(r):
            at = pl.ds(pl.multiple_of(r * 256, 256), 256)
            left = jnp.concatenate([f_ref[4 * g + i, at, :] for g in range(4)], axis=1)
            out = jnp.dot(left, tab_ref[...], preferred_element_type=F32)
            for d in range(3):
                g_ref[i, d, at, :] = out[:, d * 128 : d * 128 + 128].astype(BF)
            own_ref[i, at, :] = out[:, 128:256]
            edge = out[:, 384:512].astype(BF)
            if i == 0:
                e_ref[at, :] = edge
            else:
                e_ref[at, :] = e_ref[at, :] + edge


def dft(field, table):
    return pl.pallas_call(
        dft_kernel,
        out_shape=(
            jax.ShapeDtypeStruct((4, 3, ROWS, LANES), BF),
            jax.ShapeDtypeStruct((4, ROWS, LANES), F32),
            jax.ShapeDtypeStruct((ROWS, LANES), BF),
        ),
        scratch_shapes=[VMEM((512, 512), BF)],
        compiler_params=params(32),
        cost_estimate=cost(4e9, 4e6),
        name="dft",
    )(field, table)


def halo_kernel(top_ref, bottom_ref, t_ref, e_in_ref, gt_ref, gb_ref, e_ref):
    def columns(pairs, group):
        parts = []
        for d in range(3):
            part = t_ref[:, d * 128 : d * 128 + 128]
            parts.append(jnp.where(group_mask(128, group), part, jnp.zeros_like(part)))
        return jnp.concatenate(parts + [one_hot(128, pairs)], axis=1)

    above = columns([(127, 0), (0, 127)], 0)
    below = columns([(127, 34), (0, 33)], 3)

    @pl.loop(0, 4)
    def _(r):
        at = pl.ds(pl.multiple_of(r * 256, 256), 256)
        up = jnp.dot(top_ref[at, :], above, preferred_element_type=F32).astype(BF)
        down = jnp.dot(bottom_ref[at, :], below, preferred_element_type=F32).astype(BF)
        for d in range(3):
            gt_ref[d, at, :] = up[:, d * 128 : d * 128 + 128]
            gb_ref[d, at, :] = down[:, d * 128 : d * 128 + 128]
        e_ref[at, :] = e_in_ref[at, :] + up[:, 384:512] + down[:, 384:512]


def halo_modes(top, bottom, table, edges):
    return pl.pallas_call(
        halo_kernel,
        out_shape=(
            jax.ShapeDtypeStruct((3, ROWS, LANES), BF),
            jax.ShapeDtypeStruct((3, ROWS, LANES), BF),
            jax.ShapeDtypeStruct((ROWS, LANES), BF),
        ),
        compiler_params=params(32),
        cost_estimate=cost(1e9, 1e6),
        name="halo_modes",
    )(top, bottom, table, edges)


def clear(x_ref, a1_ref, a2_ref, rows):
    zero = jnp.zeros((CH, LANES), BF)
    for r in range(rows):
        for d in range(3):
            x_ref[r, d, 0:CH, :] = zero
            x_ref[r, d, CH + ROWS : PADDED, :] = zero

    @pl.loop(0, 8)
    def _(g):
        at = pl.ds(pl.multiple_of(g * 128, 128), 128)
        a1_ref[at, :] = jnp.zeros((128, 256), F32)
        a2_ref[at, :] = jnp.zeros((128, 256), F32)


def band_conv(w_ref, x_ref, a1_ref, a2_ref, s_ref, half, emit, after):
    @pl.loop(0, half)
    def _(p):
        for g in range(8):
            r0 = g * 128
            at = slice(r0, r0 + 128)
            cells = jnp.concatenate(
                [
                    x_ref[p, :, r0 : r0 + 256, :].reshape(768, LANES),
                    x_ref[p + half, :, r0 : r0 + 256, :].reshape(768, LANES),
                ],
                axis=1,
            )
            part = jnp.dot(w_ref[...], cells, preferred_element_type=F32)
            done = a2_ref[at, :] + part[256:384]
            a2_ref[at, :] = a1_ref[at, :] + part[128:256]
            a1_ref[at, :] = part[0:128]
            emit(jnp.maximum(p - 2, 0), at, done[:, 0:128])
            emit(p + half - 2, at, done[:, 128:256])
            s_ref[jnp.minimum(p, 2), at, :] = done[:, 128:256]
            after(p, r0)

    for g in range(8):
        at = slice(g * 128, g * 128 + 128)
        emit(half - 2, at, a2_ref[at, 0:128] + s_ref[0, at, :])
        emit(half - 1, at, a1_ref[at, 0:128] + s_ref[1, at, :])


def spectral_kernel(w_ref, g_ref, own_ref, gt_ref, gb_ref, o_ref, x_ref, a1_ref, a2_ref, s_ref):
    clear(x_ref, a1_ref, a2_ref, 6)
    lane = lax.broadcasted_iota(jnp.int32, (256, LANES), 1)
    for r0 in range(0, ROWS, 256):
        src, dst = slice(r0, r0 + 256), slice(CH + r0, CH + r0 + 256)
        for d in range(3):
            for i in range(4):
                x_ref[i + 1, d, dst, :] = g_ref[i, d, src, :]
            x_ref[0, d, dst, :] = jnp.where(
                lane < 32, gt_ref[d, src, :], pltpu.roll(g_ref[3, d, src, :], 32, 1)
            )
            x_ref[5, d, dst, :] = jnp.where(
                lane >= 96, gb_ref[d, src, :], pltpu.roll(g_ref[0, d, src, :], 96, 1)
            )

    def emit(row, at, value):
        o_ref[row, at, :] = (value + own_ref[row, at, :]).astype(BF)

    band_conv(w_ref, x_ref, a1_ref, a2_ref, s_ref, 3, emit, lambda p, r0: None)


def conv_scratch(rows):
    return [
        VMEM((rows, 3, PADDED, LANES), BF),
        VMEM((ROWS, 256), F32),
        VMEM((ROWS, 256), F32),
        VMEM((3, ROWS, LANES), F32),
    ]


def spectral(band, modes, own, above, below):
    return pl.pallas_call(
        spectral_kernel,
        out_shape=jax.ShapeDtypeStruct((4, ROWS, LANES), BF),
        scratch_shapes=conv_scratch(6),
        compiler_params=params(48),
        cost_estimate=cost(4e9, 8e6),
        name="spectral",
    )(band, modes, own, above, below)


def lift_kernel(part, w_ref, f_ref, halo_ref, el_ref, er_ref, *rest):
    o_ref, x_ref, a1_ref, a2_ref, s_ref, ed_ref = rest[-6:]
    half = 5
    first = 8 * part
    clear(x_ref, a1_ref, a2_ref, 2 * half)
    lane = lax.broadcasted_iota(jnp.int32, (128, LANES), 1)
    halo_at = 0 if part == 0 else 9
    body = slice(CH, CH + ROWS)
    for r in range(10):
        if r == halo_at:
            x_ref[r, 1, body, :] = halo_ref[...]
        else:
            x_ref[r, 1, body, :] = f_ref[first + r - 1]
    for r0 in range(0, ROWS, 128):
        at = slice(r0, r0 + 128)
        ed_ref[at, :] = jnp.where(lane % 2 == 0, el_ref[at, :], er_ref[at, :])

    def build(r, r0):
        at = slice(CH + r0, CH + r0 + 128)
        mid = x_ref[r, 1, at, :]
        edge = pltpu.roll(ed_ref[r0 : r0 + 128, :], 128 - 2 * (first + r), 1)
        x_ref[r, 0, at, :] = jnp.where(lane == 0, edge, pltpu.roll(mid, 1, 1))
        x_ref[r, 2, at, :] = jnp.where(lane == 127, edge, pltpu.roll(mid, 127, 1))

    for r0 in range(0, ROWS, 128):
        build(0, r0)
        build(half, r0)

    def after(p, r0):
        later = jnp.minimum(p + 1, half - 1)
        build(later, r0)
        build(later + half, r0)

    def emit(row, at, value):
        same = x_ref[row + 1, 1, CH + at.start : CH + at.stop, :].astype(F32)
        o_ref[row, at, :] = (value + same).astype(BF)

    band_conv(w_ref, x_ref, a1_ref, a2_ref, s_ref, half, emit, after)


def lift(part, band, field, halo, left, right, into=None):
    whole = pl.BlockSpec(memory_space=VMEM)
    operands = [band, field, halo, left, right]
    specs = [whole] * 5
    aliases = {}
    if into is not None:
        operands.append(into)
        specs.append(pl.BlockSpec(memory_space=pl.ANY))
        aliases = {5: 0}
    return pl.pallas_call(
        functools.partial(lift_kernel, part),
        grid=(1,),
        in_specs=specs,
        out_specs=pl.BlockSpec((8, ROWS, LANES), lambda i: (part, 0, 0)),
        out_shape=jax.ShapeDtypeStruct((16, ROWS, LANES), BF),
        scratch_shapes=conv_scratch(10) + [VMEM((ROWS, LANES), BF)],
        input_output_aliases=aliases,
        compiler_params=params(48),
        cost_estimate=cost(8e9, 8e6),
        name="lift",
    )(*operands)


def split(x):
    high = x.astype(BF)
    return high, (x - high.astype(F32)).astype(BF)


def mix_kernel(p_ref, re_ref, im_ref, o_ref):
    total = p_ref[0].astype(F32)
    for i in range(1, 16):
        total = total + p_ref[i].astype(F32)
    both = jnp.concatenate([total[0:CH], total[CH : 2 * CH]], axis=1)
    lane = lax.broadcasted_iota(jnp.int32, (CH, 256), 1)
    is_re = lane % 32 < MODES
    turned = jnp.where(is_re, -pltpu.roll(both, 256 - MODES, 1), pltpu.roll(both, MODES, 1))
    bh, bl = split(both)
    th, tl = split(turned)
    mode = lane % MODES
    out = jnp.zeros((CH, 256), F32)
    for k in range(MODES):
        rh, rl = split(re_ref[k])
        ih, il = split(im_ref[k])
        dot = functools.partial(jnp.dot, preferred_element_type=F32)
        one = dot(rh, bh) + dot(ih, th) + (dot(rl, bh) + dot(il, th)) + (dot(rh, bl) + dot(ih, tl))
        out = jnp.where(mode == k, one, out)
    piece = jnp.concatenate([out[:, 0:128], out[:, 128:256]], axis=0).astype(BF)
    for i in range(16):
        o_ref[i] = piece


def mix(pieces, spec_re, spec_im):
    return pl.pallas_call(
        mix_kernel,
        out_shape=jax.ShapeDtypeStruct((16, 128, LANES), BF),
        compiler_params=params(16),
        cost_estimate=cost(5e8, 1e6),
        name="mix",
    )(pieces, spec_re, spec_im)


def finish_kernel(h_ref, l_ref, m_ref, inv_ref, up_ref, down_ref, o_ref, tab_ref):
    step = pl.program_id(0)
    ii = step % 2

    row = lax.broadcasted_iota(jnp.int32, (256, LANES), 0)
    inv = inv_ref[...]
    tab_ref[...] = jnp.where((row // 32) % 4 == step // 2, inv, jnp.zeros_like(inv))

    @pl.loop(0, 4)
    def _(q):
        at = pl.ds(pl.multiple_of(q * 256, 256), 256)
        m = m_ref[ii, at, :]
        branch = jnp.dot(
            jnp.concatenate([m, m], axis=1), tab_ref[...], preferred_element_type=F32
        )
        blended = (l_ref[0, at, :].astype(F32) + branch).astype(BF)
        outs = []
        for z in range(0, 4, 2):
            pair = jnp.concatenate(
                [blended[z * 64 : z * 64 + 64], blended[z * 64 + 64 : z * 64 + 128]], axis=1
            )
            hidden = jax.nn.gelu(
                jnp.dot(up_ref[...], pair, preferred_element_type=F32)
            ).astype(BF)
            out = pair.astype(F32) + jnp.dot(
                down_ref[...], hidden, preferred_element_type=F32
            )
            outs += [out[:, 0:128], out[:, 128:256]]
        o_ref[0, at, :] = jnp.concatenate(outs, axis=0).astype(BF)


def finish(which, lifted, mixed, inverse, mlp_in, mlp_out):
    layer = lambda s, h: (4 * (s // 2) + 2 * h[0] + s % 2, 0, 0)
    fixed = lambda *shape: pl.BlockSpec(shape, lambda s, h: (0,) * len(shape))
    return pl.pallas_call(
        finish_kernel,
        grid_spec=pltpu.PrefetchScalarGridSpec(
            num_scalar_prefetch=1,
            grid=(8,),
            in_specs=[
                pl.BlockSpec((1, ROWS, LANES), layer),
                fixed(2, ROWS, LANES),
                fixed(256, LANES),
                fixed(HID, CH),
                fixed(CH, HID),
            ],
            out_specs=pl.BlockSpec((1, ROWS, LANES), layer),
            scratch_shapes=[VMEM((256, LANES), BF)],
        ),
        out_shape=jax.ShapeDtypeStruct((16, ROWS, LANES), BF),
        input_output_aliases={1: 0},
        compiler_params=params(32),
        cost_estimate=cost(5e9, 6e6),
        name="finish",
    )(which, lifted, mixed, inverse, mlp_in, mlp_out)


def per_device(forward, inverse, field, conv_w, spec_re, spec_im, mlp_in, mlp_out):
    rows_y, depth, channels, width = field.shape
    blocks, layers = lax.axis_size("gx"), lax.axis_size("gy")
    place = lax.axis_index("gx")
    core = place % 2
    f = field.reshape(rows_y, depth * channels, width)

    up_y = [(i, i + 1) for i in range(layers - 1)]
    down_y = [(j, i) for i, j in up_y]
    up_x = [(i, i + 1) for i in range(blocks - 1)]
    down_x = [(j, i) for i, j in up_x]
    partner = [(i, i ^ 1) for i in range(blocks)]
    chips = [[i for i in range(c, blocks, 2)] for c in range(2)]

    top = lax.ppermute(f[rows_y - 1], "gy", up_y)
    bottom = lax.ppermute(f[0], "gy", down_y)
    table = lax.dynamic_index_in_dim(forward, place, 0, keepdims=False)
    inv = lax.dynamic_index_in_dim(inverse, place, 0, keepdims=False)
    band = banded(conv_w)

    modes, own, edges = dft(f, table)
    above, below, edges = halo_modes(top, bottom, table, edges)
    left = lax.ppermute(edges, "gx", up_x)
    right = lax.ppermute(edges, "gx", down_x)

    part = spectral(band, modes, own, above, below)
    mine = lax.dynamic_slice_in_dim(part, 2 * core, 2, 0)
    other = lax.dynamic_slice_in_dim(part, 2 - 2 * core, 2, 0)
    theirs = lax.ppermute(other, "gx", partner)
    chip_sum = (mine.astype(F32) + theirs.astype(F32)).astype(BF)
    pieces = lax.all_to_all(
        chip_sum.reshape(16, 128, LANES), "gx", 0, 0, axis_index_groups=chips, tiled=True
    )
    lifted = lift(0, band, f, top, left, right)
    copies = mix(pieces, spec_re, spec_im)
    mixed = lax.all_to_all(copies, "gx", 0, 0, axis_index_groups=chips, tiled=True)
    lifted = lift(1, band, f, bottom, left, right, lifted)
    mixed = mixed.reshape(2, ROWS, LANES)
    mixed_other = lax.ppermute(mixed, "gx", partner)
    which = core[None].astype(jnp.int32)
    result = finish(which, lifted, mixed, inv, mlp_in, mlp_out)
    result = finish(1 - which, result, mixed_other, inv, mlp_in, mlp_out)
    return result.reshape(field.shape)


def solution(mesh):
    in_specs = (P("gy", None, None, "gx"), P(), P(), P(), P(), P())
    out_specs = P("gy", None, None, "gx")
    forward, inverse = tables(mesh.shape["gx"], LANES)
    return jax.shard_map(
        functools.partial(per_device, jnp.asarray(forward), jnp.asarray(inverse)),
        mesh=mesh, in_specs=in_specs, out_specs=out_specs, check_vma=False,
    )
```

time: 401 us -> 129 us (0.32)
  matrix products: 156 us -> 0 us
  Pallas kernels: 0 us -> 83.4 us
  local copies, waits for them, and re-layouts: 82.2 us -> 10.8 us
  waiting for transfers between devices: 44.8 us -> 5.61 us
  blocking collectives: 37.1 us -> 0 us
  other arithmetic: 33.3 us -> 1.97 us
  loops' own time: 27.6 us -> 0 us
  starting transfers between devices: 17.1 us -> 26.5 us
    pallas_call x0 -> x9, Pallas kernels: none -> 83.4 us  [the longest x2 43 us: finish(): pl.pallas_call(finish_kernel, grid_spec=pltpu.PrefetchScalarGridSpec(num_...]
    conv_general_dilated x1 -> x0, matrix products: 82.5 us -> none  [per_device(): lax.conv_general_dilated(padded[None], kernel, (1, 1, 1), ((0, 0), (1, 1)...]
    dot_general x37 -> x0, matrix products: 73 us -> none  [the longest x16 32.8 us: finish(): branch = jnp.dot(mixed_row, inverse, precision=lax.Precision.HIGHEST)]
    all_to_all x1 -> x0, blocking collectives: 37.1 us -> none  [summed_on_arrival(): pieces = lax.all_to_all(in_blocks(x, dim, devices), axis, 0, 0, tiled=True)]
    another operation x1 -> x0, loops' own time: 27.6 us -> none  [per_device(): return lax.map(finish, jnp.arange(rows_y, dtype=jnp.int32))]
    all_to_all x1 -> x2, waiting for transfers between devices: 27.7 us -> 3.72 us  [the longest x1 3.72 us: per_device(): lax.all_to_all(chip_sum.reshape(16, 128, LANES), 'gx', 0, 0, axis_index_g...]
    conv_general_dilated x3 -> x0, local copies, waits for them, and re-layouts: 21.8 us -> none  [per_device(): lax.conv_general_dilated(padded[None], kernel, (1, 1, 1), ((0, 0), (1, 1)...]
    unnamed x20 -> x19, local copies, waits for them, and re-layouts: 28.7 us -> 7.14 us
  transfers between devices with their start and end apart: 5 -> 8, of which waited for: 4 -> 2; matrix products, arithmetic and copies ran while one was open for 0% -> 1% of each run, Pallas kernels for 0% -> 42%
where the time goes in v1:
time: 129 us; the launch traced here: 128 us
  Pallas kernels  83.4 us (65%)
  starting transfers between devices  26.5 us (21%)
  local copies, waits for them, and re-layouts  10.8 us (8%)
  waiting for transfers between devices  5.61 us (4%)
  other arithmetic  1.97 us (2%)
    pallas_call x2, Pallas kernels, finish(): pl.pallas_call(finish_kernel, grid_spec=pltpu.PrefetchScalarGridSpec(num_...  43 us
    pallas_call x2, Pallas kernels, lift(): pl.pallas_call(functools.partial(lift_kernel, part), grid=(1,), in_specs=...  23.2 us
    pallas_call x1, Pallas kernels, spectral(): pl.pallas_call(spectral_kernel, out_shape=jax.ShapeDtypeStruct((4, ROWS,...  7.16 us
    unnamed x19, local copies, waits for them, and re-layouts  7.14 us
    all_to_all x1, starting transfers between devices, per_device(): lax.all_to_all(chip_sum.reshape(16, 128, LANES), 'gx', 0, 0, axis_index_g...  6.84 us
    ppermute x1, starting transfers between devices, per_device(): top = lax.ppermute(f[rows_y - 1], 'gy', up_y)  5.02 us
    pallas_call x1, Pallas kernels, dft(): pl.pallas_call(dft_kernel, out_shape=(jax.ShapeDtypeStruct((4, 3, ROWS, L...  4.93 us
    ppermute x1, starting transfers between devices, per_device(): left = lax.ppermute(edges, 'gx', up_x)  4.08 us
  transfers between devices with their start and end apart: 8, of which 2 were waited for; matrix products, arithmetic and copies ran while one was open for 1% of the time, Pallas kernels for 42%

profile of v1, /device:TPU:1, one launch (start us, length us, event | category | flops | bytes accessed | tf_op | source)
XLA Modules:
  0.0 128.5 jit_solution(3817029361365114280)
XLA Ops:
  0.0 1.1 fusion
  1.1 1.3 %collective-permute-start = (bf16[1024,128]{1,0:T(8,128)(2,1)S(1)}, bf16[1024,128]{1,0:T(8,128)(2,1)S(1)}, u32[]{:S(2)}, u32[]{:S(2)}) collective-permute-start(bf16[1024,128]{1,0:T(8,128)(2,1)S(1)} %bitcast.18), channel_id=1, source_target_pairs={{1,0},{2,1},{3,2},{5,4},{6,5},{7,6},{9,8},{10,9},{11,10},{13,12},{... | collective-permute-start | bytes 786440 | tf_op jit(solution)/shard_map/ppermute | solution.py:427
  2.4 5.0 %collective-permute-start.1 = (bf16[1024,128]{1,0:T(8,128)(2,1)S(1)}, bf16[1024,128]{1,0:T(8,128)(2,1)S(1)}, u32[]{:S(2)}, u32[]{:S(2)}) collective-permute-start(bf16[1024,128]{1,0:T(8,128)(2,1)S(1)} %bitcast.17), channel_id=1, source_target_pairs={{0,1},{1,2},{2,3},{4,5},{5,6},{6,7},{8,9},{9,10},{10,11},{12,13},{... | collective-permute-start | bytes 786440 | tf_op jit(solution)/shard_map/ppermute | solution.py:426
  7.4 2.0 %band.1.w_ref = bf16[384,768]{1,0:T(8,128)(2,1)} custom-call(bf16[27,64,64]{2,1,0:T(8,128)(2,1)} %w_ref.1), custom_call_target="tpu_custom_call" | custom-call | tf_op jit(solution)/shard_map/band/pallas_call | solution.py:72
  10.3 2.2 %copy-done.3 = bf16[16,16,64,128]{3,2,1,0:T(8,128)(2,1)S(1)} copy-done((bf16[16,16,64,128]{3,2,1,0:T(8,128)(2,1)S(1)}, bf16[16,16,64,128]{3,2,1,0:T(8,128)(2,1)}, u32[]{:S(2)}) %copy-start.3) | copy-done | bytes 4194328
  12.5 4.9 %dft.1 = (bf16[4,3,1024,128]{3,2,1,0:T(8,128)(2,1)S(1)}, f32[4,1024,128]{2,1,0:T(8,128)S(1)}, bf16[1024,128]{1,0:T(8,128)(2,1)S(1)}) custom-call(bf16[16,1024,128]{2,1,0:T(8,128)(2,1)S(1)} %bitcast.13, bf16[128,384]{1,0:T(8,128)(2,1)S(1)} %dynamic-slice_bitcast_fusion.t_ref), custom_call_target="tpu_custom_call" | custom-call | flops 4000000000 | bytes 4000000 | tf_op jit(solution)/shard_map/dft/pallas_call | solution.py:121
  17.5 1.2 halo_modes.1
  19.1 7.2 %spectral.1 = bf16[4,1024,128]{2,1,0:T(8,128)(2,1)S(1)} custom-call(bf16[384,768]{1,0:T(8,128)(2,1)S(1)} %copy-done, bf16[4,3,1024,128]{3,2,1,0:T(8,128)(2,1)} %copy-done.7, f32[4,1024,128]{2,1,0:T(8,128)S(1)} %get-tuple-element.14.own_ref, bf16[3,1024,128]{2,1,0:T(8,128)(2,1)S(1)} %get-tuple-element.15.gt_ref, ...), custom_call_target="tpu_custom_call" | custom-call | flops 4000000000 | bytes 8000000 | tf_op jit(solution)/shard_map/spectral/pallas_call | solution.py:244
  27.1 1.0 collective-permute-start.4
  28.1 1.9 %collective-permute-done.4 = bf16[2,1024,128]{2,1,0:T(8,128)(2,1)} collective-permute-done((bf16[2,1024,128]{2,1,0:T(8,128)(2,1)}, bf16[2,1024,128]{2,1,0:T(8,128)(2,1)}, u32[]{:S(2)}, u32[]{:S(2)}) %collective-permute-start.4) | collective-permute-done | bytes 524320 | tf_op jit(solution)/shard_map/ppermute | solution.py:440
  30.0 2.0 %add_convert_fusion = bf16[2,1024,128]{2,1,0:T(8,128)(2,1)} fusion(bf16[2,1024,128]{2,1,0:T(8,128)(2,1)} %collective-permute-done.4, bf16[4,1024,128]{2,1,0:T(8,128)(2,1)S(1)} %spectral.1, s32[]{:T(128)S(6)} %select_n.21), kind=kLoop, calls=%fused_computation | loop fusion | flops 1048576 | bytes 1572868 | tf_op jit(solution)/shard_map/convert_element_type | solution.py:441
  32.0 6.8 %all-to-all-start = ((bf16[16,128,128]{2,1,0:T(8,128)(2,1)}), bf16[16,128,128]{2,1,0:T(8,128)(2,1)S(1)}, u32[]{:S(2)}, u32[]{:S(2)}) async-start(bf16[16,128,128]{2,1,0:T(8,128)(2,1)} %bitcast.16), calls=%async_computation | async-start | bytes 1048576 | tf_op jit(solution)/shard_map/all_to_all | solution.py:442
  38.8 4.1 %collective-permute-start.2 = (bf16[1024,128]{1,0:T(8,128)(2,1)S(1)}, bf16[1024,128]{1,0:T(8,128)(2,1)S(1)}, u32[]{:S(2)}, u32[]{:S(2)}) collective-permute-start(bf16[1024,128]{1,0:T(8,128)(2,1)S(1)} %get-tuple-element.12), channel_id=1, source_target_pairs={{0,4},{4,8},{8,12},{12,16},{16,20},{20,24},{24,28},{28,32},{32,36}... | collective-permute-start | bytes 786440 | tf_op jit(solution)/shard_map/ppermute | solution.py:434
  42.9 1.9 %collective-permute-start.3 = (bf16[1024,128]{1,0:T(8,128)(2,1)S(1)}, bf16[1024,128]{1,0:T(8,128)(2,1)}, u32[]{:S(2)}, u32[]{:S(2)}) collective-permute-start(bf16[1024,128]{1,0:T(8,128)(2,1)S(1)} %get-tuple-element.12), channel_id=1, source_target_pairs={{4,0},{8,4},{12,8},{16,12},{20,16},{24,20},{28,24},{32,28},{36,32}... | collective-permute-start | bytes 786440 | tf_op jit(solution)/shard_map/ppermute | solution.py:435
  45.8 3.7 %all-to-all-done.p_ref = bf16[16,128,128]{2,1,0:T(8,128)(2,1)S(1)} async-done(((bf16[16,128,128]{2,1,0:T(8,128)(2,1)}), bf16[16,128,128]{2,1,0:T(8,128)(2,1)S(1)}, u32[]{:S(2)}, u32[]{:S(2)}) %all-to-all-start) | async-done | bytes 524320 | tf_op jit(solution)/shard_map/all_to_all | solution.py:442
  49.5 2.0 %mix.1 = bf16[16,128,128]{2,1,0:T(8,128)(2,1)} custom-call(bf16[16,128,128]{2,1,0:T(8,128)(2,1)S(1)} %all-to-all-done.p_ref, f32[16,64,64]{2,1,0:T(8,128)S(1)} %copy-done.1, f32[16,64,64]{2,1,0:T(8,128)S(1)} %copy-done.2), custom_call_target="tpu_custom_call" | custom-call | flops 500000000 | bytes 1000000 | tf_op jit(solution)/shard_map/mix/pallas_call | solution.py:346
  51.5 3.6 %all-to-all-start.1 = ((bf16[16,128,128]{2,1,0:T(8,128)(2,1)}), bf16[16,128,128]{2,1,0:T(8,128)(2,1)S(1)}, u32[]{:S(2)}, u32[]{:S(2)}) async-start(bf16[16,128,128]{2,1,0:T(8,128)(2,1)} %mix.1), calls=%async_computation.1 | async-start | bytes 1048576 | tf_op jit(solution)/shard_map/all_to_all | solution.py:447
  55.1 2.2 %copy-done.4 = bf16[16,16,64,128]{3,2,1,0:T(8,128)(2,1)S(1)} copy-done((bf16[16,16,64,128]{3,2,1,0:T(8,128)(2,1)S(1)}, bf16[16,16,64,128]{3,2,1,0:T(8,128)(2,1)}, u32[]{:S(2)}) %copy-start.4) | copy-done | bytes 4194328
  57.3 11.5 %lift.2.rest_0_ = bf16[16,1024,128]{2,1,0:T(8,128)(2,1)} custom-call(bf16[384,768]{1,0:T(8,128)(2,1)S(1)} %copy-done, bf16[16,1024,128]{2,1,0:T(8,128)(2,1)S(1)} %bitcast.14, bf16[1024,128]{1,0:T(8,128)(2,1)S(1)} %collective-permute-done.1.top_ref.halo_ref, bf16[1024,128]{1,0:T(8,128)(2,1)S(1)} %collective-permute-done.2.el_ref, ...), custom_call_target="tpu_custom_call" | custom-call | flops 8000000000 | bytes 8000000 | tf_op jit(solution)/shard_map/lift/pallas_call | solution.py:303
  68.8 2.9 %collective-permute-start.5 = (bf16[2,1024,128]{2,1,0:T(8,128)(2,1)S(1)}, bf16[2,1024,128]{2,1,0:T(8,128)(2,1)S(1)}, u32[]{:S(2)}, u32[]{:S(2)}) collective-permute-start(bf16[2,1024,128]{2,1,0:T(8,128)(2,1)S(1)} %bitcast.11), channel_id=1, source_target_pairs={{0,4},{4,0},{8,12},{12,8},{16,20},{20,16},{24,28},{28,24},{32,36},... | collective-permute-start | bytes 1572872 | tf_op jit(solution)/shard_map/ppermute | solution.py:450
  71.7 2.2 %copy-done.5 = bf16[16,16,64,128]{3,2,1,0:T(8,128)(2,1)S(1)} copy-done((bf16[16,16,64,128]{3,2,1,0:T(8,128)(2,1)S(1)}, bf16[16,16,64,128]{3,2,1,0:T(8,128)(2,1)}, u32[]{:S(2)}) %copy-start.5) | copy-done | bytes 4194328
  73.8 11.6 %lift.3.l_ref = bf16[16,1024,128]{2,1,0:T(8,128)(2,1)} custom-call(bf16[384,768]{1,0:T(8,128)(2,1)S(1)} %copy-done, bf16[16,1024,128]{2,1,0:T(8,128)(2,1)S(1)} %bitcast.15, bf16[1024,128]{1,0:T(8,128)(2,1)S(1)} %collective-permute-done.bottom_ref.halo_ref, bf16[1024,128]{1,0:T(8,128)(2,1)S(1)} %collective-permute-done.2.el_ref, ...), custom_call_target="tpu_custom_call", output_to_operand_aliasing={{}: (5, {})} | custom-call | flops 8000000000 | bytes 8000000 | tf_op jit(solution)/shard_map/lift/pallas_call | solution.py:303
  85.5 21.5 %finish.2.l_ref = bf16[16,1024,128]{2,1,0:T(8,128)(2,1)} custom-call(s32[1]{0:T(128)} %bitcast.h_ref, bf16[16,1024,128]{2,1,0:T(8,128)(2,1)} %lift.3.l_ref, bf16[2,1024,128]{2,1,0:T(8,128)(2,1)S(1)} %bitcast.12, bf16[256,128]{1,0:T(8,128)(2,1)S(1)} %dynamic-slice_bitcast_fusion.1.inv_ref, ...), custom_call_target="tpu_custom_call", output_to_operand_aliasing={{}: (1, {})} | custom-call | flops 5000000000 | bytes 6000000 | tf_op jit(solution)/shard_map/finish/pallas_call | solution.py:389
  107.0 21.5 %finish.3 = bf16[16,1024,128]{2,1,0:T(8,128)(2,1)} custom-call(s32[1]{0:T(128)S(6)} %sub.6.h_ref, bf16[16,1024,128]{2,1,0:T(8,128)(2,1)} %finish.2.l_ref, bf16[2,1024,128]{2,1,0:T(8,128)(2,1)S(1)} %collective-permute-done.5.m_ref, bf16[256,128]{1,0:T(8,128)(2,1)S(1)} %dynamic-slice_bitcast_fusion.1.inv_ref, ...), custom_call_target="tpu_custom_call", output_to_operand_aliasing={{}: (1, {})} | custom-call | flops 5000000000 | bytes 6000000 | tf_op jit(solution)/shard_map/finish/pallas_call | solution.py:389
  (25 shorter events, 3.2 us)
Async XLA Ops:
  1.1 16.4 %collective-permute-start = (bf16[1024,128]{1,0:T(8,128)(2,1)S(1)}, bf16[1024,128]{1,0:T(8,128)(2,1)S(1)}, u32[]{:S(2)}, u32[]{:S(2)}) collective-permute-start(bf16[1024,128]{1,0:T(8,128)(2,1)S(1)} %bitcast.18), channel_id=1, source_target_pairs={{1,0},{2,1},{3,2},{5,4},{6,5},{7,6},{9,8},{10,9},{11,10},{13,12},{... | collective-permute-start | bytes 786440 | tf_op jit(solution)/shard_map/ppermute | solution.py:427
  2.4 15.1 %collective-permute-start.1 = (bf16[1024,128]{1,0:T(8,128)(2,1)S(1)}, bf16[1024,128]{1,0:T(8,128)(2,1)S(1)}, u32[]{:S(2)}, u32[]{:S(2)}) collective-permute-start(bf16[1024,128]{1,0:T(8,128)(2,1)S(1)} %bitcast.17), channel_id=1, source_target_pairs={{0,1},{1,2},{2,3},{4,5},{5,6},{6,7},{8,9},{9,10},{10,11},{12,13},{... | collective-permute-start | bytes 786440 | tf_op jit(solution)/shard_map/ppermute | solution.py:426
  10.3 2.2 %copy-start.3 = (bf16[16,16,64,128]{3,2,1,0:T(8,128)(2,1)S(1)}, bf16[16,16,64,128]{3,2,1,0:T(8,128)(2,1)}, u32[]{:S(2)}) copy-start(bf16[16,16,64,128]{3,2,1,0:T(8,128)(2,1)} %param.8) | copy-start | bytes 12582916
  12.5 6.6 %copy-start = (bf16[384,768]{1,0:T(8,128)(2,1)S(1)}, bf16[384,768]{1,0:T(8,128)(2,1)}, u32[]{:S(2)}) copy-start(bf16[384,768]{1,0:T(8,128)(2,1)} %band.1.w_ref) | copy-start | bytes 1769476
  17.5 1.7 %copy-start.7 = (bf16[4,3,1024,128]{3,2,1,0:T(8,128)(2,1)}, bf16[4,3,1024,128]{3,2,1,0:T(8,128)(2,1)S(1)}, u32[]{:S(2)}) copy-start(bf16[4,3,1024,128]{3,2,1,0:T(8,128)(2,1)S(1)} %get-tuple-element.13.g_ref) | copy-start | bytes 9437188
  19.1 25.7 %copy-start.8 = (bf16[256,64]{0,1:T(8,128)(2,1)S(1)}, bf16[256,64]{0,1:T(8,128)(2,1)}, u32[]{:S(2)}) copy-start(bf16[256,64]{0,1:T(8,128)(2,1)} %param.12) | copy-start | bytes 98308
  19.1 30.4 %copy-start.1 = (f32[16,64,64]{2,1,0:T(8,128)S(1)}, f32[16,64,64]{2,1,0:T(8,128)}, u32[]{:S(2)}) copy-start(f32[16,64,64]{2,1,0:T(8,128)} %re_ref.1) | copy-start | bytes 786436
  19.1 30.4 %copy-start.2 = (f32[16,64,64]{2,1,0:T(8,128)S(1)}, f32[16,64,64]{2,1,0:T(8,128)}, u32[]{:S(2)}) copy-start(f32[16,64,64]{2,1,0:T(8,128)} %im_ref.1) | copy-start | bytes 786436
  27.1 2.8 %collective-permute-start.4 = (bf16[2,1024,128]{2,1,0:T(8,128)(2,1)}, bf16[2,1024,128]{2,1,0:T(8,128)(2,1)}, u32[]{:S(2)}, u32[]{:S(2)}) collective-permute-start(bf16[2,1024,128]{2,1,0:T(8,128)(2,1)} %constant_dynamic-slice_fusion), channel_id=1, source_target_pairs={{0,4},{4,0},{8,12},{12,8},{16,20},{20,16},{24,28},{28,24},{32,36},... | collective-permute-start | bytes 1572872 | tf_op jit(solution)/shard_map/ppermute | solution.py:440
  32.0 17.6 %all-to-all-start = ((bf16[16,128,128]{2,1,0:T(8,128)(2,1)}), bf16[16,128,128]{2,1,0:T(8,128)(2,1)S(1)}, u32[]{:S(2)}, u32[]{:S(2)}) async-start(bf16[16,128,128]{2,1,0:T(8,128)(2,1)} %bitcast.16), calls=%async_computation | async-start | bytes 1048576 | tf_op jit(solution)/shard_map/all_to_all | solution.py:442
  38.8 16.3 %collective-permute-start.2 = (bf16[1024,128]{1,0:T(8,128)(2,1)S(1)}, bf16[1024,128]{1,0:T(8,128)(2,1)S(1)}, u32[]{:S(2)}, u32[]{:S(2)}) collective-permute-start(bf16[1024,128]{1,0:T(8,128)(2,1)S(1)} %get-tuple-element.12), channel_id=1, source_target_pairs={{0,4},{4,8},{8,12},{12,16},{16,20},{20,24},{24,28},{28,32},{32,36}... | collective-permute-start | bytes 786440 | tf_op jit(solution)/shard_map/ppermute | solution.py:434
  42.9 12.2 %collective-permute-start.3 = (bf16[1024,128]{1,0:T(8,128)(2,1)S(1)}, bf16[1024,128]{1,0:T(8,128)(2,1)}, u32[]{:S(2)}, u32[]{:S(2)}) collective-permute-start(bf16[1024,128]{1,0:T(8,128)(2,1)S(1)} %get-tuple-element.12), channel_id=1, source_target_pairs={{4,0},{8,4},{12,8},{16,12},{20,16},{24,20},{28,24},{32,28},{36,32}... | collective-permute-start | bytes 786440 | tf_op jit(solution)/shard_map/ppermute | solution.py:435
  51.5 17.3 %all-to-all-start.1 = ((bf16[16,128,128]{2,1,0:T(8,128)(2,1)}), bf16[16,128,128]{2,1,0:T(8,128)(2,1)S(1)}, u32[]{:S(2)}, u32[]{:S(2)}) async-start(bf16[16,128,128]{2,1,0:T(8,128)(2,1)} %mix.1), calls=%async_computation.1 | async-start | bytes 1048576 | tf_op jit(solution)/shard_map/all_to_all | solution.py:447
  55.1 2.2 %copy-start.4 = (bf16[16,16,64,128]{3,2,1,0:T(8,128)(2,1)S(1)}, bf16[16,16,64,128]{3,2,1,0:T(8,128)(2,1)}, u32[]{:S(2)}) copy-start(bf16[16,16,64,128]{3,2,1,0:T(8,128)(2,1)} %param.8) | copy-start | bytes 12582916
  68.8 38.2 %collective-permute-start.5 = (bf16[2,1024,128]{2,1,0:T(8,128)(2,1)S(1)}, bf16[2,1024,128]{2,1,0:T(8,128)(2,1)S(1)}, u32[]{:S(2)}, u32[]{:S(2)}) collective-permute-start(bf16[2,1024,128]{2,1,0:T(8,128)(2,1)S(1)} %bitcast.11), channel_id=1, source_target_pairs={{0,4},{4,0},{8,12},{12,8},{16,20},{20,16},{24,28},{28,24},{32,36},... | collective-permute-start | bytes 1572872 | tf_op jit(solution)/shard_map/ppermute | solution.py:450
  71.7 2.2 %copy-start.5 = (bf16[16,16,64,128]{3,2,1,0:T(8,128)(2,1)S(1)}, bf16[16,16,64,128]{3,2,1,0:T(8,128)(2,1)}, u32[]{:S(2)}) copy-start(bf16[16,16,64,128]{3,2,1,0:T(8,128)(2,1)} %param.8) | copy-start | bytes 12582916
  73.8 11.7 %copy-start.6 = (bf16[64,256]{1,0:T(8,128)(2,1)S(1)}, bf16[64,256]{1,0:T(8,128)(2,1)}, u32[]{:S(2)}) copy-start(bf16[64,256]{1,0:T(8,128)(2,1)} %down_ref.3) | copy-start | bytes 98308

commit v2 on v1

v2 whole, which is shorter than its diff:
```python
import functools
import math

import jax
import jax.numpy as jnp
import numpy as np
from jax import lax
from jax.experimental import pallas as pl
from jax.experimental.pallas import tpu as pltpu
from jax.sharding import PartitionSpec as P

BF = jnp.bfloat16
F32 = jnp.float32
LANES = 128
CH = 64
ROWS = 1024
PADDED = ROWS + 2 * CH
MODES = 16
HID = 256
CHUNK = 512
BATCH = 1
DFT_MIB = 46
VMEM = pltpu.VMEM


def params(mib):
    return pltpu.CompilerParams(vmem_limit_bytes=mib * 2**20)


def cost(flops, read):
    return pl.CostEstimate(flops=int(flops), bytes_accessed=int(read), transcendentals=0)


def tables(blocks, width):
    total = blocks * width
    places = np.arange(-1, total + 1, dtype=np.int64)
    orders = np.arange(MODES, dtype=np.int64)
    phase = (places[:, None] * orders[None, :]) % total
    angle = phase.astype(np.float32) * np.float32(2.0 * math.pi / total)
    both = np.concatenate([np.cos(angle), -np.sin(angle)], axis=1).astype(np.float32)
    inside = both.copy()
    inside[0] = 0
    inside[-1] = 0
    forward = np.zeros((blocks, width, 3, 4, 2 * MODES), np.float32)
    inverse = np.zeros((blocks, 2 * MODES, width), np.float32)
    weight = np.where(orders == 0, 1.0, 2.0).astype(np.float32) / np.float32(total)
    weight = np.concatenate([weight, weight])
    for b in range(blocks):
        for d in range(3):
            first = b * width - d + 1 + 1
            forward[b, :, d, :, :] = inside[first : first + width][:, None, :]
        inverse[b] = (both[b * width + 1 : (b + 1) * width + 1] * weight).T
    forward = forward.reshape(blocks, width, 3 * 4 * 2 * MODES).astype(jnp.bfloat16)
    inverse = np.tile(inverse, (1, 4, 1))
    high = inverse.astype(jnp.bfloat16)
    low = (inverse - high.astype(np.float32)).astype(jnp.bfloat16)
    return forward, np.concatenate([high, low], axis=1)


def band_kernel(w_ref, o_ref):
    zero = jnp.zeros((CH, CH), BF)
    for a in range(3):
        for zo in range(2):
            for d in range(3):
                parts = []
                for zi in range(4):
                    b = zi - zo
                    parts.append(w_ref[(3 * a + b) * 3 + d] if 0 <= b <= 2 else zero)
                o_ref[a * 128 + zo * 64 : a * 128 + zo * 64 + 64, d * 256 : d * 256 + 256] = (
                    jnp.concatenate(parts, axis=1)
                )


def banded(conv_w):
    return pl.pallas_call(
        band_kernel, out_shape=jax.ShapeDtypeStruct((384, 768), BF), name="band"
    )(conv_w)


def one_hot(height, pairs):
    x = lax.broadcasted_iota(jnp.int32, (height, LANES), 0)
    lane = lax.broadcasted_iota(jnp.int32, (height, LANES), 1)
    hit = jnp.zeros((height, LANES), F32)
    for row, column in pairs:
        hit = jnp.where((x == row) & (lane == column), 1.0, hit)
    return hit.astype(BF)


def group_mask(height, group):
    lane = lax.broadcasted_iota(jnp.int32, (height, LANES), 1)
    return lane // 32 == group


def dft_kernel(f_ref, t_ref, g_ref, own_ref, e_ref, tab_ref, f_buf, sem):
    fetch = [pltpu.make_async_copy(f_ref.at[y], f_buf.at[y], sem.at[y]) for y in range(16)]
    for i in range(4):
        for g in range(4):
            fetch[4 * g + i].start()
    for g in range(4):
        for d in range(3):
            part = t_ref[:, d * 128 : d * 128 + 128]
            tab_ref[g * 128 : g * 128 + 128, d * 128 : d * 128 + 128] = jnp.where(
                group_mask(128, g), part, jnp.zeros_like(part)
            )
    for i in range(4):
        for g in range(4):
            y = 4 * g + i
            tab_ref[g * 128 : g * 128 + 128, 384:512] = one_hot(
                128, [(127, 2 * y + 2), (0, 2 * y + 1)]
            )
        for g in range(4):
            fetch[4 * g + i].wait()

        @pl.loop(0, ROWS // CHUNK)
        def _(r):
            at = pl.ds(pl.multiple_of(r * CHUNK, CHUNK), CHUNK)
            left = jnp.concatenate([f_buf[4 * g + i, at, :] for g in range(4)], axis=1)
            out = jnp.dot(left, tab_ref[...], preferred_element_type=F32)
            for d in range(3):
                g_ref[i, d, at, :] = out[:, d * 128 : d * 128 + 128].astype(BF)
            own_ref[i, at, :] = out[:, 128:256]
            edge = out[:, 384:512].astype(BF)
            if i == 0:
                e_ref[at, :] = edge
            else:
                e_ref[at, :] = e_ref[at, :] + edge


def dft(field, table):
    return pl.pallas_call(
        dft_kernel,
        in_specs=[pl.BlockSpec(memory_space=pltpu.HBM), pl.BlockSpec(memory_space=VMEM)],
        out_shape=(
            jax.ShapeDtypeStruct((4, 3, ROWS, LANES), BF),
            jax.ShapeDtypeStruct((4, ROWS, LANES), F32),
            jax.ShapeDtypeStruct((ROWS, LANES), BF),
        ),
        scratch_shapes=[
            VMEM((512, 512), BF),
            VMEM((16, ROWS, LANES), BF),
            pltpu.SemaphoreType.DMA((16,)),
        ],
        compiler_params=params(DFT_MIB),
        cost_estimate=cost(4e9, 4e6),
        name="dft",
    )(field, table)


def halo_kernel(top_ref, bottom_ref, t_ref, e_in_ref, gt_ref, gb_ref, e_ref):
    def columns(pairs, group):
        parts = []
        for d in range(3):
            part = t_ref[:, d * 128 : d * 128 + 128]
            parts.append(jnp.where(group_mask(128, group), part, jnp.zeros_like(part)))
        return jnp.concatenate(parts + [one_hot(128, pairs)], axis=1)

    above = columns([(127, 0), (0, 127)], 0)
    below = columns([(127, 34), (0, 33)], 3)

    @pl.loop(0, ROWS // CHUNK)
    def _(r):
        at = pl.ds(pl.multiple_of(r * CHUNK, CHUNK), CHUNK)
        up = jnp.dot(top_ref[at, :], above, preferred_element_type=F32).astype(BF)
        down = jnp.dot(bottom_ref[at, :], below, preferred_element_type=F32).astype(BF)
        for d in range(3):
            gt_ref[d, at, :] = up[:, d * 128 : d * 128 + 128]
            gb_ref[d, at, :] = down[:, d * 128 : d * 128 + 128]
        e_ref[at, :] = e_in_ref[at, :] + up[:, 384:512] + down[:, 384:512]


def halo_modes(top, bottom, table, edges):
    return pl.pallas_call(
        halo_kernel,
        out_shape=(
            jax.ShapeDtypeStruct((3, ROWS, LANES), BF),
            jax.ShapeDtypeStruct((3, ROWS, LANES), BF),
            jax.ShapeDtypeStruct((ROWS, LANES), BF),
        ),
        compiler_params=params(32),
        cost_estimate=cost(1e9, 1e6),
        name="halo_modes",
    )(top, bottom, table, edges)


def clear(x_ref, a1_ref, a2_ref, rows):
    zero = jnp.zeros((CH, LANES), BF)
    for r in range(rows):
        for d in range(3):
            x_ref[r, d, 0:CH, :] = zero
            x_ref[r, d, CH + ROWS : PADDED, :] = zero

    @pl.loop(0, 8)
    def _(g):
        at = pl.ds(pl.multiple_of(g * 128, 128), 128)
        a1_ref[at, :] = jnp.zeros((128, 256), F32)
        a2_ref[at, :] = jnp.zeros((128, 256), F32)


def band_conv(w_ref, x_ref, a1_ref, a2_ref, s_ref, half, emit, before, after):
    @pl.loop(0, half)
    def _(p):
        before(p)
        for g0 in range(0, 8, BATCH):
            cells = []
            for g in range(g0, g0 + BATCH):
                for layer in (p, p + half):
                    rows = x_ref[layer, :, g * 128 : g * 128 + 256, :]
                    cells.append(rows.reshape(768, LANES))
            parts = jnp.dot(
                w_ref[...], jnp.concatenate(cells, axis=1), preferred_element_type=F32
            )
            for g in range(g0, g0 + BATCH):
                at = slice(g * 128, g * 128 + 128)
                part = parts[:, (g - g0) * 256 : (g - g0) * 256 + 256]
                done = a2_ref[at, :] + part[256:384]
                a2_ref[at, :] = a1_ref[at, :] + part[128:256]
                a1_ref[at, :] = part[0:128]
                emit(jnp.maximum(p - 2, 0), at, done[:, 0:128])
                emit(p + half - 2, at, done[:, 128:256])
                s_ref[jnp.minimum(p, 2), at, :] = done[:, 128:256]
                after(p, g * 128)

    for g in range(8):
        at = slice(g * 128, g * 128 + 128)
        emit(half - 2, at, a2_ref[at, 0:128] + s_ref[0, at, :])
        emit(half - 1, at, a1_ref[at, 0:128] + s_ref[1, at, :])


def conv_scratch(rows):
    return [
        VMEM((rows, 3, PADDED, LANES), BF),
        VMEM((ROWS, 256), F32),
        VMEM((ROWS, 256), F32),
        VMEM((3, ROWS, LANES), F32),
    ]


def spectral_kernel(
    at_ref, w_ref, g_ref, own_ref, gt_ref, gb_ref, mine_ref, other_ref,
    x_ref, a1_ref, a2_ref, s_ref, o_ref
):
    clear(x_ref, a1_ref, a2_ref, 6)
    lane = lax.broadcasted_iota(jnp.int32, (256, LANES), 1)
    for r0 in range(0, ROWS, 256):
        src, dst = slice(r0, r0 + 256), slice(CH + r0, CH + r0 + 256)
        for d in range(3):
            for i in range(4):
                x_ref[i + 1, d, dst, :] = g_ref[i, d, src, :]
            x_ref[0, d, dst, :] = jnp.where(
                lane < 32, gt_ref[d, src, :], pltpu.roll(g_ref[3, d, src, :], 32, 1)
            )
            x_ref[5, d, dst, :] = jnp.where(
                lane >= 96, gb_ref[d, src, :], pltpu.roll(g_ref[0, d, src, :], 96, 1)
            )
    shift = 2 * at_ref[0]

    def emit(row, at, value):
        o_ref[(row + shift) % 4, at, :] = (value + own_ref[row, at, :]).astype(BF)

    band_conv(w_ref, x_ref, a1_ref, a2_ref, s_ref, 3, emit, lambda p: None, lambda p, r0: None)
    mine_ref[...] = o_ref[0:2]
    other_ref[...] = o_ref[2:4]


def spectral(where, band, modes, own, above, below):
    half = jax.ShapeDtypeStruct((2, ROWS, LANES), BF)
    return pl.pallas_call(
        spectral_kernel,
        in_specs=[pl.BlockSpec(memory_space=pltpu.SMEM)] + [pl.BlockSpec(memory_space=VMEM)] * 5,
        out_shape=(half, half),
        scratch_shapes=conv_scratch(6) + [VMEM((4, ROWS, LANES), BF)],
        compiler_params=params(40),
        cost_estimate=cost(4e9, 8e6),
        name="spectral",
    )(where, band, modes, own, above, below)


def add_kernel(a_ref, b_ref, o_ref):
    o_ref[...] = (a_ref[...].astype(F32) + b_ref[...].astype(F32)).astype(BF)


def add(a, b):
    return pl.pallas_call(
        add_kernel,
        out_shape=jax.ShapeDtypeStruct(a.shape, BF),
        compiler_params=params(16),
        cost_estimate=cost(1e6, 2e6),
        name="add",
    )(a, b)


def lift_kernel(
    part, w_ref, f_ref, halo_ref, el_ref, er_ref, o_ref,
    w_buf, x_ref, a1_ref, a2_ref, s_ref, ed_ref, o_buf, sem, in_sem, out_sem
):
    half = 5
    first = 8 * part
    body = slice(CH, CH + ROWS)
    edges = [
        pltpu.make_async_copy(el_ref, ed_ref.at[0], in_sem.at[0]),
        pltpu.make_async_copy(er_ref, ed_ref.at[1], in_sem.at[1]),
    ]
    weights = pltpu.make_async_copy(w_ref, w_buf, in_sem.at[2])
    fetch = []
    for r in range(10):
        src = halo_ref if first + r in (0, 17) else f_ref.at[first + r - 1]
        fetch.append(pltpu.make_async_copy(src, x_ref.at[r, 1, body, :], sem.at[r]))
    later = [r + k for r in range(1, half) for k in (0, half) if r + k != half - 1]
    for copy in edges + [fetch[0], fetch[half], weights, fetch[half - 1]]:
        copy.start()
    for r in later:
        fetch[r].start()
    clear(x_ref, a1_ref, a2_ref, 2 * half)
    lane = lax.broadcasted_iota(jnp.int32, (128, LANES), 1)
    for copy in edges:
        copy.wait()
    for r0 in range(0, ROWS, 128):
        at = slice(r0, r0 + 128)
        ed_ref[0, at, :] = jnp.where(lane % 2 == 0, ed_ref[0, at, :], ed_ref[1, at, :])

    def build(r, r0):
        at = slice(CH + r0, CH + r0 + 128)
        mid = x_ref[r, 1, at, :]
        edge = pltpu.roll(ed_ref[0, r0 : r0 + 128, :], 128 - 2 * (first + r), 1)
        x_ref[r, 0, at, :] = jnp.where(lane == 0, edge, pltpu.roll(mid, 1, 1))
        x_ref[r, 2, at, :] = jnp.where(lane == 127, edge, pltpu.roll(mid, 127, 1))

    fetch[0].wait()
    fetch[half].wait()
    for r0 in range(0, ROWS, 128):
        build(0, r0)
        build(half, r0)
    weights.wait()
    fetch[half - 1].wait()

    def arrived(r):
        pltpu.make_async_copy(halo_ref, x_ref.at[r, 1, body, :], sem.at[r]).wait()

    def out(row):
        return pltpu.make_async_copy(o_buf.at[row], o_ref.at[row], out_sem.at[row])

    def before(p):
        @pl.when(p < half - 2)
        def _():
            arrived(p + 1)

        @pl.when(p < half - 1)
        def _():
            arrived(p + 1 + half)

        @pl.when(p > 2)
        def _():
            out(p - 3).start()
            out(p + half - 3).start()

    def after(p, r0):
        following = jnp.minimum(p + 1, half - 1)
        build(following, r0)
        build(following + half, r0)

    def emit(row, at, value):
        same = x_ref[row + 1, 1, CH + at.start : CH + at.stop, :].astype(F32)
        o_buf[row, at, :] = (value + same).astype(BF)

    band_conv(w_buf, x_ref, a1_ref, a2_ref, s_ref, half, emit, before, after)
    for row in (half - 3, 2 * half - 3, half - 2, half - 1):
        out(row).start()
    for row in range(8):
        out(row).wait()


def lift(part, band, field, halo, left, right):
    anywhere = pl.BlockSpec(memory_space=pl.ANY)
    return pl.pallas_call(
        functools.partial(lift_kernel, part),
        in_specs=[anywhere] * 5,
        out_specs=anywhere,
        out_shape=jax.ShapeDtypeStruct((8, ROWS, LANES), BF),
        scratch_shapes=[VMEM((384, 768), BF)]
        + conv_scratch(10)
        + [
            VMEM((2, ROWS, LANES), BF),
            VMEM((8, ROWS, LANES), BF),
            pltpu.SemaphoreType.DMA((10,)),
            pltpu.SemaphoreType.DMA((3,)),
            pltpu.SemaphoreType.DMA((8,)),
        ],
        compiler_params=params(60),
        cost_estimate=cost(8e9, 8e6),
        name="lift",
    )(band, field, halo, left, right)


def split(x):
    high = x.astype(BF)
    return high, (x - high.astype(F32)).astype(BF)


def mix_kernel(p_ref, re_ref, im_ref, o_ref):
    total = p_ref[0].astype(F32)
    for i in range(1, 16):
        total = total + p_ref[i].astype(F32)
    both = jnp.concatenate([total[0:CH], total[CH : 2 * CH]], axis=1)
    lane = lax.broadcasted_iota(jnp.int32, (CH, 256), 1)
    is_re = lane % 32 < MODES
    turned = jnp.where(is_re, -pltpu.roll(both, 256 - MODES, 1), pltpu.roll(both, MODES, 1))
    bh, bl = split(both)
    th, tl = split(turned)
    dot = functools.partial(jnp.dot, preferred_element_type=F32)
    rh, rl = split(re_ref[...].reshape(MODES * CH, CH))
    ih, il = split(im_ref[...].reshape(MODES * CH, CH))
    high = jnp.concatenate([rh, ih], axis=1)
    low = jnp.concatenate([rl, il], axis=1)
    cells = jnp.concatenate([bh, th], axis=0)
    rest = jnp.concatenate([bl, tl], axis=0)
    every = dot(
        jnp.concatenate([high, low], axis=1), jnp.concatenate([cells, cells], axis=0)
    ) + dot(high, rest)
    mode = lane % MODES
    out = every[0:CH]
    for k in range(1, MODES):
        out = jnp.where(mode == k, every[k * CH : k * CH + CH], out)
    piece = jnp.concatenate([out[:, 0:128], out[:, 128:256]], axis=0).astype(BF)
    for i in range(16):
        o_ref[i] = piece


def mix(pieces, spec_re, spec_im):
    return pl.pallas_call(
        mix_kernel,
        out_shape=jax.ShapeDtypeStruct((16, 128, LANES), BF),
        compiler_params=params(16),
        cost_estimate=cost(5e8, 1e6),
        name="mix",
    )(pieces, spec_re, spec_im)


GELU_ONE = math.sqrt(2.0 / math.pi)
GELU_THREE = GELU_ONE * 0.044715


def finish_kernel(h_ref, la_ref, lb_ref, m_ref, inv_ref, up_ref, down_ref, *rest):
    o_ref, tab_ref = rest[-2:]

    @pl.when(pl.program_id(0) == 0)
    def _():
        row = lax.broadcasted_iota(jnp.int32, (256, LANES), 0)
        inv = inv_ref[0]
        for g in range(4):
            tab_ref[:, g * 128 : g * 128 + 128] = jnp.where(
                (row // 32) % 4 == g, inv, jnp.zeros_like(inv)
            )

    dot = functools.partial(jnp.dot, preferred_element_type=F32)
    m = m_ref[0]
    branch = dot(jnp.concatenate([m, m], axis=1), tab_ref[...])
    lifted = jnp.concatenate([ref[g, 0] for ref in (la_ref, lb_ref) for g in range(2)], axis=1)
    blended = (lifted.astype(F32) + branch).astype(BF)
    cells = jnp.concatenate(
        [blended[z * CH : z * CH + CH] for z in range(CHUNK // CH)], axis=1
    )
    x = dot(up_ref[...], cells)
    bend = jnp.tanh(x * (GELU_ONE + GELU_THREE * (x * x)))
    hidden = (0.5 * x * bend + 0.5 * x).astype(BF)
    out = cells.astype(F32) + dot(down_ref[...], hidden)
    for z in range(CHUNK // CH):
        for g in range(4):
            c = (z * 4 + g) * 128
            o_ref[g, 0, z * CH : z * CH + CH, :] = out[:, c : c + 128].astype(BF)


def finish(half_at, where, first, last, mixed, inverse, mlp_in, mlp_out, into=None):
    chunks = ROWS // CHUNK
    layer = lambda s, h: (0, 2 * h[half_at] + s // chunks, s % chunks, 0)
    fixed = lambda *shape: pl.BlockSpec(shape, lambda s, h: (0,) * len(shape))
    operands = [where, first, last, mixed, inverse, mlp_in, mlp_out]
    specs = [
        pl.BlockSpec((2, 1, CHUNK, LANES), layer),
        pl.BlockSpec((2, 1, CHUNK, LANES), layer),
        pl.BlockSpec((1, CHUNK, LANES), lambda s, h: (s // chunks, s % chunks, 0)),
        pl.BlockSpec((1, 256, LANES), lambda s, h: (h[1], 0, 0)),
        fixed(HID, CH),
        fixed(CH, HID),
    ]
    if into is not None:
        operands.append(into)
        specs.append(pl.BlockSpec(memory_space=pltpu.HBM))
    return pl.pallas_call(
        finish_kernel,
        grid_spec=pltpu.PrefetchScalarGridSpec(
            num_scalar_prefetch=1,
            grid=(2 * chunks,),
            in_specs=specs,
            out_specs=pl.BlockSpec((4, 1, CHUNK, LANES), layer),
            scratch_shapes=[VMEM((256, 512), BF)],
        ),
        out_shape=jax.ShapeDtypeStruct((4, 4, ROWS, LANES), BF),
        input_output_aliases={} if into is None else {7: 0},
        compiler_params=params(58),
        cost_estimate=cost(5e9, 6e6),
        name="finish",
    )(*operands)


def per_device(forward, inverse, field, conv_w, spec_re, spec_im, mlp_in, mlp_out):
    rows_y, depth, channels, width = field.shape
    blocks, layers = lax.axis_size("gx"), lax.axis_size("gy")
    place = lax.axis_index("gx")
    core = place % 2
    f = field.reshape(rows_y, depth * channels, width)

    up_y = [(i, i + 1) for i in range(layers - 1)]
    down_y = [(j, i) for i, j in up_y]
    up_x = [(i, i + 1) for i in range(blocks - 1)]
    down_x = [(j, i) for i, j in up_x]
    partner = [(i, i ^ 1) for i in range(blocks)]
    chips = [[i for i in range(c, blocks, 2)] for c in range(2)]

    top = lax.ppermute(f[rows_y - 1], "gy", up_y)
    bottom = lax.ppermute(f[0], "gy", down_y)
    band = banded(conv_w)
    where = jnp.stack([core, place, 1 - core]).astype(jnp.int32)
    table = lax.dynamic_index_in_dim(forward, place, 0, keepdims=False)
    modes, own, edges = dft(f, table)
    above, below, edges = halo_modes(top, bottom, table, edges)
    left = lax.ppermute(edges, "gx", up_x)
    right = lax.ppermute(edges, "gx", down_x)
    mine, other = spectral(where, band, modes, own, above, below)
    other, left, right = lax.optimization_barrier((other, left, right))
    theirs = lax.ppermute(other, "gx", partner)
    chip_sum = add(mine, theirs)
    pieces = lax.all_to_all(
        chip_sum.reshape(16, 128, LANES), "gx", 0, 0, axis_index_groups=chips, tiled=True
    )
    first = lift(0, band, f, top, left, right)
    pieces, first = lax.optimization_barrier((pieces, first))
    copies = mix(pieces, spec_re, spec_im)
    mixed = lax.all_to_all(copies, "gx", 0, 0, axis_index_groups=chips, tiled=True)
    last = lift(1, band, f, bottom, left, right)
    mixed, last = lax.optimization_barrier((mixed, last))
    mixed = mixed.reshape(2, ROWS, LANES)
    mixed_other = lax.ppermute(mixed, "gx", partner)
    first = first.reshape(2, 4, ROWS, LANES)
    last = last.reshape(2, 4, ROWS, LANES)
    result = finish(0, where, first, last, mixed, inverse, mlp_in, mlp_out)
    result = finish(2, where, first, last, mixed_other, inverse, mlp_in, mlp_out, result)
    return result.reshape(field.shape)


def solution(mesh):
    in_specs = (P("gy", None, None, "gx"), P(), P(), P(), P(), P())
    out_specs = P("gy", None, None, "gx")
    forward, inverse = tables(mesh.shape["gx"], LANES)
    return jax.shard_map(
        functools.partial(per_device, jnp.asarray(forward), jnp.asarray(inverse)),
        mesh=mesh, in_specs=in_specs, out_specs=out_specs, check_vma=False,
    )
```

time: 129 us -> 95.6 us (0.74)
  Pallas kernels: 83.4 us -> 61.2 us
  local copies, waits for them, and re-layouts: 10.8 us -> 3.55 us
  waiting for transfers between devices: 5.61 us -> 1.92 us
  other arithmetic: 1.97 us -> 0.08 us
  starting transfers between devices: 26.5 us -> 27.8 us
    pallas_call x2, Pallas kernels: 43 us -> 20.7 us  [finish(): pl.pallas_call(finish_kernel, grid_spec=pltpu.PrefetchScalarGridSpec(num_...]
    unnamed x19 -> x23, local copies, waits for them, and re-layouts: 7.14 us -> 1.59 us
    all_to_all x1, waiting for transfers between devices: 3.72 us -> 0.01 us  [per_device(): lax.all_to_all(chip_sum.reshape(16, 128, LANES), 'gx', 0, 0, axis_index_g...]
    all_to_all x1, starting transfers between devices: 3.57 us -> 6.62 us  [per_device(): lax.all_to_all(copies, 'gx', 0, 0, axis_index_groups=chips, tiled=True)]
    convert_element_type x1 -> x0, other arithmetic: 1.97 us -> none  [per_device(): chip_sum = (mine.astype(F32) + theirs.astype(F32)).astype(BF)]
    ppermute x1, starting transfers between devices: 2.85 us -> 1.25 us  [per_device(): mixed_other = lax.ppermute(mixed, 'gx', partner)]
    ppermute x1, starting transfers between devices: 1.92 us -> 3.45 us  [per_device(): right = lax.ppermute(edges, 'gx', down_x)]
    pallas_call x4 -> x5, Pallas kernels: 35.3 us -> 36.1 us  [the longest x2 24.4 us: lift(): pl.pallas_call(functools.partial(lift_kernel, part), in_specs=[anywhere]...]
  transfers between devices with their start and end apart: 8 -> 8, of which waited for: 2 -> 1; matrix products, arithmetic and copies ran while one was open for 1% -> 2% of each run, Pallas kernels for 42% -> 50%
where the time goes in v2:
time: 95.6 us; the launch traced here: 94.8 us
  Pallas kernels  61.2 us (64%)
  starting transfers between devices  27.8 us (29%)
  local copies, waits for them, and re-layouts  3.55 us (4%)
  waiting for transfers between devices  1.92 us (2%)
    pallas_call x2, Pallas kernels, lift(): pl.pallas_call(functools.partial(lift_kernel, part), in_specs=[anywhere]...  24.4 us
    pallas_call x2, Pallas kernels, finish(): pl.pallas_call(finish_kernel, grid_spec=pltpu.PrefetchScalarGridSpec(num_...  20.7 us
    all_to_all x1, starting transfers between devices, per_device(): lax.all_to_all(chip_sum.reshape(16, 128, LANES), 'gx', 0, 0, axis_index_g...  7.69 us
    all_to_all x1, starting transfers between devices, per_device(): lax.all_to_all(copies, 'gx', 0, 0, axis_index_groups=chips, tiled=True)  6.62 us
    pallas_call x1, Pallas kernels, spectral(): pl.pallas_call(spectral_kernel, in_specs=[pl.BlockSpec(memory_space=pltpu...  5.95 us
    pallas_call x1, Pallas kernels, dft(): pl.pallas_call(dft_kernel, in_specs=[pl.BlockSpec(memory_space=pltpu.HBM)...  4.87 us
    ppermute x1, starting transfers between devices, per_device(): top = lax.ppermute(f[rows_y - 1], 'gy', up_y)  4.39 us
    ppermute x1, starting transfers between devices, per_device(): right = lax.ppermute(edges, 'gx', down_x)  3.45 us
  transfers between devices with their start and end apart: 8, of which 1 were waited for; matrix products, arithmetic and copies ran while one was open for 2% of the time, Pallas kernels for 50%

profile of v2, /device:TPU:1, one launch (start us, length us, event | category | flops | bytes accessed | tf_op | source)
XLA Modules:
  0.0 94.8 jit_solution(3334359706132322620)
XLA Ops:
  0.0 1.1 %fusion = (bf16[1,16,64,128]{3,2,1,0:T(8,128)(2,1)S(1)}, bf16[1,16,64,128]{3,2,1,0:T(8,128)(2,1)S(1)}) fusion(bf16[16,16,64,128]{3,2,1,0:T(8,128)(2,1)} %param.8), kind=kLoop, calls=%fused_computation.2 | loop fusion | bytes 1048576 | tf_op jit(solution)/shard_map/slice | solution.py:520
  1.1 4.4 %collective-permute-start = (bf16[1024,128]{1,0:T(8,128)(2,1)S(1)}, bf16[1024,128]{1,0:T(8,128)(2,1)S(1)}, u32[]{:S(2)}, u32[]{:S(2)}) collective-permute-start(bf16[1024,128]{1,0:T(8,128)(2,1)S(1)} %bitcast.16), channel_id=1, source_target_pairs={{0,1},{1,2},{2,3},{4,5},{5,6},{6,7},{8,9},{9,10},{10,11},{12,13},{... | collective-permute-start | bytes 786440 | tf_op jit(solution)/shard_map/ppermute | solution.py:519
  5.5 1.3 %collective-permute-start.1 = (bf16[1024,128]{1,0:T(8,128)(2,1)S(1)}, bf16[1024,128]{1,0:T(8,128)(2,1)S(1)}, u32[]{:S(2)}, u32[]{:S(2)}) collective-permute-start(bf16[1024,128]{1,0:T(8,128)(2,1)S(1)} %bitcast.15), channel_id=1, source_target_pairs={{1,0},{2,1},{3,2},{5,4},{6,5},{7,6},{9,8},{10,9},{11,10},{13,12},{... | collective-permute-start | bytes 786440 | tf_op jit(solution)/shard_map/ppermute | solution.py:520
  6.8 2.0 %band.1.w_ref = bf16[384,768]{1,0:T(8,128)(2,1)} custom-call(bf16[27,64,64]{2,1,0:T(8,128)(2,1)} %w_ref.1), custom_call_target="tpu_custom_call" | custom-call | tf_op jit(solution)/shard_map/band/pallas_call | solution.py:75
  8.8 0.9 dynamic-slice_bitcast_fusion.t_ref
  9.7 0.1 pad_add_fusion.at_ref.h_ref
  9.8 4.9 %dft.1 = (bf16[4,3,1024,128]{3,2,1,0:T(8,128)(2,1)S(1)}, f32[4,1024,128]{2,1,0:T(8,128)S(1)}, bf16[1024,128]{1,0:T(8,128)(2,1)S(1)}) custom-call(bf16[16,1024,128]{2,1,0:T(8,128)(2,1)} %bitcast.17, bf16[128,384]{1,0:T(8,128)(2,1)S(1)} %dynamic-slice_bitcast_fusion.t_ref), custom_call_target="tpu_custom_call" | custom-call | flops 4000000000 | bytes 4000000 | tf_op jit(solution)/shard_map/dft/pallas_call | solution.py:130
  14.7 0.9 halo_modes.1
  15.6 3.5 %collective-permute-start.3 = (bf16[1024,128]{1,0:T(8,128)(2,1)S(1)}, bf16[1024,128]{1,0:T(8,128)(2,1)S(1)}, u32[]{:S(2)}, u32[]{:S(2)}) collective-permute-start(bf16[1024,128]{1,0:T(8,128)(2,1)S(1)} %get-tuple-element.27), channel_id=1, source_target_pairs={{4,0},{8,4},{12,8},{16,12},{20,16},{24,20},{28,24},{32,28},{36,32}... | collective-permute-start | bytes 786440 | tf_op jit(solution)/shard_map/ppermute | solution.py:527
  19.1 3.0 %collective-permute-start.2 = (bf16[1024,128]{1,0:T(8,128)(2,1)S(1)}, bf16[1024,128]{1,0:T(8,128)(2,1)S(1)}, u32[]{:S(2)}, u32[]{:S(2)}) collective-permute-start(bf16[1024,128]{1,0:T(8,128)(2,1)S(1)} %get-tuple-element.27), channel_id=1, source_target_pairs={{0,4},{4,8},{8,12},{12,16},{16,20},{20,24},{24,28},{28,32},{32,36}... | collective-permute-start | bytes 786440 | tf_op jit(solution)/shard_map/ppermute | solution.py:526
  22.1 6.0 %spectral.1 = (bf16[2,1024,128]{2,1,0:T(8,128)(2,1)S(1)}, bf16[2,1024,128]{2,1,0:T(8,128)(2,1)S(1)}) custom-call(s32[3]{0:T(128)S(1)} %pad_add_fusion.at_ref.h_ref, bf16[384,768]{1,0:T(8,128)(2,1)S(1)} %copy-done, bf16[4,3,1024,128]{3,2,1,0:T(8,128)(2,1)S(1)} %get-tuple-element.20.g_ref, f32[4,1024,128]{2,1,0:T(8,128)S(1)} %get-tuple-element.21.own_ref, ...), custom_call_target="tpu_custom_call" | custom-call | flops 4000000000 | bytes 8000000 | tf_op jit(solution)/shard_map/spectral/pallas_call | solution.py:267
  28.1 0.1 collective-permute-start.4
  28.2 1.9 %collective-permute-done.4.b_ref = bf16[2,1024,128]{2,1,0:T(8,128)(2,1)S(1)} collective-permute-done((bf16[2,1024,128]{2,1,0:T(8,128)(2,1)S(1)}, bf16[2,1024,128]{2,1,0:T(8,128)(2,1)S(1)}, u32[]{:S(2)}, u32[]{:S(2)}) %collective-permute-start.4) | collective-permute-done | bytes 524320 | tf_op jit(solution)/shard_map/ppermute | solution.py:530
  30.1 0.9 add.15
  31.0 7.7 %all-to-all-start = ((bf16[16,128,128]{2,1,0:T(8,128)(2,1)}), bf16[16,128,128]{2,1,0:T(8,128)(2,1)S(1)}, u32[]{:S(2)}, u32[]{:S(2)}) async-start(bf16[16,128,128]{2,1,0:T(8,128)(2,1)} %bitcast.7), calls=%async_computation | async-start | bytes 1048576 | tf_op jit(solution)/shard_map/all_to_all | solution.py:532
  38.8 12.2 %lift.2 = bf16[8,1024,128]{2,1,0:T(8,128)(2,1)} custom-call(bf16[384,768]{1,0:T(8,128)(2,1)} %band.1.w_ref, bf16[16,1024,128]{2,1,0:T(8,128)(2,1)} %bitcast.18, bf16[1024,128]{1,0:T(8,128)(2,1)} %copy-done.5, bf16[1024,128]{1,0:T(8,128)(2,1)} %copy-done.10, bf16[1024,128]{1,0:T(8,128)(2,1)} %copy-done.9), custom_call_target="tpu_custom_call" | custom-call | flops 8000000000 | bytes 8000000 | tf_op jit(solution)/shard_map/lift/pallas_call | solution.py:374
  51.0 1.4 %mix.1 = bf16[16,128,128]{2,1,0:T(8,128)(2,1)} custom-call(bf16[16,128,128]{2,1,0:T(8,128)(2,1)S(1)} %all-to-all-done.p_ref, f32[16,64,64]{2,1,0:T(8,128)S(1)} %copy-done.1, f32[16,64,64]{2,1,0:T(8,128)S(1)} %copy-done.2), custom_call_target="tpu_custom_call" | custom-call | flops 500000000 | bytes 1000000 | tf_op jit(solution)/shard_map/mix/pallas_call | solution.py:429
  52.4 6.6 %all-to-all-start.1 = ((bf16[16,128,128]{2,1,0:T(8,128)(2,1)}), bf16[16,128,128]{2,1,0:T(8,128)(2,1)S(1)}, u32[]{:S(2)}, u32[]{:S(2)}) async-start(bf16[16,128,128]{2,1,0:T(8,128)(2,1)} %mix.1), calls=%async_computation.1 | async-start | bytes 1048576 | tf_op jit(solution)/shard_map/all_to_all | solution.py:538
  59.1 12.2 %lift.3 = bf16[8,1024,128]{2,1,0:T(8,128)(2,1)} custom-call(bf16[384,768]{1,0:T(8,128)(2,1)} %band.1.w_ref, bf16[16,1024,128]{2,1,0:T(8,128)(2,1)} %bitcast.19, bf16[1024,128]{1,0:T(8,128)(2,1)} %copy-done.4, bf16[1024,128]{1,0:T(8,128)(2,1)} %copy-done.10, bf16[1024,128]{1,0:T(8,128)(2,1)} %copy-done.9), custom_call_target="tpu_custom_call" | custom-call | flops 8000000000 | bytes 8000000 | tf_op jit(solution)/shard_map/lift/pallas_call | solution.py:374
  71.3 1.3 %collective-permute-start.5 = (bf16[2,1024,128]{2,1,0:T(8,128)(2,1)S(1)}, bf16[2,1024,128]{2,1,0:T(8,128)(2,1)S(1)}, u32[]{:S(2)}, u32[]{:S(2)}) collective-permute-start(bf16[2,1024,128]{2,1,0:T(8,128)(2,1)S(1)} %bitcast.13), channel_id=1, source_target_pairs={{0,4},{4,0},{8,12},{12,8},{16,20},{20,16},{24,28},{28,24},{32,36},... | collective-permute-start | bytes 1572872 | tf_op jit(solution)/shard_map/ppermute | solution.py:542
  72.6 0.7 copy.11.up_ref
  73.3 10.4 %finish.2.rest_0_ = bf16[4,4,1024,128]{3,2,1,0:T(8,128)(2,1)} custom-call(s32[3]{0:T(128)} %copy-done.3, bf16[2,4,1024,128]{3,2,1,0:T(8,128)(2,1)} %bitcast.20, bf16[2,4,1024,128]{3,2,1,0:T(8,128)(2,1)} %bitcast.22, bf16[2,1024,128]{2,1,0:T(8,128)(2,1)} %bitcast.14, bf16[32,256,128]{2,1,0:T(8,128)(2,1)} %constant.30.clone.inv_ref, ...), custom_call_target="tpu_custom_call" | custom-call | flops 5000000000 | bytes 6000000 | tf_op jit(solution)/shard_map/finish/pallas_call | solution.py:488
  83.7 0.8 copy-done.8
  84.5 10.4 %finish.3 = bf16[4,4,1024,128]{3,2,1,0:T(8,128)(2,1)} custom-call(s32[3]{0:T(128)} %copy-done.3, bf16[2,4,1024,128]{3,2,1,0:T(8,128)(2,1)} %bitcast.21, bf16[2,4,1024,128]{3,2,1,0:T(8,128)(2,1)} %bitcast.23, bf16[2,1024,128]{2,1,0:T(8,128)(2,1)} %copy-done.8, bf16[32,256,128]{2,1,0:T(8,128)(2,1)} %constant.30.clone.inv_ref, ...), custom_call_target="tpu_custom_call", output_to_operand_aliasing={{}: (7, {})} | custom-call | flops 5000000000 | bytes 6000000 | tf_op jit(solution)/shard_map/finish/pallas_call | solution.py:488
  (28 shorter events, 0.1 us)
Async XLA Ops:
  1.1 13.6 %collective-permute-start = (bf16[1024,128]{1,0:T(8,128)(2,1)S(1)}, bf16[1024,128]{1,0:T(8,128)(2,1)S(1)}, u32[]{:S(2)}, u32[]{:S(2)}) collective-permute-start(bf16[1024,128]{1,0:T(8,128)(2,1)S(1)} %bitcast.16), channel_id=1, source_target_pairs={{0,1},{1,2},{2,3},{4,5},{5,6},{6,7},{8,9},{9,10},{10,11},{12,13},{... | collective-permute-start | bytes 786440 | tf_op jit(solution)/shard_map/ppermute | solution.py:519
  5.5 9.2 %collective-permute-start.1 = (bf16[1024,128]{1,0:T(8,128)(2,1)S(1)}, bf16[1024,128]{1,0:T(8,128)(2,1)S(1)}, u32[]{:S(2)}, u32[]{:S(2)}) collective-permute-start(bf16[1024,128]{1,0:T(8,128)(2,1)S(1)} %bitcast.15), channel_id=1, source_target_pairs={{1,0},{2,1},{3,2},{5,4},{6,5},{7,6},{9,8},{10,9},{11,10},{13,12},{... | collective-permute-start | bytes 786440 | tf_op jit(solution)/shard_map/ppermute | solution.py:520
  9.8 12.3 %copy-start.3 = (s32[3]{0:T(128)}, s32[3]{0:T(128)S(1)}, u32[]{:S(2)}) copy-start(s32[3]{0:T(128)S(1)} %pad_add_fusion.at_ref.h_ref) | copy-start | bytes 40
  14.7 7.4 %copy-start = (bf16[384,768]{1,0:T(8,128)(2,1)S(1)}, bf16[384,768]{1,0:T(8,128)(2,1)}, u32[]{:S(2)}) copy-start(bf16[384,768]{1,0:T(8,128)(2,1)} %band.1.w_ref) | copy-start | bytes 1769476
  14.7 13.4 %copy-start.5 = (bf16[1024,128]{1,0:T(8,128)(2,1)}, bf16[1024,128]{1,0:T(8,128)(2,1)S(1)}, u32[]{:S(2)}) copy-start(bf16[1024,128]{1,0:T(8,128)(2,1)S(1)} %collective-permute-done.top_ref.halo_ref) | copy-start | bytes 786436
  14.7 13.4 %copy-start.4 = (bf16[1024,128]{1,0:T(8,128)(2,1)}, bf16[1024,128]{1,0:T(8,128)(2,1)S(1)}, u32[]{:S(2)}) copy-start(bf16[1024,128]{1,0:T(8,128)(2,1)S(1)} %collective-permute-done.1.bottom_ref.halo_ref) | copy-start | bytes 786436
  15.6 12.5 %collective-permute-start.3 = (bf16[1024,128]{1,0:T(8,128)(2,1)S(1)}, bf16[1024,128]{1,0:T(8,128)(2,1)S(1)}, u32[]{:S(2)}, u32[]{:S(2)}) collective-permute-start(bf16[1024,128]{1,0:T(8,128)(2,1)S(1)} %get-tuple-element.27), channel_id=1, source_target_pairs={{4,0},{8,4},{12,8},{16,12},{20,16},{24,20},{28,24},{32,28},{36,32}... | collective-permute-start | bytes 786440 | tf_op jit(solution)/shard_map/ppermute | solution.py:527
  19.1 9.0 %collective-permute-start.2 = (bf16[1024,128]{1,0:T(8,128)(2,1)S(1)}, bf16[1024,128]{1,0:T(8,128)(2,1)S(1)}, u32[]{:S(2)}, u32[]{:S(2)}) collective-permute-start(bf16[1024,128]{1,0:T(8,128)(2,1)S(1)} %get-tuple-element.27), channel_id=1, source_target_pairs={{0,4},{4,8},{8,12},{12,16},{16,20},{20,24},{24,28},{28,32},{32,36}... | collective-permute-start | bytes 786440 | tf_op jit(solution)/shard_map/ppermute | solution.py:526
  28.1 10.6 %copy-start.9 = (bf16[1024,128]{1,0:T(8,128)(2,1)}, bf16[1024,128]{1,0:T(8,128)(2,1)S(1)}, u32[]{:S(2)}) copy-start(bf16[1024,128]{1,0:T(8,128)(2,1)S(1)} %collective-permute-done.3.er_ref) | copy-start | bytes 786436
  28.1 10.6 %copy-start.10 = (bf16[1024,128]{1,0:T(8,128)(2,1)}, bf16[1024,128]{1,0:T(8,128)(2,1)S(1)}, u32[]{:S(2)}) copy-start(bf16[1024,128]{1,0:T(8,128)(2,1)S(1)} %collective-permute-done.2.el_ref) | copy-start | bytes 786436
  28.1 2.0 %collective-permute-start.4 = (bf16[2,1024,128]{2,1,0:T(8,128)(2,1)S(1)}, bf16[2,1024,128]{2,1,0:T(8,128)(2,1)S(1)}, u32[]{:S(2)}, u32[]{:S(2)}) collective-permute-start(bf16[2,1024,128]{2,1,0:T(8,128)(2,1)S(1)} %get-tuple-element.28), channel_id=1, source_target_pairs={{0,4},{4,0},{8,12},{12,8},{16,20},{20,16},{24,28},{28,24},{32,36},... | collective-permute-start | bytes 1572872 | tf_op jit(solution)/shard_map/ppermute | solution.py:530
  31.0 19.9 %all-to-all-start = ((bf16[16,128,128]{2,1,0:T(8,128)(2,1)}), bf16[16,128,128]{2,1,0:T(8,128)(2,1)S(1)}, u32[]{:S(2)}, u32[]{:S(2)}) async-start(bf16[16,128,128]{2,1,0:T(8,128)(2,1)} %bitcast.7), calls=%async_computation | async-start | bytes 1048576 | tf_op jit(solution)/shard_map/all_to_all | solution.py:532
  38.8 12.2 %copy-start.1 = (f32[16,64,64]{2,1,0:T(8,128)S(1)}, f32[16,64,64]{2,1,0:T(8,128)}, u32[]{:S(2)}) copy-start(f32[16,64,64]{2,1,0:T(8,128)} %re_ref.1) | copy-start | bytes 786436
  38.8 12.2 %copy-start.2 = (f32[16,64,64]{2,1,0:T(8,128)S(1)}, f32[16,64,64]{2,1,0:T(8,128)}, u32[]{:S(2)}) copy-start(f32[16,64,64]{2,1,0:T(8,128)} %im_ref.1) | copy-start | bytes 786436
  52.4 18.9 %all-to-all-start.1 = ((bf16[16,128,128]{2,1,0:T(8,128)(2,1)}), bf16[16,128,128]{2,1,0:T(8,128)(2,1)S(1)}, u32[]{:S(2)}, u32[]{:S(2)}) async-start(bf16[16,128,128]{2,1,0:T(8,128)(2,1)} %mix.1), calls=%async_computation.1 | async-start | bytes 1048576 | tf_op jit(solution)/shard_map/all_to_all | solution.py:538
  59.1 13.5 %copy-start.7 = (bf16[256,64]{0,1:T(8,128)(2,1)S(1)}, bf16[256,64]{0,1:T(8,128)(2,1)}, u32[]{:S(2)}) copy-start(bf16[256,64]{0,1:T(8,128)(2,1)} %param.12) | copy-start | bytes 98308
  71.3 2.0 %copy-start.6 = (bf16[16,128,128]{2,1,0:T(8,128)(2,1)}, bf16[16,128,128]{2,1,0:T(8,128)(2,1)S(1)}, u32[]{:S(2)}) copy-start(bf16[16,128,128]{2,1,0:T(8,128)(2,1)S(1)} %all-to-all-done.1) | copy-start | bytes 1572868
  71.3 12.4 %collective-permute-start.5 = (bf16[2,1024,128]{2,1,0:T(8,128)(2,1)S(1)}, bf16[2,1024,128]{2,1,0:T(8,128)(2,1)S(1)}, u32[]{:S(2)}, u32[]{:S(2)}) collective-permute-start(bf16[2,1024,128]{2,1,0:T(8,128)(2,1)S(1)} %bitcast.13), channel_id=1, source_target_pairs={{0,4},{4,0},{8,12},{12,8},{16,20},{20,16},{24,28},{28,24},{32,36},... | collective-permute-start | bytes 1572872 | tf_op jit(solution)/shard_map/ppermute | solution.py:542
  83.7 0.8 copy-start.8

commit v3 on v2

--- a/solution.py
+++ b/solution.py
@@ -18,8 +18,6 @@
 MODES = 16
 HID = 256
 CHUNK = 512
-BATCH = 1
-DFT_MIB = 46
 VMEM = pltpu.VMEM
 
 
@@ -71,12 +69,6 @@
                 )
 
 
-def banded(conv_w):
-    return pl.pallas_call(
-        band_kernel, out_shape=jax.ShapeDtypeStruct((384, 768), BF), name="band"
-    )(conv_w)
-
-
 def one_hot(height, pairs):
     x = lax.broadcasted_iota(jnp.int32, (height, LANES), 0)
     lane = lax.broadcasted_iota(jnp.int32, (height, LANES), 1)
@@ -91,11 +83,12 @@
     return lane // 32 == group
 
 
-def dft_kernel(f_ref, t_ref, g_ref, own_ref, e_ref, tab_ref, f_buf, sem):
+def dft_kernel(f_ref, t_ref, w_ref, g_ref, own_ref, e_ref, band_ref, tab_ref, f_buf, sem):
     fetch = [pltpu.make_async_copy(f_ref.at[y], f_buf.at[y], sem.at[y]) for y in range(16)]
     for i in range(4):
         for g in range(4):
             fetch[4 * g + i].start()
+    band_kernel(w_ref, band_ref)
     for g in range(4):
         for d in range(3):
             part = t_ref[:, d * 128 : d * 128 + 128]
@@ -126,24 +119,25 @@
                 e_ref[at, :] = e_ref[at, :] + edge
 
 
-def dft(field, table):
+def dft(field, table, conv_w):
     return pl.pallas_call(
         dft_kernel,
-        in_specs=[pl.BlockSpec(memory_space=pltpu.HBM), pl.BlockSpec(memory_space=VMEM)],
+        in_specs=[pl.BlockSpec(memory_space=pltpu.HBM)] + [pl.BlockSpec(memory_space=VMEM)] * 2,
         out_shape=(
             jax.ShapeDtypeStruct((4, 3, ROWS, LANES), BF),
             jax.ShapeDtypeStruct((4, ROWS, LANES), F32),
             jax.ShapeDtypeStruct((ROWS, LANES), BF),
+            jax.ShapeDtypeStruct((384, 768), BF),
         ),
         scratch_shapes=[
             VMEM((512, 512), BF),
             VMEM((16, ROWS, LANES), BF),
             pltpu.SemaphoreType.DMA((16,)),
         ],
-        compiler_params=params(DFT_MIB),
+        compiler_params=params(46),
         cost_estimate=cost(4e9, 4e6),
         name="dft",
-    )(field, table)
+    )(field, table, conv_w)
 
 
 def halo_kernel(top_ref, bottom_ref, t_ref, e_in_ref, gt_ref, gb_ref, e_ref):
@@ -182,13 +176,7 @@
     )(top, bottom, table, edges)
 
 
-def clear(x_ref, a1_ref, a2_ref, rows):
-    zero = jnp.zeros((CH, LANES), BF)
-    for r in range(rows):
-        for d in range(3):
-            x_ref[r, d, 0:CH, :] = zero
-            x_ref[r, d, CH + ROWS : PADDED, :] = zero
-
+def clear(a1_ref, a2_ref):
     @pl.loop(0, 8)
     def _(g):
         at = pl.ds(pl.multiple_of(g * 128, 128), 128)
@@ -196,39 +184,34 @@
         a2_ref[at, :] = jnp.zeros((128, 256), F32)
 
 
-def band_conv(w_ref, x_ref, a1_ref, a2_ref, s_ref, half, emit, before, after):
-    @pl.loop(0, half)
-    def _(p):
-        before(p)
-        for g0 in range(0, 8, BATCH):
-            cells = []
-            for g in range(g0, g0 + BATCH):
-                for layer in (p, p + half):
-                    rows = x_ref[layer, :, g * 128 : g * 128 + 256, :]
-                    cells.append(rows.reshape(768, LANES))
-            parts = jnp.dot(
-                w_ref[...], jnp.concatenate(cells, axis=1), preferred_element_type=F32
-            )
-            for g in range(g0, g0 + BATCH):
-                at = slice(g * 128, g * 128 + 128)
-                part = parts[:, (g - g0) * 256 : (g - g0) * 256 + 256]
-                done = a2_ref[at, :] + part[256:384]
-                a2_ref[at, :] = a1_ref[at, :] + part[128:256]
-                a1_ref[at, :] = part[0:128]
-                emit(jnp.maximum(p - 2, 0), at, done[:, 0:128])
-                emit(p + half - 2, at, done[:, 128:256])
-                s_ref[jnp.minimum(p, 2), at, :] = done[:, 128:256]
-                after(p, g * 128)
-
+def clear_ends(planes):
+    for plane in planes:
+        plane[0:CH, :] = jnp.zeros((CH, LANES), BF)
+        plane[CH + ROWS : PADDED, :] = jnp.zeros((CH, LANES), BF)
+
+
+def band_step(p, half, w_ref, cells, a1_ref, a2_ref, s_ref, emit, after):
+    for g in range(8):
+        at = slice(g * 128, g * 128 + 128)
+        part = jnp.dot(w_ref[...], cells(g * 128), preferred_element_type=F32)
+        done = a2_ref[at, :] + part[256:384]
+        a2_ref[at, :] = a1_ref[at, :] + part[128:256]
+        a1_ref[at, :] = part[0:128]
+        emit(jnp.maximum(p - 2, 0), at, done[:, 0:128])
+        emit(p + half - 2, at, done[:, 128:256])
+        s_ref[jnp.minimum(p, 2), at, :] = done[:, 128:256]
+        after(g * 128)
+
+
+def band_seam(half, a1_ref, a2_ref, s_ref, emit):
     for g in range(8):
         at = slice(g * 128, g * 128 + 128)
         emit(half - 2, at, a2_ref[at, 0:128] + s_ref[0, at, :])
         emit(half - 1, at, a1_ref[at, 0:128] + s_ref[1, at, :])
 
 
-def conv_scratch(rows):
+def conv_scratch():
     return [
-        VMEM((rows, 3, PADDED, LANES), BF),
         VMEM((ROWS, 256), F32),
         VMEM((ROWS, 256), F32),
         VMEM((3, ROWS, LANES), F32),
@@ -236,10 +219,11 @@
 
 
 def spectral_kernel(
-    at_ref, w_ref, g_ref, own_ref, gt_ref, gb_ref, mine_ref, other_ref,
+    at_ref, w_ref, g_ref, own_ref, gt_ref, gb_ref, e_ref, mine_ref, other_ref,
     x_ref, a1_ref, a2_ref, s_ref, o_ref
 ):
-    clear(x_ref, a1_ref, a2_ref, 6)
+    clear(a1_ref, a2_ref)
+    clear_ends([x_ref.at[r, d] for r in range(6) for d in range(3)])
     lane = lax.broadcasted_iota(jnp.int32, (256, LANES), 1)
     for r0 in range(0, ROWS, 256):
         src, dst = slice(r0, r0 + 256), slice(CH + r0, CH + r0 + 256)
@@ -257,26 +241,41 @@
     def emit(row, at, value):
         o_ref[(row + shift) % 4, at, :] = (value + own_ref[row, at, :]).astype(BF)
 
-    band_conv(w_ref, x_ref, a1_ref, a2_ref, s_ref, 3, emit, lambda p: None, lambda p, r0: None)
+    @pl.loop(0, 3)
+    def _(p):
+        def cells(r0):
+            rows = slice(r0, r0 + 256)
+            return jnp.concatenate(
+                [x_ref[layer, :, rows, :].reshape(768, LANES) for layer in (p, p + 3)], axis=1
+            )
+
+        band_step(p, 3, w_ref, cells, a1_ref, a2_ref, s_ref, emit, lambda r0: None)
+
+    band_seam(3, a1_ref, a2_ref, s_ref, emit)
     mine_ref[...] = o_ref[0:2]
-    other_ref[...] = o_ref[2:4]
-
-
-def spectral(where, band, modes, own, above, below):
-    half = jax.ShapeDtypeStruct((2, ROWS, LANES), BF)
+    other_ref[0:2] = o_ref[2:4]
+    other_ref[2] = e_ref[...]
+
+
+def spectral(where, band, modes, own, above, below, edges):
     return pl.pallas_call(
         spectral_kernel,
-        in_specs=[pl.BlockSpec(memory_space=pltpu.SMEM)] + [pl.BlockSpec(memory_space=VMEM)] * 5,
-        out_shape=(half, half),
-        scratch_shapes=conv_scratch(6) + [VMEM((4, ROWS, LANES), BF)],
+        in_specs=[pl.BlockSpec(memory_space=pltpu.SMEM)] + [pl.BlockSpec(memory_space=VMEM)] * 6,
+        out_shape=(
+            jax.ShapeDtypeStruct((2, ROWS, LANES), BF),
+            jax.ShapeDtypeStruct((3, ROWS, LANES), BF),
+        ),
+        scratch_shapes=[VMEM((6, 3, PADDED, LANES), BF)]
+        + conv_scratch()
+        + [VMEM((4, ROWS, LANES), BF)],
         compiler_params=params(40),
         cost_estimate=cost(4e9, 8e6),
         name="spectral",
-    )(where, band, modes, own, above, below)
+    )(where, band, modes, own, above, below, edges)
 
 
 def add_kernel(a_ref, b_ref, o_ref):
-    o_ref[...] = (a_ref[...].astype(F32) + b_ref[...].astype(F32)).astype(BF)
+    o_ref[...] = (a_ref[...].astype(F32) + b_ref[0:2].astype(F32)).astype(BF)
 
 
 def add(a, b):
@@ -290,51 +289,56 @@
 
 
 def lift_kernel(
-    part, w_ref, f_ref, halo_ref, el_ref, er_ref, o_ref,
-    w_buf, x_ref, a1_ref, a2_ref, s_ref, ed_ref, o_buf, sem, in_sem, out_sem
+    part, at_ref, w_ref, f_ref, halo_ref, theirs_ref, across_ref, o_ref,
+    w_buf, x_ref, even_ref, odd_ref, a1_ref, a2_ref, s_ref, ed_ref, o_buf, sem, in_sem, out_sem
 ):
     half = 5
     first = 8 * part
     body = slice(CH, CH + ROWS)
     edges = [
-        pltpu.make_async_copy(el_ref, ed_ref.at[0], in_sem.at[0]),
-        pltpu.make_async_copy(er_ref, ed_ref.at[1], in_sem.at[1]),
+        pltpu.make_async_copy(theirs_ref.at[2], ed_ref.at[0], in_sem.at[0]),
+        pltpu.make_async_copy(across_ref, ed_ref.at[1], in_sem.at[1]),
     ]
     weights = pltpu.make_async_copy(w_ref, w_buf, in_sem.at[2])
     fetch = []
     for r in range(10):
         src = halo_ref if first + r in (0, 17) else f_ref.at[first + r - 1]
-        fetch.append(pltpu.make_async_copy(src, x_ref.at[r, 1, body, :], sem.at[r]))
+        fetch.append(pltpu.make_async_copy(src, x_ref.at[r, body, :], sem.at[r]))
     later = [r + k for r in range(1, half) for k in (0, half) if r + k != half - 1]
     for copy in edges + [fetch[0], fetch[half], weights, fetch[half - 1]]:
         copy.start()
     for r in later:
         fetch[r].start()
-    clear(x_ref, a1_ref, a2_ref, 2 * half)
+    clear(a1_ref, a2_ref)
+    clear_ends([x_ref.at[r] for r in range(2 * half)])
+    clear_ends([ref.at[k, d] for ref in (even_ref, odd_ref) for k in range(2) for d in range(2)])
     lane = lax.broadcasted_iota(jnp.int32, (128, LANES), 1)
     for copy in edges:
         copy.wait()
     for r0 in range(0, ROWS, 128):
         at = slice(r0, r0 + 128)
-        ed_ref[0, at, :] = jnp.where(lane % 2 == 0, ed_ref[0, at, :], ed_ref[1, at, :])
-
-    def build(r, r0):
+        ed_ref[0, at, :] = jnp.where(
+            (lane + at_ref[0]) % 2 == 1, ed_ref[0, at, :], ed_ref[1, at, :]
+        )
+
+    def build(into, p, r0):
         at = slice(CH + r0, CH + r0 + 128)
-        mid = x_ref[r, 1, at, :]
-        edge = pltpu.roll(ed_ref[0, r0 : r0 + 128, :], 128 - 2 * (first + r), 1)
-        x_ref[r, 0, at, :] = jnp.where(lane == 0, edge, pltpu.roll(mid, 1, 1))
-        x_ref[r, 2, at, :] = jnp.where(lane == 127, edge, pltpu.roll(mid, 127, 1))
+        for k in range(2):
+            r = p + k * half
+            mid = x_ref[r, at, :]
+            edge = pltpu.roll(ed_ref[0, r0 : r0 + 128, :], 128 - 2 * (first + r), 1)
+            into[k, 0, at, :] = jnp.where(lane == 0, edge, pltpu.roll(mid, 1, 1))
+            into[k, 1, at, :] = jnp.where(lane == 127, edge, pltpu.roll(mid, 127, 1))
 
     fetch[0].wait()
     fetch[half].wait()
     for r0 in range(0, ROWS, 128):
-        build(0, r0)
-        build(half, r0)
+        build(even_ref, 0, r0)
     weights.wait()
     fetch[half - 1].wait()
 
     def arrived(r):
-        pltpu.make_async_copy(halo_ref, x_ref.at[r, 1, body, :], sem.at[r]).wait()
+        pltpu.make_async_copy(halo_ref, x_ref.at[r, body, :], sem.at[r]).wait()
 
     def out(row):
         return pltpu.make_async_copy(o_buf.at[row], o_ref.at[row], out_sem.at[row])
@@ -353,31 +357,58 @@
             out(p - 3).start()
             out(p + half - 3).start()
 
-    def after(p, r0):
-        following = jnp.minimum(p + 1, half - 1)
-        build(following, r0)
-        build(following + half, r0)
-
     def emit(row, at, value):
-        same = x_ref[row + 1, 1, CH + at.start : CH + at.stop, :].astype(F32)
+        same = x_ref[row + 1, CH + at.start : CH + at.stop, :].astype(F32)
         o_buf[row, at, :] = (value + same).astype(BF)
 
-    band_conv(w_buf, x_ref, a1_ref, a2_ref, s_ref, half, emit, before, after)
+    def step(p, shifted, following):
+        before(p)
+
+        def cells(r0):
+            rows = slice(r0, r0 + 256)
+            sides = []
+            for k in range(2):
+                middle = x_ref[p + k * half, rows, :]
+                sides.append(
+                    jnp.concatenate(
+                        [shifted[k, 0, rows, :], middle, shifted[k, 1, rows, :]], axis=0
+                    )
+                )
+            return jnp.concatenate(sides, axis=1)
+
+        def after(r0):
+            if following is not None:
+                build(following, p + 1, r0)
+
+        band_step(p, half, w_buf, cells, a1_ref, a2_ref, s_ref, emit, after)
+
+    @pl.loop(0, half // 2)
+    def _(q):
+        step(2 * q, even_ref, odd_ref)
+        step(2 * q + 1, odd_ref, even_ref)
+
+    step(jnp.int32(half - 1), even_ref, None)
+    band_seam(half, a1_ref, a2_ref, s_ref, emit)
     for row in (half - 3, 2 * half - 3, half - 2, half - 1):
         out(row).start()
     for row in range(8):
         out(row).wait()
 
 
-def lift(part, band, field, halo, left, right):
+def lift(part, where, band, field, halo, theirs, across):
     anywhere = pl.BlockSpec(memory_space=pl.ANY)
     return pl.pallas_call(
         functools.partial(lift_kernel, part),
-        in_specs=[anywhere] * 5,
+        in_specs=[pl.BlockSpec(memory_space=pltpu.SMEM)] + [anywhere] * 5,
         out_specs=anywhere,
         out_shape=jax.ShapeDtypeStruct((8, ROWS, LANES), BF),
-        scratch_shapes=[VMEM((384, 768), BF)]
-        + conv_scratch(10)
+        scratch_shapes=[
+            VMEM((384, 768), BF),
+            VMEM((10, PADDED, LANES), BF),
+            VMEM((2, 2, PADDED, LANES), BF),
+            VMEM((2, 2, PADDED, LANES), BF),
+        ]
+        + conv_scratch()
         + [
             VMEM((2, ROWS, LANES), BF),
             VMEM((8, ROWS, LANES), BF),
@@ -388,7 +419,7 @@
         compiler_params=params(60),
         cost_estimate=cost(8e9, 8e6),
         name="lift",
-    )(band, field, halo, left, right)
+    )(where, band, field, halo, theirs, across)
 
 
 def split(x):
@@ -459,10 +490,11 @@
     cells = jnp.concatenate(
         [blended[z * CH : z * CH + CH] for z in range(CHUNK // CH)], axis=1
     )
+    half_down = (0.5 * down_ref[...].astype(F32)).astype(BF)
     x = dot(up_ref[...], cells)
     bend = jnp.tanh(x * (GELU_ONE + GELU_THREE * (x * x)))
-    hidden = (0.5 * x * bend + 0.5 * x).astype(BF)
-    out = cells.astype(F32) + dot(down_ref[...], hidden)
+    hidden = (x * bend + x).astype(BF)
+    out = cells.astype(F32) + dot(half_down, hidden)
     for z in range(CHUNK // CH):
         for g in range(4):
             c = (z * 4 + g) * 128
@@ -511,32 +543,30 @@
 
     up_y = [(i, i + 1) for i in range(layers - 1)]
     down_y = [(j, i) for i, j in up_y]
-    up_x = [(i, i + 1) for i in range(blocks - 1)]
-    down_x = [(j, i) for i, j in up_x]
+    neighbour = [(i, i + 1) for i in range(1, blocks - 1, 2)]
+    neighbour = neighbour + [(j, i) for i, j in neighbour]
     partner = [(i, i ^ 1) for i in range(blocks)]
     chips = [[i for i in range(c, blocks, 2)] for c in range(2)]
 
     top = lax.ppermute(f[rows_y - 1], "gy", up_y)
     bottom = lax.ppermute(f[0], "gy", down_y)
-    band = banded(conv_w)
     where = jnp.stack([core, place, 1 - core]).astype(jnp.int32)
     table = lax.dynamic_index_in_dim(forward, place, 0, keepdims=False)
-    modes, own, edges = dft(f, table)
+    modes, own, edges, band = dft(f, table, conv_w)
     above, below, edges = halo_modes(top, bottom, table, edges)
-    left = lax.ppermute(edges, "gx", up_x)
-    right = lax.ppermute(edges, "gx", down_x)
-    mine, other = spectral(where, band, modes, own, above, below)
-    other, left, right = lax.optimization_barrier((other, left, right))
+    across = lax.ppermute(edges, "gx", neighbour)
+    mine, other = spectral(where, band, modes, own, above, below, edges)
+    other, across = lax.optimization_barrier((other, across))
     theirs = lax.ppermute(other, "gx", partner)
     chip_sum = add(mine, theirs)
     pieces = lax.all_to_all(
         chip_sum.reshape(16, 128, LANES), "gx", 0, 0, axis_index_groups=chips, tiled=True
     )
-    first = lift(0, band, f, top, left, right)
+    first = lift(0, where, band, f, top, theirs, across)
     pieces, first = lax.optimization_barrier((pieces, first))
     copies = mix(pieces, spec_re, spec_im)
     mixed = lax.all_to_all(copies, "gx", 0, 0, axis_index_groups=chips, tiled=True)
-    last = lift(1, band, f, bottom, left, right)
+    last = lift(1, where, band, f, bottom, theirs, across)
     mixed, last = lax.optimization_barrier((mixed, last))
     mixed = mixed.reshape(2, ROWS, LANES)
     mixed_other = lax.ppermute(mixed, "gx", partner)

time: 95.6 us -> 89.2 us (0.933)
  Pallas kernels: 61.2 us -> 55.7 us
  starting transfers between devices: 27.8 us -> 24.8 us
  waiting for transfers between devices: 1.92 us -> 3.17 us
  local copies, waits for them, and re-layouts: 3.55 us -> 4.57 us
    pallas_call x3 -> x2, Pallas kernels: 26.4 us -> 22.3 us  [lift(): pl.pallas_call(functools.partial(lift_kernel, part), in_specs=[pl.BlockSp...]
    ppermute x2 -> x1, starting transfers between devices: 6.47 us -> 4.68 us  [per_device(): across = lax.ppermute(edges, 'gx', neighbour)]
    pallas_call x2, Pallas kernels: 20.7 us -> 19.1 us  [finish(): pl.pallas_call(finish_kernel, grid_spec=pltpu.PrefetchScalarGridSpec(num_...]
    all_to_all x1, starting transfers between devices: 7.69 us -> 6.47 us  [per_device(): lax.all_to_all(chip_sum.reshape(16, 128, LANES), 'gx', 0, 0, axis_index_g...]
    unnamed x23 -> x25, local copies, waits for them, and re-layouts: 1.59 us -> 2.6 us
  transfers between devices with their start and end apart: 8 -> 7, of which waited for: 1 -> 2; matrix products, arithmetic and copies ran while one was open for 2% -> 2% of each run, Pallas kernels for 50% -> 48%
where the time goes in v3:
time: 89.2 us; the launch traced here: 88.6 us
  Pallas kernels  55.7 us (62%)
  starting transfers between devices  24.8 us (28%)
  local copies, waits for them, and re-layouts  4.57 us (5%)
  waiting for transfers between devices  3.17 us (4%)
    pallas_call x2, Pallas kernels, lift(): pl.pallas_call(functools.partial(lift_kernel, part), in_specs=[pl.BlockSp...  22.3 us
    pallas_call x2, Pallas kernels, finish(): pl.pallas_call(finish_kernel, grid_spec=pltpu.PrefetchScalarGridSpec(num_...  19.1 us
    all_to_all x1, starting transfers between devices, per_device(): lax.all_to_all(copies, 'gx', 0, 0, axis_index_groups=chips, tiled=True)  6.66 us
    all_to_all x1, starting transfers between devices, per_device(): lax.all_to_all(chip_sum.reshape(16, 128, LANES), 'gx', 0, 0, axis_index_g...  6.47 us
    pallas_call x1, Pallas kernels, spectral(): pl.pallas_call(spectral_kernel, in_specs=[pl.BlockSpec(memory_space=pltpu...  6.02 us
    pallas_call x1, Pallas kernels, dft(): pl.pallas_call(dft_kernel, in_specs=[pl.BlockSpec(memory_space=pltpu.HBM)...  4.87 us
    ppermute x1, starting transfers between devices, per_device(): across = lax.ppermute(edges, 'gx', neighbour)  4.68 us
    ppermute x1, starting transfers between devices, per_device(): top = lax.ppermute(f[rows_y - 1], 'gy', up_y)  4.39 us
  transfers between devices with their start and end apart: 7, of which 2 were waited for; matrix products, arithmetic and copies ran while one was open for 2% of the time, Pallas kernels for 48%

profile of v3, /device:TPU:1, one launch (start us, length us, event | category | flops | bytes accessed | tf_op | source)
XLA Modules:
  0.0 88.6 jit_solution(13199236867273831015)
XLA Ops:
  0.0 1.1 %fusion = (bf16[1,16,64,128]{3,2,1,0:T(8,128)(2,1)S(1)}, bf16[1,16,64,128]{3,2,1,0:T(8,128)(2,1)S(1)}) fusion(bf16[16,16,64,128]{3,2,1,0:T(8,128)(2,1)} %param.8), kind=kLoop, calls=%fused_computation.2 | loop fusion | bytes 1048576 | tf_op jit(solution)/shard_map/slice | solution.py:552
  1.1 4.4 %collective-permute-start = (bf16[1024,128]{1,0:T(8,128)(2,1)S(1)}, bf16[1024,128]{1,0:T(8,128)(2,1)S(1)}, u32[]{:S(2)}, u32[]{:S(2)}) collective-permute-start(bf16[1024,128]{1,0:T(8,128)(2,1)S(1)} %bitcast.16), channel_id=1, source_target_pairs={{0,1},{1,2},{2,3},{4,5},{5,6},{6,7},{8,9},{9,10},{10,11},{12,13},{... | collective-permute-start | bytes 786440 | tf_op jit(solution)/shard_map/ppermute | solution.py:551
  5.5 1.3 %collective-permute-start.1 = (bf16[1024,128]{1,0:T(8,128)(2,1)S(1)}, bf16[1024,128]{1,0:T(8,128)(2,1)S(1)}, u32[]{:S(2)}, u32[]{:S(2)}) collective-permute-start(bf16[1024,128]{1,0:T(8,128)(2,1)S(1)} %bitcast.15), channel_id=1, source_target_pairs={{1,0},{2,1},{3,2},{5,4},{6,5},{7,6},{9,8},{10,9},{11,10},{13,12},{... | collective-permute-start | bytes 786440 | tf_op jit(solution)/shard_map/ppermute | solution.py:552
  6.8 0.9 %dynamic-slice_bitcast_fusion.t_ref = bf16[128,384]{1,0:T(8,128)(2,1)S(1)} fusion(bf16[32,128,384]{2,1,0:T(8,128)(2,1)} %constant.29.clone, s32[]{:T(128)S(6)} %select_n.12), kind=kLoop, calls=%fused_computation | loop fusion | bytes 196612 | tf_op jit(solution)/shard_map/jit(dynamic_index_in_dim)/squeeze | solution.py:554
  7.7 0.1 pad_add_fusion.at_ref.h_ref
  7.8 1.0 %copy-done.4 = bf16[27,64,64]{2,1,0:T(8,128)(2,1)S(1)} copy-done((bf16[27,64,64]{2,1,0:T(8,128)(2,1)S(1)}, bf16[27,64,64]{2,1,0:T(8,128)(2,1)}, u32[]{:S(2)}) %copy-start.4) | copy-done | bytes 221208
  8.8 4.9 %dft.1 = (bf16[4,3,1024,128]{3,2,1,0:T(8,128)(2,1)S(1)}, f32[4,1024,128]{2,1,0:T(8,128)S(1)}, bf16[1024,128]{1,0:T(8,128)(2,1)S(1)}, bf16[384,768]{1,0:T(8,128)(2,1)S(1)}) custom-call(bf16[16,1024,128]{2,1,0:T(8,128)(2,1)} %bitcast.17, bf16[128,384]{1,0:T(8,128)(2,1)S(1)} %dynamic-slice_bitcast_fusion.t_ref, bf16[27,64,64]{2,1,0:T(8,128)(2,1)S(1)} %copy-done.4), custom_call_target="tpu_custom_call" | custom-call | flops 4000000000 | bytes 4000000 | tf_op jit(solution)/shard_map/dft/pallas_call | solution.py:123
  13.7 0.9 collective-permute-done.1.bottom_ref.halo_ref
  14.6 0.9 halo_modes.1
  15.5 4.7 %collective-permute-start.2 = (bf16[1024,128]{1,0:T(8,128)(2,1)S(1)}, bf16[1024,128]{1,0:T(8,128)(2,1)S(1)}, u32[]{:S(2)}, u32[]{:S(2)}) collective-permute-start(bf16[1024,128]{1,0:T(8,128)(2,1)S(1)} %get-tuple-element.26.e_ref), channel_id=1, source_target_pairs={{4,8},{12,16},{20,24},{28,32},{36,40},{44,48},{52,56},{60,64},{68,... | collective-permute-start | bytes 786440 | tf_op jit(solution)/shard_map/ppermute | solution.py:557
  20.2 6.0 %spectral.1 = (bf16[2,1024,128]{2,1,0:T(8,128)(2,1)S(1)}, bf16[3,1024,128]{2,1,0:T(8,128)(2,1)S(1)}) custom-call(s32[3]{0:T(128)S(1)} %pad_add_fusion.at_ref.h_ref, bf16[384,768]{1,0:T(8,128)(2,1)S(1)} %get-tuple-element.20.w_ref, bf16[4,3,1024,128]{3,2,1,0:T(8,128)(2,1)S(1)} %get-tuple-element.21.g_ref, f32[4,1024,128]{2,1,0:T(8,128)S(1)} %get-tuple-element.22.own_ref, ...), custom_call_target="tpu_custom_call" | custom-call | flops 4000000000 | bytes 8000000 | tf_op jit(solution)/shard_map/spectral/pallas_call | solution.py:261
  26.2 0.1 collective-permute-start.3
  26.3 2.3 %collective-permute-done.3.b_ref.theirs_ref = bf16[3,1024,128]{2,1,0:T(8,128)(2,1)S(1)} collective-permute-done((bf16[3,1024,128]{2,1,0:T(8,128)(2,1)S(1)}, bf16[3,1024,128]{2,1,0:T(8,128)(2,1)S(1)}, u32[]{:S(2)}, u32[]{:S(2)}) %collective-permute-start.3) | collective-permute-done | bytes 786464 | tf_op jit(solution)/shard_map/ppermute | solution.py:560
  28.6 1.0 %add.15 = bf16[2,1024,128]{2,1,0:T(8,128)(2,1)} custom-call(bf16[2,1024,128]{2,1,0:T(8,128)(2,1)S(1)} %get-tuple-element.27.a_ref, bf16[3,1024,128]{2,1,0:T(8,128)(2,1)S(1)} %collective-permute-done.3.b_ref.theirs_ref), custom_call_target="tpu_custom_call" | custom-call | flops 1000000 | bytes 2000000 | tf_op jit(solution)/shard_map/add/pallas_call | solution.py:282
  29.6 6.5 %all-to-all-start = ((bf16[16,128,128]{2,1,0:T(8,128)(2,1)}), bf16[16,128,128]{2,1,0:T(8,128)(2,1)S(1)}, u32[]{:S(2)}, u32[]{:S(2)}) async-start(bf16[16,128,128]{2,1,0:T(8,128)(2,1)} %bitcast.7), calls=%async_computation | async-start | bytes 1048576 | tf_op jit(solution)/shard_map/all_to_all | solution.py:562
  36.2 11.1 %lift.2 = bf16[8,1024,128]{2,1,0:T(8,128)(2,1)} custom-call(s32[3]{0:T(128)} %copy-done.3, bf16[384,768]{1,0:T(8,128)(2,1)} %copy-done.7, bf16[16,1024,128]{2,1,0:T(8,128)(2,1)} %bitcast.18, bf16[1024,128]{1,0:T(8,128)(2,1)} %copy-done.6, bf16[3,1024,128]{2,1,0:T(8,128)(2,1)} %copy-done, bf16[1024,128]{1,0:T(8,128)(2,1)} %copy-done.11), custom_call_target="tpu_custom_call" | custom-call | flops 8000000000 | bytes 8000000 | tf_op jit(solution)/shard_map/lift/pallas_call | solution.py:400
  47.3 1.4 %mix.1 = bf16[16,128,128]{2,1,0:T(8,128)(2,1)} custom-call(bf16[16,128,128]{2,1,0:T(8,128)(2,1)S(1)} %all-to-all-done.p_ref, f32[16,64,64]{2,1,0:T(8,128)S(1)} %copy-done.1, f32[16,64,64]{2,1,0:T(8,128)S(1)} %copy-done.2), custom_call_target="tpu_custom_call" | custom-call | flops 500000000 | bytes 1000000 | tf_op jit(solution)/shard_map/mix/pallas_call | solution.py:460
  48.8 6.7 %all-to-all-start.1 = ((bf16[16,128,128]{2,1,0:T(8,128)(2,1)}), bf16[16,128,128]{2,1,0:T(8,128)(2,1)S(1)}, u32[]{:S(2)}, u32[]{:S(2)}) async-start(bf16[16,128,128]{2,1,0:T(8,128)(2,1)} %mix.1), calls=%async_computation.1 | async-start | bytes 1048576 | tf_op jit(solution)/shard_map/all_to_all | solution.py:568
  55.5 11.2 %lift.3 = bf16[8,1024,128]{2,1,0:T(8,128)(2,1)} custom-call(s32[3]{0:T(128)} %copy-done.3, bf16[384,768]{1,0:T(8,128)(2,1)} %copy-done.7, bf16[16,1024,128]{2,1,0:T(8,128)(2,1)} %bitcast.19, bf16[1024,128]{1,0:T(8,128)(2,1)} %copy-done.5, bf16[3,1024,128]{2,1,0:T(8,128)(2,1)} %copy-done, bf16[1024,128]{1,0:T(8,128)(2,1)} %copy-done.11), custom_call_target="tpu_custom_call" | custom-call | flops 8000000000 | bytes 8000000 | tf_op jit(solution)/shard_map/lift/pallas_call | solution.py:400
  66.7 1.2 %collective-permute-start.4 = (bf16[2,1024,128]{2,1,0:T(8,128)(2,1)S(1)}, bf16[2,1024,128]{2,1,0:T(8,128)(2,1)S(1)}, u32[]{:S(2)}, u32[]{:S(2)}) collective-permute-start(bf16[2,1024,128]{2,1,0:T(8,128)(2,1)S(1)} %bitcast.13), channel_id=1, source_target_pairs={{0,4},{4,0},{8,12},{12,8},{16,20},{20,16},{24,28},{28,24},{32,36},... | collective-permute-start | bytes 1572872 | tf_op jit(solution)/shard_map/ppermute | solution.py:572
  67.9 0.7 copy.11.up_ref
  68.7 9.6 %finish.2.rest_0_ = bf16[4,4,1024,128]{3,2,1,0:T(8,128)(2,1)} custom-call(s32[3]{0:T(128)} %copy-done.3, bf16[2,4,1024,128]{3,2,1,0:T(8,128)(2,1)} %bitcast.20, bf16[2,4,1024,128]{3,2,1,0:T(8,128)(2,1)} %bitcast.22, bf16[2,1024,128]{2,1,0:T(8,128)(2,1)} %bitcast.14, bf16[32,256,128]{2,1,0:T(8,128)(2,1)} %constant.30.clone.inv_ref, ...), custom_call_target="tpu_custom_call" | custom-call | flops 5000000000 | bytes 6000000 | tf_op jit(solution)/shard_map/finish/pallas_call | solution.py:520
  78.3 0.8 copy-done.10
  79.1 9.6 %finish.3 = bf16[4,4,1024,128]{3,2,1,0:T(8,128)(2,1)} custom-call(s32[3]{0:T(128)} %copy-done.3, bf16[2,4,1024,128]{3,2,1,0:T(8,128)(2,1)} %bitcast.21, bf16[2,4,1024,128]{3,2,1,0:T(8,128)(2,1)} %bitcast.23, bf16[2,1024,128]{2,1,0:T(8,128)(2,1)} %copy-done.10, bf16[32,256,128]{2,1,0:T(8,128)(2,1)} %constant.30.clone.inv_ref, ...), custom_call_target="tpu_custom_call", output_to_operand_aliasing={{}: (7, {})} | custom-call | flops 5000000000 | bytes 6000000 | tf_op jit(solution)/shard_map/finish/pallas_call | solution.py:520
  (27 shorter events, 0.1 us)
Async XLA Ops:
  1.1 12.6 %collective-permute-start = (bf16[1024,128]{1,0:T(8,128)(2,1)S(1)}, bf16[1024,128]{1,0:T(8,128)(2,1)S(1)}, u32[]{:S(2)}, u32[]{:S(2)}) collective-permute-start(bf16[1024,128]{1,0:T(8,128)(2,1)S(1)} %bitcast.16), channel_id=1, source_target_pairs={{0,1},{1,2},{2,3},{4,5},{5,6},{6,7},{8,9},{9,10},{10,11},{12,13},{... | collective-permute-start | bytes 786440 | tf_op jit(solution)/shard_map/ppermute | solution.py:551
  5.5 9.1 %collective-permute-start.1 = (bf16[1024,128]{1,0:T(8,128)(2,1)S(1)}, bf16[1024,128]{1,0:T(8,128)(2,1)S(1)}, u32[]{:S(2)}, u32[]{:S(2)}) collective-permute-start(bf16[1024,128]{1,0:T(8,128)(2,1)S(1)} %bitcast.15), channel_id=1, source_target_pairs={{1,0},{2,1},{3,2},{5,4},{6,5},{7,6},{9,8},{10,9},{11,10},{13,12},{... | collective-permute-start | bytes 786440 | tf_op jit(solution)/shard_map/ppermute | solution.py:552
  7.8 12.4 %copy-start.3 = (s32[3]{0:T(128)}, s32[3]{0:T(128)S(1)}, u32[]{:S(2)}) copy-start(s32[3]{0:T(128)S(1)} %pad_add_fusion.at_ref.h_ref) | copy-start | bytes 40
  7.8 1.0 %copy-start.4 = (bf16[27,64,64]{2,1,0:T(8,128)(2,1)S(1)}, bf16[27,64,64]{2,1,0:T(8,128)(2,1)}, u32[]{:S(2)}) copy-start(bf16[27,64,64]{2,1,0:T(8,128)(2,1)} %w_ref.1) | copy-start | bytes 663556
  13.7 12.5 %copy-start.7 = (bf16[384,768]{1,0:T(8,128)(2,1)}, bf16[384,768]{1,0:T(8,128)(2,1)S(1)}, u32[]{:S(2)}) copy-start(bf16[384,768]{1,0:T(8,128)(2,1)S(1)} %get-tuple-element.20.w_ref) | copy-start | bytes 1769476
  13.7 12.5 %copy-start.6 = (bf16[1024,128]{1,0:T(8,128)(2,1)}, bf16[1024,128]{1,0:T(8,128)(2,1)S(1)}, u32[]{:S(2)}) copy-start(bf16[1024,128]{1,0:T(8,128)(2,1)S(1)} %collective-permute-done.top_ref.halo_ref) | copy-start | bytes 786436
  14.6 11.6 %copy-start.5 = (bf16[1024,128]{1,0:T(8,128)(2,1)}, bf16[1024,128]{1,0:T(8,128)(2,1)S(1)}, u32[]{:S(2)}) copy-start(bf16[1024,128]{1,0:T(8,128)(2,1)S(1)} %collective-permute-done.1.bottom_ref.halo_ref) | copy-start | bytes 786436
  15.5 10.8 %collective-permute-start.2 = (bf16[1024,128]{1,0:T(8,128)(2,1)S(1)}, bf16[1024,128]{1,0:T(8,128)(2,1)S(1)}, u32[]{:S(2)}, u32[]{:S(2)}) collective-permute-start(bf16[1024,128]{1,0:T(8,128)(2,1)S(1)} %get-tuple-element.26.e_ref), channel_id=1, source_target_pairs={{4,8},{12,16},{20,24},{28,32},{36,40},{44,48},{52,56},{60,64},{68,... | collective-permute-start | bytes 786440 | tf_op jit(solution)/shard_map/ppermute | solution.py:557
  26.2 9.9 %copy-start.11 = (bf16[1024,128]{1,0:T(8,128)(2,1)}, bf16[1024,128]{1,0:T(8,128)(2,1)S(1)}, u32[]{:S(2)}) copy-start(bf16[1024,128]{1,0:T(8,128)(2,1)S(1)} %collective-permute-done.2.across_ref) | copy-start | bytes 786436
  26.2 2.4 %collective-permute-start.3 = (bf16[3,1024,128]{2,1,0:T(8,128)(2,1)S(1)}, bf16[3,1024,128]{2,1,0:T(8,128)(2,1)S(1)}, u32[]{:S(2)}, u32[]{:S(2)}) collective-permute-start(bf16[3,1024,128]{2,1,0:T(8,128)(2,1)S(1)} %get-tuple-element.29), channel_id=1, source_target_pairs={{0,4},{4,0},{8,12},{12,8},{16,20},{20,16},{24,28},{28,24},{32,36},... | collective-permute-start | bytes 2359304 | tf_op jit(solution)/shard_map/ppermute | solution.py:560
  28.6 7.5 %copy-start = (bf16[3,1024,128]{2,1,0:T(8,128)(2,1)}, bf16[3,1024,128]{2,1,0:T(8,128)(2,1)S(1)}, u32[]{:S(2)}) copy-start(bf16[3,1024,128]{2,1,0:T(8,128)(2,1)S(1)} %collective-permute-done.3.b_ref.theirs_ref) | copy-start | bytes 2359300
  29.6 17.7 %all-to-all-start = ((bf16[16,128,128]{2,1,0:T(8,128)(2,1)}), bf16[16,128,128]{2,1,0:T(8,128)(2,1)S(1)}, u32[]{:S(2)}, u32[]{:S(2)}) async-start(bf16[16,128,128]{2,1,0:T(8,128)(2,1)} %bitcast.7), calls=%async_computation | async-start | bytes 1048576 | tf_op jit(solution)/shard_map/all_to_all | solution.py:562
  36.1 11.2 %copy-start.1 = (f32[16,64,64]{2,1,0:T(8,128)S(1)}, f32[16,64,64]{2,1,0:T(8,128)}, u32[]{:S(2)}) copy-start(f32[16,64,64]{2,1,0:T(8,128)} %re_ref.1) | copy-start | bytes 786436
  36.1 11.2 %copy-start.2 = (f32[16,64,64]{2,1,0:T(8,128)S(1)}, f32[16,64,64]{2,1,0:T(8,128)}, u32[]{:S(2)}) copy-start(f32[16,64,64]{2,1,0:T(8,128)} %im_ref.1) | copy-start | bytes 786436
  48.8 17.9 %all-to-all-start.1 = ((bf16[16,128,128]{2,1,0:T(8,128)(2,1)}), bf16[16,128,128]{2,1,0:T(8,128)(2,1)S(1)}, u32[]{:S(2)}, u32[]{:S(2)}) async-start(bf16[16,128,128]{2,1,0:T(8,128)(2,1)} %mix.1), calls=%async_computation.1 | async-start | bytes 1048576 | tf_op jit(solution)/shard_map/all_to_all | solution.py:568
  55.4 12.5 %copy-start.9 = (bf16[256,64]{0,1:T(8,128)(2,1)S(1)}, bf16[256,64]{0,1:T(8,128)(2,1)}, u32[]{:S(2)}) copy-start(bf16[256,64]{0,1:T(8,128)(2,1)} %param.12) | copy-start | bytes 98308
  66.7 2.0 %copy-start.8 = (bf16[16,128,128]{2,1,0:T(8,128)(2,1)}, bf16[16,128,128]{2,1,0:T(8,128)(2,1)S(1)}, u32[]{:S(2)}) copy-start(bf16[16,128,128]{2,1,0:T(8,128)(2,1)S(1)} %all-to-all-done.1) | copy-start | bytes 1572868
  66.7 11.6 %collective-permute-start.4 = (bf16[2,1024,128]{2,1,0:T(8,128)(2,1)S(1)}, bf16[2,1024,128]{2,1,0:T(8,128)(2,1)S(1)}, u32[]{:S(2)}, u32[]{:S(2)}) collective-permute-start(bf16[2,1024,128]{2,1,0:T(8,128)(2,1)S(1)} %bitcast.13), channel_id=1, source_target_pairs={{0,4},{4,0},{8,12},{12,8},{16,20},{20,16},{24,28},{28,24},{32,36},... | collective-permute-start | bytes 1572872 | tf_op jit(solution)/shard_map/ppermute | solution.py:572
  78.3 0.8 copy-start.10

commit v4 on v3

--- a/solution.py
+++ b/solution.py
@@ -83,12 +83,17 @@
     return lane // 32 == group
 
 
-def dft_kernel(f_ref, t_ref, w_ref, g_ref, own_ref, e_ref, band_ref, tab_ref, f_buf, sem):
+def dft_kernel(
+    f_ref, t_ref, w_ref, g_ref, own_ref, e_ref, band_ref, tab_ref, f_buf, w_buf, sem, w_sem
+):
+    weights = pltpu.make_async_copy(w_ref, w_buf, w_sem)
+    weights.start()
     fetch = [pltpu.make_async_copy(f_ref.at[y], f_buf.at[y], sem.at[y]) for y in range(16)]
     for i in range(4):
         for g in range(4):
             fetch[4 * g + i].start()
-    band_kernel(w_ref, band_ref)
+    weights.wait()
+    band_kernel(w_buf, band_ref)
     for g in range(4):
         for d in range(3):
             part = t_ref[:, d * 128 : d * 128 + 128]
@@ -122,7 +127,11 @@
 def dft(field, table, conv_w):
     return pl.pallas_call(
         dft_kernel,
-        in_specs=[pl.BlockSpec(memory_space=pltpu.HBM)] + [pl.BlockSpec(memory_space=VMEM)] * 2,
+        in_specs=[
+            pl.BlockSpec(memory_space=pltpu.HBM),
+            pl.BlockSpec(memory_space=VMEM),
+            pl.BlockSpec(memory_space=pltpu.HBM),
+        ],
         out_shape=(
             jax.ShapeDtypeStruct((4, 3, ROWS, LANES), BF),
             jax.ShapeDtypeStruct((4, ROWS, LANES), F32),
@@ -132,7 +141,9 @@
         scratch_shapes=[
             VMEM((512, 512), BF),
             VMEM((16, ROWS, LANES), BF),
+            VMEM((27, CH, CH), BF),
             pltpu.SemaphoreType.DMA((16,)),
+            pltpu.SemaphoreType.DMA,
         ],
         compiler_params=params(46),
         cost_estimate=cost(4e9, 4e6),
@@ -471,10 +482,11 @@
 
 
 def finish_kernel(h_ref, la_ref, lb_ref, m_ref, inv_ref, up_ref, down_ref, *rest):
-    o_ref, tab_ref = rest[-2:]
+    o_ref, tab_ref, up_buf = rest[-3:]
 
     @pl.when(pl.program_id(0) == 0)
     def _():
+        up_buf[...] = jnp.transpose(up_ref[...].astype(F32)).astype(BF)
         row = lax.broadcasted_iota(jnp.int32, (256, LANES), 0)
         inv = inv_ref[0]
         for g in range(4):
@@ -491,7 +503,7 @@
         [blended[z * CH : z * CH + CH] for z in range(CHUNK // CH)], axis=1
     )
     half_down = (0.5 * down_ref[...].astype(F32)).astype(BF)
-    x = dot(up_ref[...], cells)
+    x = dot(up_buf[...], cells)
     bend = jnp.tanh(x * (GELU_ONE + GELU_THREE * (x * x)))
     hidden = (x * bend + x).astype(BF)
     out = cells.astype(F32) + dot(half_down, hidden)
@@ -505,13 +517,13 @@
     chunks = ROWS // CHUNK
     layer = lambda s, h: (0, 2 * h[half_at] + s // chunks, s % chunks, 0)
     fixed = lambda *shape: pl.BlockSpec(shape, lambda s, h: (0,) * len(shape))
-    operands = [where, first, last, mixed, inverse, mlp_in, mlp_out]
+    operands = [where, first, last, mixed, inverse, mlp_in.T, mlp_out]
     specs = [
         pl.BlockSpec((2, 1, CHUNK, LANES), layer),
         pl.BlockSpec((2, 1, CHUNK, LANES), layer),
         pl.BlockSpec((1, CHUNK, LANES), lambda s, h: (s // chunks, s % chunks, 0)),
         pl.BlockSpec((1, 256, LANES), lambda s, h: (h[1], 0, 0)),
-        fixed(HID, CH),
+        fixed(CH, HID),
         fixed(CH, HID),
     ]
     if into is not None:
@@ -524,11 +536,11 @@
             grid=(2 * chunks,),
             in_specs=specs,
             out_specs=pl.BlockSpec((4, 1, CHUNK, LANES), layer),
-            scratch_shapes=[VMEM((256, 512), BF)],
+            scratch_shapes=[VMEM((256, 512), BF), VMEM((HID, CH), BF)],
         ),
         out_shape=jax.ShapeDtypeStruct((4, 4, ROWS, LANES), BF),
         input_output_aliases={} if into is None else {7: 0},
-        compiler_params=params(58),
+        compiler_params=params(52),
         cost_estimate=cost(5e9, 6e6),
         name="finish",
     )(*operands)

time: 89.2 us -> 87.3 us (0.979)
  local copies, waits for them, and re-layouts: 4.57 us -> 3.04 us
    unnamed x25 -> x24, local copies, waits for them, and re-layouts: 2.6 us -> 1.07 us
  transfers between devices with their start and end apart: 7 -> 7, of which waited for: 2 -> 2; matrix products, arithmetic and copies ran while one was open for 2% -> 1% of each run, Pallas kernels for 48% -> 49%
where the time goes in v4:
time: 87.3 us; the launch traced here: 86.7 us
  Pallas kernels  55.6 us (64%)
  starting transfers between devices  24.8 us (28%)
  local copies, waits for them, and re-layouts  3.04 us (3%)
  waiting for transfers between devices  2.89 us (3%)
    pallas_call x2, Pallas kernels, lift(): pl.pallas_call(functools.partial(lift_kernel, part), in_specs=[pl.BlockSp...  22.3 us
    pallas_call x2, Pallas kernels, finish(): pl.pallas_call(finish_kernel, grid_spec=pltpu.PrefetchScalarGridSpec(num_...  18.8 us
    all_to_all x1, starting transfers between devices, per_device(): lax.all_to_all(copies, 'gx', 0, 0, axis_index_groups=chips, tiled=True)  6.66 us
    all_to_all x1, starting transfers between devices, per_device(): lax.all_to_all(chip_sum.reshape(16, 128, LANES), 'gx', 0, 0, axis_index_g...  6.47 us
    pallas_call x1, Pallas kernels, spectral(): pl.pallas_call(spectral_kernel, in_specs=[pl.BlockSpec(memory_space=pltpu...  6.02 us
    pallas_call x1, Pallas kernels, dft(): pl.pallas_call(dft_kernel, in_specs=[pl.BlockSpec(memory_space=pltpu.HBM)...  5.14 us
    ppermute x1, starting transfers between devices, per_device(): across = lax.ppermute(edges, 'gx', neighbour)  4.68 us
    ppermute x1, starting transfers between devices, per_device(): top = lax.ppermute(f[rows_y - 1], 'gy', up_y)  4.39 us
  transfers between devices with their start and end apart: 7, of which 2 were waited for; matrix products, arithmetic and copies ran while one was open for 1% of the time, Pallas kernels for 49%

profile of v4, /device:TPU:1, one launch (start us, length us, event | category | flops | bytes accessed | tf_op | source)
XLA Modules:
  0.0 86.7 jit_solution(3145137308414497442)
XLA Ops:
  0.0 1.1 %fusion = (bf16[1,16,64,128]{3,2,1,0:T(8,128)(2,1)S(1)}, bf16[1,16,64,128]{3,2,1,0:T(8,128)(2,1)S(1)}) fusion(bf16[16,16,64,128]{3,2,1,0:T(8,128)(2,1)} %param.8), kind=kLoop, calls=%fused_computation.2 | loop fusion | bytes 1048576 | tf_op jit(solution)/shard_map/slice | solution.py:564
  1.1 4.4 %collective-permute-start = (bf16[1024,128]{1,0:T(8,128)(2,1)S(1)}, bf16[1024,128]{1,0:T(8,128)(2,1)S(1)}, u32[]{:S(2)}, u32[]{:S(2)}) collective-permute-start(bf16[1024,128]{1,0:T(8,128)(2,1)S(1)} %bitcast.19), channel_id=1, source_target_pairs={{0,1},{1,2},{2,3},{4,5},{5,6},{6,7},{8,9},{9,10},{10,11},{12,13},{... | collective-permute-start | bytes 786440 | tf_op jit(solution)/shard_map/ppermute | solution.py:563
  5.5 1.3 %collective-permute-start.1 = (bf16[1024,128]{1,0:T(8,128)(2,1)S(1)}, bf16[1024,128]{1,0:T(8,128)(2,1)S(1)}, u32[]{:S(2)}, u32[]{:S(2)}) collective-permute-start(bf16[1024,128]{1,0:T(8,128)(2,1)S(1)} %bitcast.18), channel_id=1, source_target_pairs={{1,0},{2,1},{3,2},{5,4},{6,5},{7,6},{9,8},{10,9},{11,10},{13,12},{... | collective-permute-start | bytes 786440 | tf_op jit(solution)/shard_map/ppermute | solution.py:564
  6.8 0.9 %dynamic-slice_bitcast_fusion.t_ref = bf16[128,384]{1,0:T(8,128)(2,1)S(1)} fusion(bf16[32,128,384]{2,1,0:T(8,128)(2,1)} %constant.29.clone, s32[]{:T(128)S(6)} %select_n.12), kind=kLoop, calls=%fused_computation | loop fusion | bytes 196612 | tf_op jit(solution)/shard_map/jit(dynamic_index_in_dim)/squeeze | solution.py:566
  7.7 0.1 pad_add_fusion.at_ref.h_ref
  7.8 1.0 %copy-done.5 = bf16[27,64,64]{2,1,0:T(8,128)(2,1)S(1)} copy-done((bf16[27,64,64]{2,1,0:T(8,128)(2,1)S(1)}, bf16[27,64,64]{2,1,0:T(8,128)(2,1)}, u32[]{:S(2)}) %copy-start.5) | copy-done | bytes 221208
  8.8 5.1 %dft.1 = (bf16[4,3,1024,128]{3,2,1,0:T(8,128)(2,1)S(1)}, f32[4,1024,128]{2,1,0:T(8,128)S(1)}, bf16[1024,128]{1,0:T(8,128)(2,1)S(1)}, bf16[384,768]{1,0:T(8,128)(2,1)S(1)}) custom-call(bf16[16,1024,128]{2,1,0:T(8,128)(2,1)} %bitcast.20, bf16[128,384]{1,0:T(8,128)(2,1)S(1)} %dynamic-slice_bitcast_fusion.t_ref, bf16[27,64,64]{2,1,0:T(8,128)(2,1)S(1)} %copy-done.5), custom_call_target="tpu_custom_call" | custom-call | flops 4000000000 | bytes 4000000 | tf_op jit(solution)/shard_map/dft/pallas_call | solution.py:128
  14.0 0.6 collective-permute-done.1.bottom_ref.halo_ref
  14.6 0.9 %halo_modes.1 = (bf16[3,1024,128]{2,1,0:T(8,128)(2,1)S(1)}, bf16[3,1024,128]{2,1,0:T(8,128)(2,1)S(1)}, bf16[1024,128]{1,0:T(8,128)(2,1)S(1)}) custom-call(bf16[1024,128]{1,0:T(8,128)(2,1)S(1)} %collective-permute-done.top_ref.halo_ref, bf16[1024,128]{1,0:T(8,128)(2,1)S(1)} %collective-permute-done.1.bottom_ref.halo_ref, ...), custom_call_target="tpu_custom_call" | custom-call | flops 1000000000 | bytes 1000000 | tf_op jit(solution)/shard_map/halo_modes/pallas_call | solution.py:177
  15.5 4.7 %collective-permute-start.2 = (bf16[1024,128]{1,0:T(8,128)(2,1)S(1)}, bf16[1024,128]{1,0:T(8,128)(2,1)S(1)}, u32[]{:S(2)}, u32[]{:S(2)}) collective-permute-start(bf16[1024,128]{1,0:T(8,128)(2,1)S(1)} %get-tuple-element.26.e_ref), channel_id=1, source_target_pairs={{4,8},{12,16},{20,24},{28,32},{36,40},{44,48},{52,56},{60,64},{68,... | collective-permute-start | bytes 786440 | tf_op jit(solution)/shard_map/ppermute | solution.py:569
  20.2 6.0 %spectral.1 = (bf16[2,1024,128]{2,1,0:T(8,128)(2,1)S(1)}, bf16[3,1024,128]{2,1,0:T(8,128)(2,1)S(1)}) custom-call(s32[3]{0:T(128)S(1)} %pad_add_fusion.at_ref.h_ref, bf16[384,768]{1,0:T(8,128)(2,1)S(1)} %get-tuple-element.20.w_ref, bf16[4,3,1024,128]{3,2,1,0:T(8,128)(2,1)S(1)} %get-tuple-element.21.g_ref, f32[4,1024,128]{2,1,0:T(8,128)S(1)} %get-tuple-element.22.own_ref, ...), custom_call_target="tpu_custom_call" | custom-call | flops 4000000000 | bytes 8000000 | tf_op jit(solution)/shard_map/spectral/pallas_call | solution.py:272
  26.2 0.1 collective-permute-start.3
  26.3 2.3 %collective-permute-done.3.b_ref.theirs_ref = bf16[3,1024,128]{2,1,0:T(8,128)(2,1)S(1)} collective-permute-done((bf16[3,1024,128]{2,1,0:T(8,128)(2,1)S(1)}, bf16[3,1024,128]{2,1,0:T(8,128)(2,1)S(1)}, u32[]{:S(2)}, u32[]{:S(2)}) %collective-permute-start.3) | collective-permute-done | bytes 786464 | tf_op jit(solution)/shard_map/ppermute | solution.py:572
  28.6 1.0 %add.15 = bf16[2,1024,128]{2,1,0:T(8,128)(2,1)} custom-call(bf16[2,1024,128]{2,1,0:T(8,128)(2,1)S(1)} %get-tuple-element.27.a_ref, bf16[3,1024,128]{2,1,0:T(8,128)(2,1)S(1)} %collective-permute-done.3.b_ref.theirs_ref), custom_call_target="tpu_custom_call" | custom-call | flops 1000000 | bytes 2000000 | tf_op jit(solution)/shard_map/add/pallas_call | solution.py:293
  29.6 6.5 %all-to-all-start = ((bf16[16,128,128]{2,1,0:T(8,128)(2,1)}), bf16[16,128,128]{2,1,0:T(8,128)(2,1)S(1)}, u32[]{:S(2)}, u32[]{:S(2)}) async-start(bf16[16,128,128]{2,1,0:T(8,128)(2,1)} %bitcast.7), calls=%async_computation | async-start | bytes 1048576 | tf_op jit(solution)/shard_map/all_to_all | solution.py:574
  36.1 0.0 copy-start.1
  36.2 11.1 %lift.2 = bf16[8,1024,128]{2,1,0:T(8,128)(2,1)} custom-call(s32[3]{0:T(128)} %copy-done.3, bf16[384,768]{1,0:T(8,128)(2,1)} %copy-done.10, bf16[16,1024,128]{2,1,0:T(8,128)(2,1)} %bitcast.21, bf16[1024,128]{1,0:T(8,128)(2,1)} %copy-done.7, bf16[3,1024,128]{2,1,0:T(8,128)(2,1)} %copy-done, bf16[1024,128]{1,0:T(8,128)(2,1)} %copy-done.11), custom_call_target="tpu_custom_call" | custom-call | flops 8000000000 | bytes 8000000 | tf_op jit(solution)/shard_map/lift/pallas_call | solution.py:411
  47.3 1.4 %mix.1 = bf16[16,128,128]{2,1,0:T(8,128)(2,1)} custom-call(bf16[16,128,128]{2,1,0:T(8,128)(2,1)S(1)} %all-to-all-done.p_ref, f32[16,64,64]{2,1,0:T(8,128)S(1)} %copy-done.1, f32[16,64,64]{2,1,0:T(8,128)S(1)} %copy-done.2), custom_call_target="tpu_custom_call" | custom-call | flops 500000000 | bytes 1000000 | tf_op jit(solution)/shard_map/mix/pallas_call | solution.py:471
  48.8 6.7 %all-to-all-start.1 = ((bf16[16,128,128]{2,1,0:T(8,128)(2,1)}), bf16[16,128,128]{2,1,0:T(8,128)(2,1)S(1)}, u32[]{:S(2)}, u32[]{:S(2)}) async-start(bf16[16,128,128]{2,1,0:T(8,128)(2,1)} %mix.1), calls=%async_computation.1 | async-start | bytes 1048576 | tf_op jit(solution)/shard_map/all_to_all | solution.py:580
  55.5 0.0 copy-start.9
  55.5 11.2 %lift.3 = bf16[8,1024,128]{2,1,0:T(8,128)(2,1)} custom-call(s32[3]{0:T(128)} %copy-done.3, bf16[384,768]{1,0:T(8,128)(2,1)} %copy-done.10, bf16[16,1024,128]{2,1,0:T(8,128)(2,1)} %bitcast.22, bf16[1024,128]{1,0:T(8,128)(2,1)} %copy-done.6, bf16[3,1024,128]{2,1,0:T(8,128)(2,1)} %copy-done, bf16[1024,128]{1,0:T(8,128)(2,1)} %copy-done.11), custom_call_target="tpu_custom_call" | custom-call | flops 8000000000 | bytes 8000000 | tf_op jit(solution)/shard_map/lift/pallas_call | solution.py:411
  66.7 1.2 %collective-permute-start.4 = (bf16[2,1024,128]{2,1,0:T(8,128)(2,1)S(1)}, bf16[2,1024,128]{2,1,0:T(8,128)(2,1)S(1)}, u32[]{:S(2)}, u32[]{:S(2)}) collective-permute-start(bf16[2,1024,128]{2,1,0:T(8,128)(2,1)S(1)} %bitcast.14), channel_id=1, source_target_pairs={{0,4},{4,0},{8,12},{12,8},{16,20},{20,16},{24,28},{28,24},{32,36},... | collective-permute-start | bytes 1572872 | tf_op jit(solution)/shard_map/ppermute | solution.py:584
  67.9 9.4 %finish.2.rest_0_ = bf16[4,4,1024,128]{3,2,1,0:T(8,128)(2,1)} custom-call(s32[3]{0:T(128)S(1)} %copy-done.4, bf16[2,4,1024,128]{3,2,1,0:T(8,128)(2,1)} %bitcast.23, bf16[2,4,1024,128]{3,2,1,0:T(8,128)(2,1)} %bitcast.25, bf16[2,1024,128]{2,1,0:T(8,128)(2,1)S(1)} %bitcast.15, bf16[32,256,128]{2,1,0:T(8,128)(2,1)} %constant.30.clone.inv_ref, ...), custom_call_target="tpu_custom_call" | custom-call | flops 5000000000 | bytes 6000000 | tf_op jit(solution)/shard_map/finish/pallas_call | solution.py:532
  77.3 9.4 %finish.3 = bf16[4,4,1024,128]{3,2,1,0:T(8,128)(2,1)} custom-call(s32[3]{0:T(128)S(1)} %copy-done.4, bf16[2,4,1024,128]{3,2,1,0:T(8,128)(2,1)} %bitcast.24, bf16[2,4,1024,128]{3,2,1,0:T(8,128)(2,1)} %bitcast.26, bf16[2,1024,128]{2,1,0:T(8,128)(2,1)S(1)} %collective-permute-done.4.m_ref, ...), custom_call_target="tpu_custom_call", output_to_operand_aliasing={{}: (7, {})} | custom-call | flops 5000000000 | bytes 6000000 | tf_op jit(solution)/shard_map/finish/pallas_call | solution.py:532
  (26 shorter events, 0.1 us)
Async XLA Ops:
  1.1 12.9 %collective-permute-start = (bf16[1024,128]{1,0:T(8,128)(2,1)S(1)}, bf16[1024,128]{1,0:T(8,128)(2,1)S(1)}, u32[]{:S(2)}, u32[]{:S(2)}) collective-permute-start(bf16[1024,128]{1,0:T(8,128)(2,1)S(1)} %bitcast.19), channel_id=1, source_target_pairs={{0,1},{1,2},{2,3},{4,5},{5,6},{6,7},{8,9},{9,10},{10,11},{12,13},{... | collective-permute-start | bytes 786440 | tf_op jit(solution)/shard_map/ppermute | solution.py:563
  5.5 9.1 %collective-permute-start.1 = (bf16[1024,128]{1,0:T(8,128)(2,1)S(1)}, bf16[1024,128]{1,0:T(8,128)(2,1)S(1)}, u32[]{:S(2)}, u32[]{:S(2)}) collective-permute-start(bf16[1024,128]{1,0:T(8,128)(2,1)S(1)} %bitcast.18), channel_id=1, source_target_pairs={{1,0},{2,1},{3,2},{5,4},{6,5},{7,6},{9,8},{10,9},{11,10},{13,12},{... | collective-permute-start | bytes 786440 | tf_op jit(solution)/shard_map/ppermute | solution.py:564
  7.8 12.4 %copy-start.3 = (s32[3]{0:T(128)}, s32[3]{0:T(128)S(1)}, u32[]{:S(2)}) copy-start(s32[3]{0:T(128)S(1)} %pad_add_fusion.at_ref.h_ref) | copy-start | bytes 40
  7.8 1.0 %copy-start.5 = (bf16[27,64,64]{2,1,0:T(8,128)(2,1)S(1)}, bf16[27,64,64]{2,1,0:T(8,128)(2,1)}, u32[]{:S(2)}) copy-start(bf16[27,64,64]{2,1,0:T(8,128)(2,1)} %w_ref.1) | copy-start | bytes 663556
  13.9 12.3 %copy-start.10 = (bf16[384,768]{1,0:T(8,128)(2,1)}, bf16[384,768]{1,0:T(8,128)(2,1)S(1)}, u32[]{:S(2)}) copy-start(bf16[384,768]{1,0:T(8,128)(2,1)S(1)} %get-tuple-element.20.w_ref) | copy-start | bytes 1769476
  14.0 12.2 %copy-start.7 = (bf16[1024,128]{1,0:T(8,128)(2,1)}, bf16[1024,128]{1,0:T(8,128)(2,1)S(1)}, u32[]{:S(2)}) copy-start(bf16[1024,128]{1,0:T(8,128)(2,1)S(1)} %collective-permute-done.top_ref.halo_ref) | copy-start | bytes 786436
  14.6 11.6 %copy-start.6 = (bf16[1024,128]{1,0:T(8,128)(2,1)}, bf16[1024,128]{1,0:T(8,128)(2,1)S(1)}, u32[]{:S(2)}) copy-start(bf16[1024,128]{1,0:T(8,128)(2,1)S(1)} %collective-permute-done.1.bottom_ref.halo_ref) | copy-start | bytes 786436
  15.5 10.8 %collective-permute-start.2 = (bf16[1024,128]{1,0:T(8,128)(2,1)S(1)}, bf16[1024,128]{1,0:T(8,128)(2,1)S(1)}, u32[]{:S(2)}, u32[]{:S(2)}) collective-permute-start(bf16[1024,128]{1,0:T(8,128)(2,1)S(1)} %get-tuple-element.26.e_ref), channel_id=1, source_target_pairs={{4,8},{12,16},{20,24},{28,32},{36,40},{44,48},{52,56},{60,64},{68,... | collective-permute-start | bytes 786440 | tf_op jit(solution)/shard_map/ppermute | solution.py:569
  26.2 9.9 %copy-start.11 = (bf16[1024,128]{1,0:T(8,128)(2,1)}, bf16[1024,128]{1,0:T(8,128)(2,1)S(1)}, u32[]{:S(2)}) copy-start(bf16[1024,128]{1,0:T(8,128)(2,1)S(1)} %collective-permute-done.2.across_ref) | copy-start | bytes 786436
  26.2 2.4 %collective-permute-start.3 = (bf16[3,1024,128]{2,1,0:T(8,128)(2,1)S(1)}, bf16[3,1024,128]{2,1,0:T(8,128)(2,1)S(1)}, u32[]{:S(2)}, u32[]{:S(2)}) collective-permute-start(bf16[3,1024,128]{2,1,0:T(8,128)(2,1)S(1)} %get-tuple-element.29), channel_id=1, source_target_pairs={{0,4},{4,0},{8,12},{12,8},{16,20},{20,16},{24,28},{28,24},{32,36},... | collective-permute-start | bytes 2359304 | tf_op jit(solution)/shard_map/ppermute | solution.py:572
  28.6 7.5 %copy-start = (bf16[3,1024,128]{2,1,0:T(8,128)(2,1)}, bf16[3,1024,128]{2,1,0:T(8,128)(2,1)S(1)}, u32[]{:S(2)}) copy-start(bf16[3,1024,128]{2,1,0:T(8,128)(2,1)S(1)} %collective-permute-done.3.b_ref.theirs_ref) | copy-start | bytes 2359300
  29.6 17.7 %all-to-all-start = ((bf16[16,128,128]{2,1,0:T(8,128)(2,1)}), bf16[16,128,128]{2,1,0:T(8,128)(2,1)S(1)}, u32[]{:S(2)}, u32[]{:S(2)}) async-start(bf16[16,128,128]{2,1,0:T(8,128)(2,1)} %bitcast.7), calls=%async_computation | async-start | bytes 1048576 | tf_op jit(solution)/shard_map/all_to_all | solution.py:574
  36.1 11.2 %copy-start.1 = (f32[16,64,64]{2,1,0:T(8,128)S(1)}, f32[16,64,64]{2,1,0:T(8,128)}, u32[]{:S(2)}) copy-start(f32[16,64,64]{2,1,0:T(8,128)} %re_ref.1) | copy-start | bytes 786436
  36.1 11.2 %copy-start.2 = (f32[16,64,64]{2,1,0:T(8,128)S(1)}, f32[16,64,64]{2,1,0:T(8,128)}, u32[]{:S(2)}) copy-start(f32[16,64,64]{2,1,0:T(8,128)} %im_ref.1) | copy-start | bytes 786436
  48.8 17.9 %all-to-all-start.1 = ((bf16[16,128,128]{2,1,0:T(8,128)(2,1)}), bf16[16,128,128]{2,1,0:T(8,128)(2,1)S(1)}, u32[]{:S(2)}, u32[]{:S(2)}) async-start(bf16[16,128,128]{2,1,0:T(8,128)(2,1)} %mix.1), calls=%async_computation.1 | async-start | bytes 1048576 | tf_op jit(solution)/shard_map/all_to_all | solution.py:580
  55.4 12.5 %copy-start.4 = (s32[3]{0:T(128)S(1)}, s32[3]{0:T(128)}, u32[]{:S(2)}) copy-start(s32[3]{0:T(128)} %copy-done.3) | copy-start | bytes 40
  55.5 12.5 %copy-start.8 = (bf16[256,64]{0,1:T(8,128)(2,1)S(1)}, bf16[256,64]{0,1:T(8,128)(2,1)}, u32[]{:S(2)}) copy-start(bf16[256,64]{0,1:T(8,128)(2,1)} %param.12) | copy-start | bytes 98308
  55.5 12.5 %copy-start.9 = (bf16[64,256]{1,0:T(8,128)(2,1)S(1)}, bf16[64,256]{1,0:T(8,128)(2,1)}, u32[]{:S(2)}) copy-start(bf16[64,256]{1,0:T(8,128)(2,1)} %down_ref.3) | copy-start | bytes 98308
  66.7 10.6 %collective-permute-start.4 = (bf16[2,1024,128]{2,1,0:T(8,128)(2,1)S(1)}, bf16[2,1024,128]{2,1,0:T(8,128)(2,1)S(1)}, u32[]{:S(2)}, u32[]{:S(2)}) collective-permute-start(bf16[2,1024,128]{2,1,0:T(8,128)(2,1)S(1)} %bitcast.14), channel_id=1, source_target_pairs={{0,4},{4,0},{8,12},{12,8},{16,20},{20,16},{24,28},{28,24},{32,36},... | collective-permute-start | bytes 1572872 | tf_op jit(solution)/shard_map/ppermute | solution.py:584

commit v5 on v4

--- a/solution.py
+++ b/solution.py
@@ -187,14 +187,6 @@
     )(top, bottom, table, edges)
 
 
-def clear(a1_ref, a2_ref):
-    @pl.loop(0, 8)
-    def _(g):
-        at = pl.ds(pl.multiple_of(g * 128, 128), 128)
-        a1_ref[at, :] = jnp.zeros((128, 256), F32)
-        a2_ref[at, :] = jnp.zeros((128, 256), F32)
-
-
 def clear_ends(planes):
     for plane in planes:
         plane[0:CH, :] = jnp.zeros((CH, LANES), BF)
@@ -205,12 +197,14 @@
     for g in range(8):
         at = slice(g * 128, g * 128 + 128)
         part = jnp.dot(w_ref[...], cells(g * 128), preferred_element_type=F32)
-        done = a2_ref[at, :] + part[256:384]
-        a2_ref[at, :] = a1_ref[at, :] + part[128:256]
+        done = part[256:384] + a2_ref[at, :] if p > 0 else part[256:384]
+        a2_ref[at, :] = part[128:256] + a1_ref[at, :] if p > 0 else part[128:256]
         a1_ref[at, :] = part[0:128]
-        emit(jnp.maximum(p - 2, 0), at, done[:, 0:128])
-        emit(p + half - 2, at, done[:, 128:256])
-        s_ref[jnp.minimum(p, 2), at, :] = done[:, 128:256]
+        if p >= 2:
+            emit(p - 2, at, done[:, 0:128])
+            emit(p + half - 2, at, done[:, 128:256])
+        else:
+            s_ref[p, at, :] = done[:, 128:256]
         after(g * 128)
 
 
@@ -225,7 +219,7 @@
     return [
         VMEM((ROWS, 256), F32),
         VMEM((ROWS, 256), F32),
-        VMEM((3, ROWS, LANES), F32),
+        VMEM((2, ROWS, LANES), F32),
     ]
 
 
@@ -233,7 +227,6 @@
     at_ref, w_ref, g_ref, own_ref, gt_ref, gb_ref, e_ref, mine_ref, other_ref,
     x_ref, a1_ref, a2_ref, s_ref, o_ref
 ):
-    clear(a1_ref, a2_ref)
     clear_ends([x_ref.at[r, d] for r in range(6) for d in range(3)])
     lane = lax.broadcasted_iota(jnp.int32, (256, LANES), 1)
     for r0 in range(0, ROWS, 256):
@@ -252,9 +245,9 @@
     def emit(row, at, value):
         o_ref[(row + shift) % 4, at, :] = (value + own_ref[row, at, :]).astype(BF)
 
-    @pl.loop(0, 3)
-    def _(p):
-        def cells(r0):
+    for p in range(3):
+
+        def cells(r0, p=p):
             rows = slice(r0, r0 + 256)
             return jnp.concatenate(
                 [x_ref[layer, :, rows, :].reshape(768, LANES) for layer in (p, p + 3)], axis=1
@@ -320,7 +313,6 @@
         copy.start()
     for r in later:
         fetch[r].start()
-    clear(a1_ref, a2_ref)
     clear_ends([x_ref.at[r] for r in range(2 * half)])
     clear_ends([ref.at[k, d] for ref in (even_ref, odd_ref) for k in range(2) for d in range(2)])
     lane = lax.broadcasted_iota(jnp.int32, (128, LANES), 1)
@@ -355,16 +347,11 @@
         return pltpu.make_async_copy(o_buf.at[row], o_ref.at[row], out_sem.at[row])
 
     def before(p):
-        @pl.when(p < half - 2)
-        def _():
+        if p < half - 2:
             arrived(p + 1)
-
-        @pl.when(p < half - 1)
-        def _():
+        if p < half - 1:
             arrived(p + 1 + half)
-
-        @pl.when(p > 2)
-        def _():
+        if p > 2:
             out(p - 3).start()
             out(p + half - 3).start()
 
@@ -393,12 +380,9 @@
 
         band_step(p, half, w_buf, cells, a1_ref, a2_ref, s_ref, emit, after)
 
-    @pl.loop(0, half // 2)
-    def _(q):
-        step(2 * q, even_ref, odd_ref)
-        step(2 * q + 1, odd_ref, even_ref)
-
-    step(jnp.int32(half - 1), even_ref, None)
+    for p in range(half):
+        planes = (even_ref, odd_ref)
+        step(p, planes[p % 2], planes[(p + 1) % 2] if p < half - 1 else None)
     band_seam(half, a1_ref, a2_ref, s_ref, emit)
     for row in (half - 3, 2 * half - 3, half - 2, half - 1):
         out(row).start()

time: 87.3 us -> 86.1 us (0.986)
  Pallas kernels: 55.6 us -> 54.1 us
    pallas_call x1, Pallas kernels: 6.02 us -> 4.84 us  [spectral(): pl.pallas_call(spectral_kernel, in_specs=[pl.BlockSpec(memory_space=pltpu...]
  transfers between devices with their start and end apart: 7 -> 7, of which waited for: 2 -> 2; matrix products, arithmetic and copies ran while one was open for 1% -> 1% of each run, Pallas kernels for 49% -> 48%
where the time goes in v5:
time: 86.1 us; the launch traced here: 85.5 us
  Pallas kernels  54.1 us (63%)
  starting transfers between devices  25.1 us (29%)
  local copies, waits for them, and re-layouts  3.04 us (4%)
  waiting for transfers between devices  2.89 us (3%)
    pallas_call x2, Pallas kernels, lift(): pl.pallas_call(functools.partial(lift_kernel, part), in_specs=[pl.BlockSp...  22 us
    pallas_call x2, Pallas kernels, finish(): pl.pallas_call(finish_kernel, grid_spec=pltpu.PrefetchScalarGridSpec(num_...  18.7 us
    all_to_all x1, starting transfers between devices, per_device(): lax.all_to_all(copies, 'gx', 0, 0, axis_index_groups=chips, tiled=True)  6.65 us
    all_to_all x1, starting transfers between devices, per_device(): lax.all_to_all(chip_sum.reshape(16, 128, LANES), 'gx', 0, 0, axis_index_g...  6.63 us
    pallas_call x1, Pallas kernels, dft(): pl.pallas_call(dft_kernel, in_specs=[pl.BlockSpec(memory_space=pltpu.HBM)...  5.14 us
    pallas_call x1, Pallas kernels, spectral(): pl.pallas_call(spectral_kernel, in_specs=[pl.BlockSpec(memory_space=pltpu...  4.84 us
    ppermute x1, starting transfers between devices, per_device(): across = lax.ppermute(edges, 'gx', neighbour)  4.68 us
    ppermute x1, starting transfers between devices, per_device(): top = lax.ppermute(f[rows_y - 1], 'gy', up_y)  4.39 us
  transfers between devices with their start and end apart: 7, of which 2 were waited for; matrix products, arithmetic and copies ran while one was open for 1% of the time, Pallas kernels for 48%

profile of v5, /device:TPU:1, one launch (start us, length us, event | category | flops | bytes accessed | tf_op | source)
XLA Modules:
  0.0 85.5 jit_solution(886162771771692481)
XLA Ops:
  0.0 1.1 %fusion = (bf16[1,16,64,128]{3,2,1,0:T(8,128)(2,1)S(1)}, bf16[1,16,64,128]{3,2,1,0:T(8,128)(2,1)S(1)}) fusion(bf16[16,16,64,128]{3,2,1,0:T(8,128)(2,1)} %param.8), kind=kLoop, calls=%fused_computation.2 | loop fusion | bytes 1048576 | tf_op jit(solution)/shard_map/slice | solution.py:548
  1.1 4.4 %collective-permute-start = (bf16[1024,128]{1,0:T(8,128)(2,1)S(1)}, bf16[1024,128]{1,0:T(8,128)(2,1)S(1)}, u32[]{:S(2)}, u32[]{:S(2)}) collective-permute-start(bf16[1024,128]{1,0:T(8,128)(2,1)S(1)} %bitcast.19), channel_id=1, source_target_pairs={{0,1},{1,2},{2,3},{4,5},{5,6},{6,7},{8,9},{9,10},{10,11},{12,13},{... | collective-permute-start | bytes 786440 | tf_op jit(solution)/shard_map/ppermute | solution.py:547
  5.5 1.3 %collective-permute-start.1 = (bf16[1024,128]{1,0:T(8,128)(2,1)S(1)}, bf16[1024,128]{1,0:T(8,128)(2,1)S(1)}, u32[]{:S(2)}, u32[]{:S(2)}) collective-permute-start(bf16[1024,128]{1,0:T(8,128)(2,1)S(1)} %bitcast.18), channel_id=1, source_target_pairs={{1,0},{2,1},{3,2},{5,4},{6,5},{7,6},{9,8},{10,9},{11,10},{13,12},{... | collective-permute-start | bytes 786440 | tf_op jit(solution)/shard_map/ppermute | solution.py:548
  6.8 0.9 %dynamic-slice_bitcast_fusion.t_ref = bf16[128,384]{1,0:T(8,128)(2,1)S(1)} fusion(bf16[32,128,384]{2,1,0:T(8,128)(2,1)} %constant.29.clone, s32[]{:T(128)S(6)} %select_n.12), kind=kLoop, calls=%fused_computation | loop fusion | bytes 196612 | tf_op jit(solution)/shard_map/jit(dynamic_index_in_dim)/squeeze | solution.py:550
  7.7 0.1 pad_add_fusion.at_ref.h_ref
  7.8 1.0 %copy-done.5 = bf16[27,64,64]{2,1,0:T(8,128)(2,1)S(1)} copy-done((bf16[27,64,64]{2,1,0:T(8,128)(2,1)S(1)}, bf16[27,64,64]{2,1,0:T(8,128)(2,1)}, u32[]{:S(2)}) %copy-start.5) | copy-done | bytes 221208
  8.8 5.1 %dft.1 = (bf16[4,3,1024,128]{3,2,1,0:T(8,128)(2,1)S(1)}, f32[4,1024,128]{2,1,0:T(8,128)S(1)}, bf16[1024,128]{1,0:T(8,128)(2,1)S(1)}, bf16[384,768]{1,0:T(8,128)(2,1)S(1)}) custom-call(bf16[16,1024,128]{2,1,0:T(8,128)(2,1)} %bitcast.20, bf16[128,384]{1,0:T(8,128)(2,1)S(1)} %dynamic-slice_bitcast_fusion.t_ref, bf16[27,64,64]{2,1,0:T(8,128)(2,1)S(1)} %copy-done.5), custom_call_target="tpu_custom_call" | custom-call | flops 4000000000 | bytes 4000000 | tf_op jit(solution)/shard_map/dft/pallas_call | solution.py:128
  14.0 0.6 collective-permute-done.1.bottom_ref.halo_ref
  14.6 0.9 %halo_modes.1 = (bf16[3,1024,128]{2,1,0:T(8,128)(2,1)S(1)}, bf16[3,1024,128]{2,1,0:T(8,128)(2,1)S(1)}, bf16[1024,128]{1,0:T(8,128)(2,1)S(1)}) custom-call(bf16[1024,128]{1,0:T(8,128)(2,1)S(1)} %collective-permute-done.top_ref.halo_ref, bf16[1024,128]{1,0:T(8,128)(2,1)S(1)} %collective-permute-done.1.bottom_ref.halo_ref, ...), custom_call_target="tpu_custom_call" | custom-call | flops 1000000000 | bytes 1000000 | tf_op jit(solution)/shard_map/halo_modes/pallas_call | solution.py:177
  15.5 4.7 %collective-permute-start.2 = (bf16[1024,128]{1,0:T(8,128)(2,1)S(1)}, bf16[1024,128]{1,0:T(8,128)(2,1)S(1)}, u32[]{:S(2)}, u32[]{:S(2)}) collective-permute-start(bf16[1024,128]{1,0:T(8,128)(2,1)S(1)} %get-tuple-element.26.e_ref), channel_id=1, source_target_pairs={{4,8},{12,16},{20,24},{28,32},{36,40},{44,48},{52,56},{60,64},{68,... | collective-permute-start | bytes 786440 | tf_op jit(solution)/shard_map/ppermute | solution.py:553
  20.2 4.8 %spectral.1 = (bf16[2,1024,128]{2,1,0:T(8,128)(2,1)S(1)}, bf16[3,1024,128]{2,1,0:T(8,128)(2,1)S(1)}) custom-call(s32[3]{0:T(128)S(1)} %pad_add_fusion.at_ref.h_ref, bf16[384,768]{1,0:T(8,128)(2,1)S(1)} %get-tuple-element.20.w_ref, bf16[4,3,1024,128]{3,2,1,0:T(8,128)(2,1)S(1)} %get-tuple-element.21.g_ref, f32[4,1024,128]{2,1,0:T(8,128)S(1)} %get-tuple-element.22.own_ref, ...), custom_call_target="tpu_custom_call" | custom-call | flops 4000000000 | bytes 8000000 | tf_op jit(solution)/shard_map/spectral/pallas_call | solution.py:265
  25.1 0.1 collective-permute-start.3
  25.2 2.3 %collective-permute-done.3.b_ref.theirs_ref = bf16[3,1024,128]{2,1,0:T(8,128)(2,1)S(1)} collective-permute-done((bf16[3,1024,128]{2,1,0:T(8,128)(2,1)S(1)}, bf16[3,1024,128]{2,1,0:T(8,128)(2,1)S(1)}, u32[]{:S(2)}, u32[]{:S(2)}) %collective-permute-start.3) | collective-permute-done | bytes 786464 | tf_op jit(solution)/shard_map/ppermute | solution.py:556
  27.4 1.0 %add.15 = bf16[2,1024,128]{2,1,0:T(8,128)(2,1)} custom-call(bf16[2,1024,128]{2,1,0:T(8,128)(2,1)S(1)} %get-tuple-element.27.a_ref, bf16[3,1024,128]{2,1,0:T(8,128)(2,1)S(1)} %collective-permute-done.3.b_ref.theirs_ref), custom_call_target="tpu_custom_call" | custom-call | flops 1000000 | bytes 2000000 | tf_op jit(solution)/shard_map/add/pallas_call | solution.py:286
  28.5 6.6 %all-to-all-start = ((bf16[16,128,128]{2,1,0:T(8,128)(2,1)}), bf16[16,128,128]{2,1,0:T(8,128)(2,1)S(1)}, u32[]{:S(2)}, u32[]{:S(2)}) async-start(bf16[16,128,128]{2,1,0:T(8,128)(2,1)} %bitcast.7), calls=%async_computation | async-start | bytes 1048576 | tf_op jit(solution)/shard_map/all_to_all | solution.py:558
  35.1 11.0 %lift.2 = bf16[8,1024,128]{2,1,0:T(8,128)(2,1)} custom-call(s32[3]{0:T(128)} %copy-done.3, bf16[384,768]{1,0:T(8,128)(2,1)} %copy-done.10, bf16[16,1024,128]{2,1,0:T(8,128)(2,1)} %bitcast.21, bf16[1024,128]{1,0:T(8,128)(2,1)} %copy-done.7, bf16[3,1024,128]{2,1,0:T(8,128)(2,1)} %copy-done, bf16[1024,128]{1,0:T(8,128)(2,1)} %copy-done.11), custom_call_target="tpu_custom_call" | custom-call | flops 8000000000 | bytes 8000000 | tf_op jit(solution)/shard_map/lift/pallas_call | solution.py:395
  46.2 1.4 %mix.1 = bf16[16,128,128]{2,1,0:T(8,128)(2,1)} custom-call(bf16[16,128,128]{2,1,0:T(8,128)(2,1)S(1)} %all-to-all-done.p_ref, f32[16,64,64]{2,1,0:T(8,128)S(1)} %copy-done.1, f32[16,64,64]{2,1,0:T(8,128)S(1)} %copy-done.2), custom_call_target="tpu_custom_call" | custom-call | flops 500000000 | bytes 1000000 | tf_op jit(solution)/shard_map/mix/pallas_call | solution.py:455
  47.6 6.7 %all-to-all-start.1 = ((bf16[16,128,128]{2,1,0:T(8,128)(2,1)}), bf16[16,128,128]{2,1,0:T(8,128)(2,1)S(1)}, u32[]{:S(2)}, u32[]{:S(2)}) async-start(bf16[16,128,128]{2,1,0:T(8,128)(2,1)} %mix.1), calls=%async_computation.1 | async-start | bytes 1048576 | tf_op jit(solution)/shard_map/all_to_all | solution.py:564
  54.3 0.0 copy-start.8
  54.3 0.0 copy-start.9
  54.3 11.0 %lift.3 = bf16[8,1024,128]{2,1,0:T(8,128)(2,1)} custom-call(s32[3]{0:T(128)} %copy-done.3, bf16[384,768]{1,0:T(8,128)(2,1)} %copy-done.10, bf16[16,1024,128]{2,1,0:T(8,128)(2,1)} %bitcast.22, bf16[1024,128]{1,0:T(8,128)(2,1)} %copy-done.6, bf16[3,1024,128]{2,1,0:T(8,128)(2,1)} %copy-done, bf16[1024,128]{1,0:T(8,128)(2,1)} %copy-done.11), custom_call_target="tpu_custom_call" | custom-call | flops 8000000000 | bytes 8000000 | tf_op jit(solution)/shard_map/lift/pallas_call | solution.py:395
  65.4 1.4 %collective-permute-start.4 = (bf16[2,1024,128]{2,1,0:T(8,128)(2,1)S(1)}, bf16[2,1024,128]{2,1,0:T(8,128)(2,1)S(1)}, u32[]{:S(2)}, u32[]{:S(2)}) collective-permute-start(bf16[2,1024,128]{2,1,0:T(8,128)(2,1)S(1)} %bitcast.14), channel_id=1, source_target_pairs={{0,4},{4,0},{8,12},{12,8},{16,20},{20,16},{24,28},{28,24},{32,36},... | collective-permute-start | bytes 1572872 | tf_op jit(solution)/shard_map/ppermute | solution.py:568
  66.8 9.4 %finish.2.rest_0_ = bf16[4,4,1024,128]{3,2,1,0:T(8,128)(2,1)} custom-call(s32[3]{0:T(128)S(1)} %copy-done.4, bf16[2,4,1024,128]{3,2,1,0:T(8,128)(2,1)} %bitcast.23, bf16[2,4,1024,128]{3,2,1,0:T(8,128)(2,1)} %bitcast.25, bf16[2,1024,128]{2,1,0:T(8,128)(2,1)S(1)} %bitcast.15, bf16[32,256,128]{2,1,0:T(8,128)(2,1)} %constant.30.clone.inv_ref, ...), custom_call_target="tpu_custom_call" | custom-call | flops 5000000000 | bytes 6000000 | tf_op jit(solution)/shard_map/finish/pallas_call | solution.py:516
  76.1 9.4 %finish.3 = bf16[4,4,1024,128]{3,2,1,0:T(8,128)(2,1)} custom-call(s32[3]{0:T(128)S(1)} %copy-done.4, bf16[2,4,1024,128]{3,2,1,0:T(8,128)(2,1)} %bitcast.24, bf16[2,4,1024,128]{3,2,1,0:T(8,128)(2,1)} %bitcast.26, bf16[2,1024,128]{2,1,0:T(8,128)(2,1)S(1)} %collective-permute-done.4.m_ref, ...), custom_call_target="tpu_custom_call", output_to_operand_aliasing={{}: (7, {})} | custom-call | flops 5000000000 | bytes 6000000 | tf_op jit(solution)/shard_map/finish/pallas_call | solution.py:516
  (26 shorter events, 0.1 us)
Async XLA Ops:
  1.1 12.9 %collective-permute-start = (bf16[1024,128]{1,0:T(8,128)(2,1)S(1)}, bf16[1024,128]{1,0:T(8,128)(2,1)S(1)}, u32[]{:S(2)}, u32[]{:S(2)}) collective-permute-start(bf16[1024,128]{1,0:T(8,128)(2,1)S(1)} %bitcast.19), channel_id=1, source_target_pairs={{0,1},{1,2},{2,3},{4,5},{5,6},{6,7},{8,9},{9,10},{10,11},{12,13},{... | collective-permute-start | bytes 786440 | tf_op jit(solution)/shard_map/ppermute | solution.py:547
  5.5 9.1 %collective-permute-start.1 = (bf16[1024,128]{1,0:T(8,128)(2,1)S(1)}, bf16[1024,128]{1,0:T(8,128)(2,1)S(1)}, u32[]{:S(2)}, u32[]{:S(2)}) collective-permute-start(bf16[1024,128]{1,0:T(8,128)(2,1)S(1)} %bitcast.18), channel_id=1, source_target_pairs={{1,0},{2,1},{3,2},{5,4},{6,5},{7,6},{9,8},{10,9},{11,10},{13,12},{... | collective-permute-start | bytes 786440 | tf_op jit(solution)/shard_map/ppermute | solution.py:548
  7.8 12.4 %copy-start.3 = (s32[3]{0:T(128)}, s32[3]{0:T(128)S(1)}, u32[]{:S(2)}) copy-start(s32[3]{0:T(128)S(1)} %pad_add_fusion.at_ref.h_ref) | copy-start | bytes 40
  7.8 1.0 %copy-start.5 = (bf16[27,64,64]{2,1,0:T(8,128)(2,1)S(1)}, bf16[27,64,64]{2,1,0:T(8,128)(2,1)}, u32[]{:S(2)}) copy-start(bf16[27,64,64]{2,1,0:T(8,128)(2,1)} %w_ref.1) | copy-start | bytes 663556
  13.9 11.1 %copy-start.10 = (bf16[384,768]{1,0:T(8,128)(2,1)}, bf16[384,768]{1,0:T(8,128)(2,1)S(1)}, u32[]{:S(2)}) copy-start(bf16[384,768]{1,0:T(8,128)(2,1)S(1)} %get-tuple-element.20.w_ref) | copy-start | bytes 1769476
  14.0 11.1 %copy-start.7 = (bf16[1024,128]{1,0:T(8,128)(2,1)}, bf16[1024,128]{1,0:T(8,128)(2,1)S(1)}, u32[]{:S(2)}) copy-start(bf16[1024,128]{1,0:T(8,128)(2,1)S(1)} %collective-permute-done.top_ref.halo_ref) | copy-start | bytes 786436
  14.6 10.5 %copy-start.6 = (bf16[1024,128]{1,0:T(8,128)(2,1)}, bf16[1024,128]{1,0:T(8,128)(2,1)S(1)}, u32[]{:S(2)}) copy-start(bf16[1024,128]{1,0:T(8,128)(2,1)S(1)} %collective-permute-done.1.bottom_ref.halo_ref) | copy-start | bytes 786436
  15.5 9.6 %collective-permute-start.2 = (bf16[1024,128]{1,0:T(8,128)(2,1)S(1)}, bf16[1024,128]{1,0:T(8,128)(2,1)S(1)}, u32[]{:S(2)}, u32[]{:S(2)}) collective-permute-start(bf16[1024,128]{1,0:T(8,128)(2,1)S(1)} %get-tuple-element.26.e_ref), channel_id=1, source_target_pairs={{4,8},{12,16},{20,24},{28,32},{36,40},{44,48},{52,56},{60,64},{68,... | collective-permute-start | bytes 786440 | tf_op jit(solution)/shard_map/ppermute | solution.py:553
  25.1 10.0 %copy-start.11 = (bf16[1024,128]{1,0:T(8,128)(2,1)}, bf16[1024,128]{1,0:T(8,128)(2,1)S(1)}, u32[]{:S(2)}) copy-start(bf16[1024,128]{1,0:T(8,128)(2,1)S(1)} %collective-permute-done.2.across_ref) | copy-start | bytes 786436
  25.1 2.4 %collective-permute-start.3 = (bf16[3,1024,128]{2,1,0:T(8,128)(2,1)S(1)}, bf16[3,1024,128]{2,1,0:T(8,128)(2,1)S(1)}, u32[]{:S(2)}, u32[]{:S(2)}) collective-permute-start(bf16[3,1024,128]{2,1,0:T(8,128)(2,1)S(1)} %get-tuple-element.29), channel_id=1, source_target_pairs={{0,4},{4,0},{8,12},{12,8},{16,20},{20,16},{24,28},{28,24},{32,36},... | collective-permute-start | bytes 2359304 | tf_op jit(solution)/shard_map/ppermute | solution.py:556
  27.4 7.7 %copy-start = (bf16[3,1024,128]{2,1,0:T(8,128)(2,1)}, bf16[3,1024,128]{2,1,0:T(8,128)(2,1)S(1)}, u32[]{:S(2)}) copy-start(bf16[3,1024,128]{2,1,0:T(8,128)(2,1)S(1)} %collective-permute-done.3.b_ref.theirs_ref) | copy-start | bytes 2359300
  28.5 17.7 %all-to-all-start = ((bf16[16,128,128]{2,1,0:T(8,128)(2,1)}), bf16[16,128,128]{2,1,0:T(8,128)(2,1)S(1)}, u32[]{:S(2)}, u32[]{:S(2)}) async-start(bf16[16,128,128]{2,1,0:T(8,128)(2,1)} %bitcast.7), calls=%async_computation | async-start | bytes 1048576 | tf_op jit(solution)/shard_map/all_to_all | solution.py:558
  35.1 11.0 %copy-start.1 = (f32[16,64,64]{2,1,0:T(8,128)S(1)}, f32[16,64,64]{2,1,0:T(8,128)}, u32[]{:S(2)}) copy-start(f32[16,64,64]{2,1,0:T(8,128)} %re_ref.1) | copy-start | bytes 786436
  35.1 11.0 %copy-start.2 = (f32[16,64,64]{2,1,0:T(8,128)S(1)}, f32[16,64,64]{2,1,0:T(8,128)}, u32[]{:S(2)}) copy-start(f32[16,64,64]{2,1,0:T(8,128)} %im_ref.1) | copy-start | bytes 786436
  47.6 17.8 %all-to-all-start.1 = ((bf16[16,128,128]{2,1,0:T(8,128)(2,1)}), bf16[16,128,128]{2,1,0:T(8,128)(2,1)S(1)}, u32[]{:S(2)}, u32[]{:S(2)}) async-start(bf16[16,128,128]{2,1,0:T(8,128)(2,1)} %mix.1), calls=%async_computation.1 | async-start | bytes 1048576 | tf_op jit(solution)/shard_map/all_to_all | solution.py:564
  54.3 12.5 %copy-start.4 = (s32[3]{0:T(128)S(1)}, s32[3]{0:T(128)}, u32[]{:S(2)}) copy-start(s32[3]{0:T(128)} %copy-done.3) | copy-start | bytes 40
  54.3 12.5 %copy-start.8 = (bf16[256,64]{0,1:T(8,128)(2,1)S(1)}, bf16[256,64]{0,1:T(8,128)(2,1)}, u32[]{:S(2)}) copy-start(bf16[256,64]{0,1:T(8,128)(2,1)} %param.12) | copy-start | bytes 98308
  54.3 12.5 %copy-start.9 = (bf16[64,256]{1,0:T(8,128)(2,1)S(1)}, bf16[64,256]{1,0:T(8,128)(2,1)}, u32[]{:S(2)}) copy-start(bf16[64,256]{1,0:T(8,128)(2,1)} %down_ref.3) | copy-start | bytes 98308
  65.4 10.8 %collective-permute-start.4 = (bf16[2,1024,128]{2,1,0:T(8,128)(2,1)S(1)}, bf16[2,1024,128]{2,1,0:T(8,128)(2,1)S(1)}, u32[]{:S(2)}, u32[]{:S(2)}) collective-permute-start(bf16[2,1024,128]{2,1,0:T(8,128)(2,1)S(1)} %bitcast.14), channel_id=1, source_target_pairs={{0,4},{4,0},{8,12},{12,8},{16,20},{20,16},{24,28},{28,24},{32,36},... | collective-permute-start | bytes 1572872 | tf_op jit(solution)/shard_map/ppermute | solution.py:568
